TPU v7x, 128 devices: a whole 4x4x4 slice. The times are simulated.
128 devices in a mesh: ctx: 8 (over x, y_hi), tp: 16 (over z, y_lo, core).
Axes of the slice: x: 4, y: 4 (y_hi: 2, y_lo: 2; y = y_hi * 2 + y_lo), z: 4, core: 2. Of those that a mesh axis runs over, the one named last changes fastest.
Arguments:
- pre_queries: bfloat16 [2048, 24576], P('ctx', 'tp'), may hold values from -256 to 256
- pre_latent: bfloat16 [2048, 576], P(('ctx', 'tp')), may hold values from -6 to 6
- absorb_keys: bfloat16 [512, 16384], P(None, 'tp'), may hold values from -0.25 to 0.25
- absorb_values: bfloat16 [512, 16384], P(None, 'tp'), may hold values from -0.75 to 0.75
- step_queries: bfloat16 [4, 256, 24576], P(None, 'ctx', 'tp'), may hold values from -256 to 256
- step_latent: bfloat16 [4, 256, 576], P(None, 'ctx'), may hold values from -6 to 6
- context_lengths: int32 [256], P('ctx'), may hold values from 1 to 2048, as said below
- page_table: int32 [256, 32], P('ctx'), may hold values from 0 to 31, each once within a row
- out_weight: bfloat16 [16384, 7168], P('tp'), may hold values from -0.046875 to 0.046875
Outputs:
- prefill_heads: bfloat16 [2048, 16384], P('ctx', 'tp')
- decode_out: bfloat16 [4, 256, 7168], P(None, 'ctx', 'tp')
Inputs may be any that keep to these rules, and one draw needn't show every extreme that they name: `context_lengths`: at least one decode row has the whole pool in its context. `page_table`: each row lists every page of the pool once.
All inputs are finite; a program needn't handle non-finite values.
Results may differ from a plain program's by a relative error of at most 0.024.
Values may be sent and summed in bfloat16 or wider, within the bound.
No kernel may reach another device: no remote copies, remote signals or barrier semaphores. Data moves between devices by JAX's collectives and lax.ppermute only.
A program may use at most 128 MiB of HBM per device.

v0:
```python
import math

import jax
import jax.numpy as jnp
from jax import lax
from jax.sharding import PartitionSpec as P

LATENT = 512
ROPE = 64
NOPE = 128
VALUE_DIM = 128
PAGE = 64
STEPS = 4


masked_score = -1e30


def absorb(queries, key_map, heads):
    count = queries.shape[0]
    shaped = queries.reshape(count, heads, NOPE + ROPE)
    absorbed = jnp.einsum(
        "thi,jhi->thj", shaped[:, :, :NOPE], key_map, preferred_element_type=jnp.float32
    ).astype(jnp.bfloat16)
    return jnp.concatenate([absorbed, shaped[:, :, NOPE:]], axis=2)


def on_device(
    pre_queries,
    pre_latent,
    absorb_keys,
    absorb_values,
    step_queries,
    step_latent,
    context_lengths,
    page_table,
    out_weight,
):
    heads = pre_queries.shape[1] // (NOPE + ROPE)
    pre_rows = pre_queries.shape[0]
    scale = 1.0 / math.sqrt(NOPE + ROPE)
    key_map = absorb_keys.reshape(LATENT, heads, NOPE)
    value_map = absorb_values.reshape(LATENT, heads, VALUE_DIM)
    joined = absorb(pre_queries, key_map, heads).reshape(pre_rows * heads, LATENT + ROPE)
    first = lax.axis_index("ctx") * pre_rows
    query_pos = first + jnp.arange(pre_rows * heads, dtype=jnp.int32) // heads
    count = pre_rows * heads
    piece = lax.all_gather(pre_latent, ("ctx", "tp"), axis=0, tiled=True)
    running = jnp.full((count,), masked_score, jnp.float32)
    key_pos = jnp.arange(piece.shape[0], dtype=jnp.int32)
    allowed = key_pos[None, :] <= query_pos[:, None]
    scores = jnp.dot(joined, piece.T, preferred_element_type=jnp.float32) * scale
    newest = jnp.maximum(running, jnp.max(jnp.where(allowed, scores, masked_score), axis=1))
    weights = jnp.where(allowed, jnp.exp(scores - newest[:, None]), 0.0)
    totals = jnp.sum(weights, axis=1)
    numerator = jnp.dot(
        weights.astype(jnp.bfloat16), piece[:, :LATENT], preferred_element_type=jnp.float32
    )
    running, totals, numerator = (newest, totals, numerator)
    finish_mixed = (
        (numerator / totals[:, None]).astype(jnp.bfloat16).reshape(pre_rows, heads, LATENT)
    )
    projected = jnp.einsum(
        "thj,jhv->thv", finish_mixed, value_map, preferred_element_type=jnp.float32
    )
    prefill_heads = projected.astype(jnp.bfloat16).reshape(pre_rows, heads * VALUE_DIM)
    pool = lax.all_gather(pre_latent, ("ctx", "tp"), axis=0, tiled=True)
    pool_latent = pool[:, :LATENT]
    total_tokens = pool.shape[0]
    rows = context_lengths.shape[0]
    pages = page_table.shape[1]
    page_ids = jnp.arange(pages, dtype=jnp.int32)
    matches = page_table[:, :, None] == page_ids[None, None, :]
    slot = jnp.sum(jnp.where(matches, page_ids[None, :, None], 0), axis=1)
    place = (slot[:, :, None] * PAGE + jnp.arange(PAGE, dtype=jnp.int32)[None, None, :]).reshape(
        rows, total_tokens
    )
    visible = (place < context_lengths[:, None])[:, None, :]
    results = []
    for step in range(STEPS):
        step_joined = absorb(step_queries[step], key_map, heads)
        pool_scores = jnp.dot(
            step_joined.reshape(rows * heads, LATENT + ROPE),
            pool.T,
            preferred_element_type=jnp.float32,
        )
        pool_scores = pool_scores.reshape(rows, heads, total_tokens) * scale
        new_keys = step_latent[: step + 1]
        new_scores = (
            jnp.einsum("rhk,jrk->rhj", step_joined, new_keys, preferred_element_type=jnp.float32)
            * scale
        )
        largest = jnp.maximum(
            jnp.max(jnp.where(visible, pool_scores, masked_score), axis=2),
            jnp.max(new_scores, axis=2),
        )
        pool_weights = jnp.where(visible, jnp.exp(pool_scores - largest[:, :, None]), 0.0)
        new_weights = jnp.exp(new_scores - largest[:, :, None])
        totals = jnp.sum(pool_weights, axis=2) + jnp.sum(new_weights, axis=2)
        numerator = jnp.dot(
            pool_weights.astype(jnp.bfloat16).reshape(rows * heads, total_tokens),
            pool_latent,
            preferred_element_type=jnp.float32,
        )
        numerator = numerator.reshape(rows, heads, LATENT) + jnp.einsum(
            "rhj,jrk->rhk",
            new_weights.astype(jnp.bfloat16),
            new_keys[:, :, :LATENT],
            preferred_element_type=jnp.float32,
        )
        mixed = (numerator / totals[:, :, None]).astype(jnp.bfloat16)
        head_out = jnp.einsum(
            "rhj,jhv->rhv", mixed, value_map, preferred_element_type=jnp.float32
        ).astype(jnp.bfloat16)
        term = jnp.dot(
            head_out.reshape(rows, heads * VALUE_DIM),
            out_weight,
            preferred_element_type=jnp.float32,
        )
        results.append(
            lax.psum_scatter(term.astype(jnp.bfloat16), "tp", scatter_dimension=1, tiled=True)
        )
    decode_out = jnp.stack(results)
    return (prefill_heads, decode_out)


def solution(mesh):
    return jax.shard_map(
        on_device,
        mesh=mesh,
        in_specs=(
            P("ctx", "tp"),
            P(("ctx", "tp"), None),
            P(None, "tp"),
            P(None, "tp"),
            P(None, "ctx", "tp"),
            P(None, "ctx", None),
            P("ctx"),
            P("ctx", None),
            P("tp", None),
        ),
        out_specs=(P("ctx", "tp"), P(None, "ctx", "tp")),
        check_vma=False,
    )
```

profile of v0, /device:TPU:1, one launch (start us, length us, event | category | flops | bytes accessed | tf_op | source)
XLA Modules:
  0.0 500.2 jit_solution(10075562667426816348)
XLA Ops:
  7.2 0.7 all-gather.2.cloned.1.call-update
  8.0 1.1 fusion.209
  10.7 0.7 convert_bitcast_fusion
  11.6 3.5 copy.233
  15.8 1.0 copy.250
  16.9 0.5 fusion.70
  17.4 0.3 fusion.158
  17.9 0.5 fusion.72
  18.5 0.5 fusion.73
  19.0 0.5 fusion.71
  19.5 0.6 bitcast_convert_fusion
  20.2 0.3 fusion.210
  20.5 0.3 fusion.211
  20.9 0.9 fusion.212
  21.9 187.0 %all-gather.2.cloned.1.call-done = bf16[2048,576]{1,0:T(8,128)(2,1)} async-done(((bf16[16,576]{1,0:T(8,128)(2,1)}), bf16[2048,576]{1,0:T(8,128)(2,1)}) %all-gather.2.cloned.1.call-update) | async-done | bytes 2359312 | tf_op jit(solution)/shard_map/all_gather | solution.py:48
  209.0 3.0 select_reduce_fusion.4
  212.1 2.8 convolution_multiply_fusion.1
  214.9 2.9 convolution_multiply_fusion
  217.9 3.2 fusion.21
  221.1 1.1 fusion.168
  222.2 1.1 fusion.170
  223.4 1.2 fusion.182
  224.6 1.9 fusion.23
  226.6 3.3 fusion.107
  229.9 7.8 %convolution_convert_fusion = bf16[32,7168]{1,0:T(8,128)(2,1)S(1)} fusion(bf16[1024,7168]{1,0:T(8,128)(2,1)} %param.17, bf16[8,4,8,128]{3,2,1,0:T(8,128)(2,1)S(1)} %fusion.107), kind=kOutput, calls=%fused_computation.6 | convolution fusion | flops 469991424 | bytes 15204352 | tf_op jit(solution)/shard_map/dot_general | solution.py:115
  237.8 1.6 copy.291
  239.6 3.2 fusion.104
  242.8 8.0 %convolution_convert_fusion.1 = bf16[32,7168]{1,0:T(8,128)(2,1)S(1)} fusion(bf16[1024,7168]{1,0:T(8,128)(2,1)} %param.17, bf16[8,4,8,128]{3,2,1,0:T(8,128)(2,1)S(1)} %fusion.104), kind=kOutput, calls=%fused_computation.7 | convolution fusion | flops 469991424 | bytes 15204352 | tf_op jit(solution)/shard_map/dot_general | solution.py:115
  250.7 1.7 copy.289
  252.5 2.9 fusion.101
  255.5 7.8 %convolution_convert_fusion.2 = bf16[32,7168]{1,0:T(8,128)(2,1)S(1)} fusion(bf16[1024,7168]{1,0:T(8,128)(2,1)} %param.17, bf16[8,4,8,128]{3,2,1,0:T(8,128)(2,1)S(1)} %fusion.101), kind=kOutput, calls=%fused_computation.8 | convolution fusion | flops 469991424 | bytes 15204352 | tf_op jit(solution)/shard_map/dot_general | solution.py:115
  263.3 1.6 copy.287
  265.1 13.0 %select_reduce_fusion = (f32[2048]{0:T(1024)S(1)}, f32[2048,2048]{0,1:T(8,128)}) fusion(s32[2048]{0:T(1024)S(1)} %fusion.200, bf16[2048,576]{1,0:T(8,128)(2,1)} %all-gather.2.cloned.1.call-done, bf16[256,8,576]{2,1,0:T(8,128)(2,1)} %copy.233), kind=kOutput, calls=%fused_computation.1 | convolution fusion | flops 4848613376 | bytes 21512192 | tf_op jit(solution)/shard_map/dot_general | solution.py:52
  278.1 2.7 fusion.98
  280.8 7.9 %convolution_convert_fusion.3 = bf16[32,7168]{1,0:T(8,128)(2,1)S(1)} fusion(bf16[1024,7168]{1,0:T(8,128)(2,1)} %param.17, bf16[8,4,8,128]{3,2,1,0:T(8,128)(2,1)S(1)} %fusion.98), kind=kOutput, calls=%fused_computation.9 | convolution fusion | flops 469991424 | bytes 15204352 | tf_op jit(solution)/shard_map/dot_general | solution.py:115
  288.7 1.7 copy.285
  290.4 8.2 %fusion = f32[2048]{0:T(1024)S(1)} fusion(f32[2048,2048]{0,1:T(8,128)} %get-tuple-element.32, f32[2048]{0:T(1024)S(1)} %broadcast_maximum_fusion, s32[2048]{0:T(1024)S(1)} %fusion.200), kind=kLoop, calls=%fused_computation.3 | loop fusion | flops 20969472 | bytes 16801792 | tf_op jit(solution)/shard_map/reduce_sum | solution.py:55
  298.7 9.0 %fusion.20 = bf16[256,8,512]{2,1,0:T(8,128)(2,1)S(1)} fusion(f32[2048]{0:T(1024)S(1)} %fusion, f32[2048,2048]{0,1:T(8,128)} %get-tuple-element.32, f32[2048]{0:T(1024)S(1)} %broadcast_maximum_fusion, s32[2048]{0:T(1024)S(1)} %fusion.200, bf16[2048,576]{1,0:T(8,128)(2,1)} %all-gather.2.cloned.1.call-done), kind=kOutput, calls=%fused_computation.41 | convolution fusion | flops 4318035968 | bytes 20996096 | tf_op jit(solution)/shard_map/dot_general | solution.py:56
  307.6 0.9 fusion.31
  308.5 1.0 copy.282
  309.6 1.0 copy.292
  310.5 53.0 %reduce-scatter.17.cloned.1.call-done = bf16[448,32]{1,0:T(8,128)(2,1)} async-done(((bf16[7168,32]{1,0:T(8,128)(2,1)}), bf16[448,32]{1,0:T(8,128)(2,1)}) %reduce-scatter.17.cloned.1.call-update) | async-done | bytes 28688
  363.5 1.0 copy.290
  364.5 63.1 %reduce-scatter.15.cloned.1.call-done = bf16[448,32]{1,0:T(8,128)(2,1)} async-done(((bf16[7168,32]{1,0:T(8,128)(2,1)}), bf16[448,32]{1,0:T(8,128)(2,1)}) %reduce-scatter.15.cloned.1.call-update) | async-done | bytes 28688
  427.6 1.0 copy.288
  428.6 63.4 %reduce-scatter.13.cloned.1.call-done = bf16[448,32]{1,0:T(8,128)(2,1)} async-done(((bf16[7168,32]{1,0:T(8,128)(2,1)}), bf16[448,32]{1,0:T(8,128)(2,1)}) %reduce-scatter.13.cloned.1.call-update) | async-done | bytes 28688
  492.0 1.0 copy.286
  493.0 0.7 pad_maximum_fusion.5
  (115 shorter events, 3.9 us)
Async XLA Ops:
  7.2 3.5 copy-start
  7.2 3.2 copy-start.8
  7.2 201.8 %all-gather.2.cloned.1.call-start = ((), (), s32[]{:S(2)}) async-start(), calls=%async_computation.4 | async-start | bytes 2641920 | tf_op jit(solution)/shard_map/all_gather | solution.py:48
  7.9 301.6 %reduce-scatter.19.cloned.1.call-start = ((), (), s32[]{:S(2)}) async-start(), calls=%async_computation.8 | async-start | bytes 1949696
  9.2 2.2 copy-start.9
  9.4 0.7 copy-start.10
  9.5 0.7 copy-start.11
  9.7 0.6 copy-start.12
  11.6 3.5 copy-start.20
  11.6 4.3 slice-start
  11.6 5.3 %slice-start.1 = ((bf16[32,8,192]{2,1,0:T(8,128)(2,1)}), bf16[32,8,128]{2,1,0:T(8,128)(2,1)S(1)}, s32[]{:S(2)}) async-start(bf16[32,8,192]{2,1,0:T(8,128)(2,1)} %copy-done.9), calls=%async_computation.10 | async-start | bytes 131072 | tf_op jit(solution)/shard_map/slice | solution.py:23
  15.1 2.3 copy-start.15
  15.1 2.7 slice-start.2
  15.1 2.8 slice-start.4
  15.3 2.5 slice-start.6
  15.4 2.6 slice-start.3
  16.9 1.6 slice-start.5
  17.4 1.6 copy-start.16
  17.7 1.2 slice-start.7
  18.5 2.1 copy-start.3
  19.0 2.8 copy-start.5
  19.0 2.8 copy-start.21
  19.5 189.5 %copy-start.17 = (bf16[32,8,576]{2,0,1:T(8,128)(2,1)S(1)}, bf16[32,8,576]{2,0,1:T(8,128)(2,1)}, u32[]{:S(2)}) copy-start(bf16[32,8,576]{2,0,1:T(8,128)(2,1)} %copy-done.16) | copy-start | bytes 884740
  21.9 190.2 %copy-start.4 = (bf16[32,8,576]{2,0,1:T(8,128)(2,1)S(1)}, bf16[32,8,576]{2,0,1:T(8,128)(2,1)}, u32[]{:S(2)}) copy-start(bf16[32,8,576]{2,0,1:T(8,128)(2,1)} %copy-done.3) | copy-start | bytes 884740
  212.0 2.9 copy-start.6
  214.9 2.9 copy-start.2
  217.8 3.2 copy-start.19
  237.7 1.8 copy-start.14
  239.4 124.1 %reduce-scatter.17.cloned.1.call-start = ((), (), s32[]{:S(2)}) async-start(), calls=%async_computation.7 | async-start | bytes 1949696
  242.7 9.8 %copy-start.13 = (f32[32,8,512]{2,1,0:T(8,128)S(1)}, f32[32,8,512]{2,1,0:T(8,128)}, u32[]{:S(2)}) copy-start(f32[32,8,512]{2,1,0:T(8,128)} %fusion.182) | copy-start | bytes 1572868
  242.7 9.8 %copy-start.22 = (bf16[512,1024]{1,0:T(8,128)(2,1)S(1)}, bf16[512,1024]{1,0:T(8,128)(2,1)}, u32[]{:S(2)}) copy-start(bf16[512,1024]{1,0:T(8,128)(2,1)} %param.12) | copy-start | bytes 3145732
  265.0 13.1 %copy-start.7 = (bf16[32,8,2048]{2,1,0:T(8,128)(2,1)S(1)}, bf16[32,8,2048]{2,1,0:T(8,128)(2,1)}, u32[]{:S(2)}) copy-start(bf16[32,8,2048]{2,1,0:T(8,128)(2,1)} %get-tuple-element.21) | copy-start | bytes 3145732
  265.0 13.1 %copy-start.18 = (f32[32,512]{1,0:T(8,128)S(1)}, f32[32,512]{1,0:T(8,128)}, u32[]{:S(2)}) copy-start(f32[32,512]{1,0:T(8,128)} %bitcast_convert_fusion) | copy-start | bytes 196612
  265.1 162.6 %reduce-scatter.15.cloned.1.call-start = ((), (), s32[]{:S(2)}) async-start(), calls=%async_computation.6 | async-start | bytes 1949696
  290.3 201.7 %reduce-scatter.13.cloned.1.call-start = ((), (), s32[]{:S(2)}) async-start(), calls=%async_computation.5 | async-start | bytes 1949696
  298.7 195.0 %copy-start.1 = (bf16[512,1024]{1,0:T(8,128)(2,1)S(1)}, bf16[512,1024]{1,0:T(8,128)(2,1)}, u32[]{:S(2)}) copy-start(bf16[512,1024]{1,0:T(8,128)(2,1)} %param.11) | copy-start | bytes 3145732
Sparse Core Ops, SparseCore 0:
  9.7 199.1 all-gather.1
  239.5 58.9 reduce-scatter.18
  301.1 62.3 reduce-scatter.16
  365.8 61.8 reduce-scatter.14
  430.0 61.9 reduce-scatter.12
where the time goes:
time: 504 us; the launch traced here: 500 us
  waiting for transfers between devices  367 us (73%)
  matrix products  86.1 us (17%)
  local copies, waits for them, and re-layouts  19.8 us (4%)
  between operations  14.5 us (3%)
  other arithmetic  12.3 us (2%)
    all_gather x1, waiting for transfers between devices, on_device(): piece = lax.all_gather(pre_latent, ('ctx', 'tp'), axis=0, tiled=True)  187 us
    unnamed x9, waiting for transfers between devices  180 us
    dot_general x4, matrix products, on_device(): jnp.dot(head_out.reshape(rows, heads * VALUE_DIM), out_weight, preferred_...  31.5 us
    unnamed x61, local copies, waits for them, and re-layouts  13.7 us
    dot_general x1, matrix products, on_device(): jnp.dot(joined, piece.T, preferred_element_type=jnp.float32) * scale  13 us
    dot_general x4, matrix products, on_device(): jnp.einsum('rhj,jhv->rhv', mixed, value_map, preferred_element_type=jnp.f...  12.1 us
    dot_general x4, matrix products, on_device(): jnp.dot(step_joined.reshape(rows * heads, LATENT + ROPE), pool.T, preferr...  11.9 us
  transfers between devices with their start and end apart: 5, of which 4 were waited for; matrix products, arithmetic and copies ran while one was open for 17% of the time, Pallas kernels for 0%

commit v1 on v0

v1 whole, which is shorter than its diff:
```python
import functools
import itertools
import math

import jax
import jax.numpy as jnp
from jax import lax
from jax.experimental import pallas as pl
from jax.experimental.pallas import tpu as pltpu
from jax.sharding import PartitionSpec as P

LATENT = 512
ROPE = 64
NOPE = 128
VALUE_DIM = 128
PAGE = 64
STEPS = 4
WIDTH = LATENT + ROPE
HEAD = NOPE + ROPE
HEADS = 8
TOKENS = 256
ROWS = 32
QUERIES = STEPS * ROWS
HALF = 1024
POOL = 2 * HALF
MODEL = 7168
SHARE = 448
BOTH = ("ctx", "tp")

hidden = -1e30
to_exp2 = math.log2(math.e) / math.sqrt(HEAD)
vmem = pl.BlockSpec(memory_space=pltpu.VMEM)
smem = pl.BlockSpec(memory_space=pltpu.SMEM)
anywhere = pl.BlockSpec(memory_space=pl.ANY)
params = pltpu.CompilerParams(vmem_limit_bytes=56 * 1024 * 1024)


def flat(x, y, z, core):
    return (x * 2 + y // 2) * 16 + z * 4 + (y % 2) * 2 + core


def chips():
    return itertools.product(range(4), range(4), range(4), range(2))


def other_core():
    return [(flat(x, y, z, c), flat(x, y, z, 1 - c)) for x, y, z, c in chips()]


def to_group(dz, dy):
    return [(flat(x, y, z, c), flat(x, y ^ dy, (z + dz) % 4, c)) for x, y, z, c in chips()]


def same_core_groups():
    return [
        [
            flat(x, yh * 2 + yl, z, core)
            for x, yh, z, yl in itertools.product(range(4), range(2), range(4), range(2))
        ]
        for core in range(2)
    ]


def dot(a, b):
    return jnp.dot(a, b, preferred_element_type=jnp.float32)


def dot_t(a, b):
    return lax.dot_general(a, b, (((1,), (1,)), ((), ())), preferred_element_type=jnp.float32)


def absorb_kernel(pre_ref, step_ref, key_ref, pre_out, step_out):
    for source, out in ((pre_ref, pre_out), (step_ref, step_out)):
        for pair in range(HEADS // 2):
            both = source[:, pair * 2 * HEAD : (pair + 1) * 2 * HEAD]
            for part in range(2):
                head = pair * 2 + part
                query = both[:, part * HEAD : (part + 1) * HEAD]
                key_map = key_ref[:, head * NOPE : (head + 1) * NOPE]
                out[head, :, :LATENT] = dot_t(query[:, :NOPE], key_map).astype(jnp.bfloat16)
                out[head, :, LATENT:] = query[:, NOPE:]


def absorb(pre_queries, step_queries, absorb_keys):
    return pl.pallas_call(
        absorb_kernel,
        out_shape=(
            jax.ShapeDtypeStruct((HEADS, TOKENS, WIDTH), jnp.bfloat16),
            jax.ShapeDtypeStruct((HEADS, QUERIES, WIDTH), jnp.bfloat16),
        ),
        in_specs=[vmem] * 3,
        out_specs=(vmem, vmem),
        compiler_params=params,
        cost_estimate=pl.CostEstimate(
            flops=2 * 3072 * 128 * 512, bytes_accessed=6_000_000, transcendentals=0
        ),
        name="absorb",
    )(pre_queries, step_queries, absorb_keys)


def softmax_rows(scores, bias_ref, weights, bias_rows, block):
    rows = scores.shape[0]
    inverse = []
    for start in range(0, rows, block):
        shifted = (
            scores[start : start + block, :]
            + bias_ref[start % bias_rows : start % bias_rows + block, :]
        )
        largest = jnp.max(shifted, axis=1, keepdims=True)
        expo = jnp.exp2(shifted * to_exp2 - largest * to_exp2)
        inverse.append(1.0 / jnp.sum(expo, axis=1, keepdims=True))
        weights[start : start + block, :] = expo.astype(jnp.bfloat16)
    return jnp.concatenate(inverse, axis=0)


def attend(count, queries, keys, bias_ref, scores, weights, emit, bias_rows, block):
    def score(i, slot):
        query = queries[i]
        at = 0
        for ref in keys:
            size = ref.shape[0]
            scores[slot, :, at : at + size] = dot_t(query, ref[...])
            at += size

    def finish(i, slot):
        inverse = softmax_rows(scores.at[slot], bias_ref, weights, bias_rows, block)
        total = None
        at = 0
        for ref in keys:
            size = ref.shape[0]
            term = dot(weights[:, at : at + size], ref[:, :LATENT])
            total = term if total is None else total + term
            at += size
        emit(i, (total * inverse).astype(jnp.bfloat16))

    score(0, 0)

    def step(i, carry):
        slot = lax.rem(i, 2)
        score(i + 1, 1 - slot)
        finish(i, slot)
        return carry

    lax.fori_loop(0, count - 1, step, 0)
    finish(count - 1, (count - 1) % 2)


def token_in_half(shape, dim, core):
    row = lax.broadcasted_iota(jnp.int32, shape, dim)
    return (row // 16) * 32 + core * 16 + row % 16


def prefill_kernel(info, queries, first, second, value_ref, out_ref, bias, scores, weights):
    ctx, core = info[0], info[1]
    query = ctx * TOKENS + lax.broadcasted_iota(jnp.int32, (TOKENS, HALF), 0)
    for half in range(2):
        token = token_in_half((TOKENS, HALF), 1, core if half == 0 else 1 - core)
        bias[:, half * HALF : (half + 1) * HALF] = jnp.where(token <= query, 0.0, hidden)

    def emit(i, mixed):
        columns = pl.ds(pl.multiple_of(i * VALUE_DIM, VALUE_DIM), VALUE_DIM)
        out_ref[:, columns] = dot(mixed, value_ref[:, columns]).astype(jnp.bfloat16)

    attend(HEADS, queries, [first, second], bias, scores, weights, emit, TOKENS, 32)


def prefill(info, queries, first, second, absorb_values):
    return pl.pallas_call(
        prefill_kernel,
        out_shape=jax.ShapeDtypeStruct((TOKENS, HEADS * VALUE_DIM), jnp.bfloat16),
        in_specs=[smem] + [vmem] * 4,
        out_specs=vmem,
        scratch_shapes=[
            pltpu.VMEM((TOKENS, POOL), jnp.float32),
            pltpu.VMEM((2, TOKENS, POOL), jnp.float32),
            pltpu.VMEM((TOKENS, POOL), jnp.bfloat16),
        ],
        compiler_params=params,
        cost_estimate=pl.CostEstimate(
            flops=2 * 2048 * 2048 * 1088, bytes_accessed=6_000_000, transcendentals=2048 * 2048
        ),
        name="prefill",
    )(info, queries, first, second, absorb_values)


def decode_kernel(
    info, queries, first, second, newest, limit_ref, value_ref, weight_hbm,
    out_ref, bias, scores, weights, heads_out, weight, sem,
):
    core, z, yl = info[1], info[2], info[3]
    load = pltpu.make_async_copy(weight_hbm, weight, sem)
    load.start()
    limit = limit_ref[...]
    for half in range(2):
        token = token_in_half((QUERIES, HALF), 1, core if half == 0 else 1 - core) % PAGE
        page = lax.broadcasted_iota(jnp.int32, (ROWS, HALF), 0)
        of = lax.broadcasted_iota(jnp.int32, (ROWS, HALF), 1) // (PAGE // 2)
        spread = dot(limit, (page == of).astype(jnp.bfloat16))
        bias[:, half * HALF : (half + 1) * HALF] = jnp.where(
            token.astype(jnp.float32) < spread, 0.0, hidden
        )
    mine = lax.broadcasted_iota(jnp.int32, (QUERIES, QUERIES), 0)
    theirs = lax.broadcasted_iota(jnp.int32, (QUERIES, QUERIES), 1)
    seen = (mine % ROWS == theirs % ROWS) & (theirs // ROWS <= mine // ROWS)
    bias[:, POOL:] = jnp.where(seen, 0.0, hidden)

    def emit(i, mixed):
        for part in range(2):
            columns = pl.ds(pl.multiple_of((i * 2 + part) * VALUE_DIM, VALUE_DIM), VALUE_DIM)
            rows = mixed[part * QUERIES : (part + 1) * QUERIES]
            heads_out[:, columns] = dot(rows, value_ref[:, columns]).astype(jnp.bfloat16)

    attend(HEADS // 2, queries, [first, second, newest], bias, scores, weights, emit, QUERIES, 32)
    load.wait()

    def project(pair, carry):
        columns = pl.ds(pl.multiple_of(pair * 2 * SHARE, 2 * SHARE), 2 * SHARE)
        term = dot(heads_out[...], weight[:, columns])
        turned = term.T.astype(jnp.bfloat16)
        place = lax.rem(pair // 2 - z + 4, 4) * 2 + lax.rem(pair + yl, 2)
        out_ref[core, place] = turned[:SHARE]
        out_ref[1 - core, place] = turned[SHARE:]
        return carry

    lax.fori_loop(0, MODEL // (2 * SHARE), project, 0)


def decode(info, queries, first, second, newest, limit, absorb_values, out_weight):
    keys = POOL + QUERIES
    return pl.pallas_call(
        decode_kernel,
        out_shape=jax.ShapeDtypeStruct((2, 8, SHARE, QUERIES), jnp.bfloat16),
        in_specs=[smem] + [vmem] * 6 + [anywhere],
        out_specs=vmem,
        scratch_shapes=[
            pltpu.VMEM((QUERIES, keys), jnp.float32),
            pltpu.VMEM((2, 2 * QUERIES, keys), jnp.float32),
            pltpu.VMEM((2 * QUERIES, keys), jnp.bfloat16),
            pltpu.VMEM((QUERIES, HEADS * VALUE_DIM), jnp.bfloat16),
            pltpu.VMEM((HEADS * VALUE_DIM, MODEL), jnp.bfloat16),
            pltpu.SemaphoreType.DMA(()),
        ],
        compiler_params=params,
        cost_estimate=pl.CostEstimate(
            flops=2 * 1024 * 2176 * 1088 + 2 * 128 * 1024 * 7168,
            bytes_accessed=22_000_000,
            transcendentals=1024 * 2176,
        ),
        name="decode",
    )(info, queries, first, second, newest, limit, absorb_values, out_weight)


def on_device(
    pre_queries,
    pre_latent,
    absorb_keys,
    absorb_values,
    step_queries,
    step_latent,
    context_lengths,
    page_table,
    out_weight,
):
    tp = lax.axis_index("tp")
    core, yl, z = tp % 2, (tp // 2) % 2, tp // 4
    info = jnp.stack([lax.axis_index("ctx"), core, z, yl]).astype(jnp.int32)
    pre_joined, step_joined = absorb(
        pre_queries, step_queries.reshape(QUERIES, HEADS * HEAD), absorb_keys
    )
    pages = page_table.shape[1]
    page_ids = jnp.arange(pages, dtype=jnp.int32)
    matches = page_table[:, :, None] == page_ids[None, None, :]
    slot = jnp.sum(jnp.where(matches, page_ids[None, :, None], 0), axis=1)
    limit = jnp.clip(context_lengths[:, None] - slot * PAGE, 0, PAGE).astype(jnp.bfloat16)
    limit = jnp.tile(limit, (STEPS, 1))

    first = lax.all_to_all(
        jnp.broadcast_to(pre_latent[None], (64, 16, WIDTH)),
        BOTH,
        0,
        0,
        axis_index_groups=same_core_groups(),
    ).reshape(HALF, WIDTH)
    second = lax.ppermute(first, BOTH, other_core())

    shares = decode(
        info,
        step_joined.reshape(HEADS // 2, 2 * QUERIES, WIDTH),
        first,
        second,
        step_latent.reshape(QUERIES, WIDTH),
        limit,
        absorb_values,
        out_weight,
    )
    arrived = lax.ppermute(shares[1], BOTH, other_core())
    chip = (shares[0].astype(jnp.float32) + arrived.astype(jnp.float32)).astype(jnp.bfloat16)
    total = chip[0].astype(jnp.float32)
    for place in range(1, 8):
        got = lax.ppermute(chip[place], BOTH, to_group(place // 2, place % 2))
        total = total + got.astype(jnp.float32)
    decode_out = total.astype(jnp.bfloat16).T.reshape(STEPS, ROWS, SHARE)

    prefill_heads = prefill(info, pre_joined, first, second, absorb_values)
    return (prefill_heads, decode_out)


def solution(mesh):
    return jax.shard_map(
        on_device,
        mesh=mesh,
        in_specs=(
            P("ctx", "tp"),
            P(("ctx", "tp"), None),
            P(None, "tp"),
            P(None, "tp"),
            P(None, "ctx", "tp"),
            P(None, "ctx", None),
            P("ctx"),
            P("ctx", None),
            P("tp", None),
        ),
        out_specs=(P("ctx", "tp"), P(None, "ctx", "tp")),
        check_vma=False,
    )
```

time: 504 us -> 100 us (0.20)
  waiting for transfers between devices: 367 us -> 3.08 us
  matrix products: 86.1 us -> 0 us
  Pallas kernels: 0 us -> 45.4 us
  blocking collectives: 0 us -> 32 us
  between operations: 14.5 us -> 0.75 us
  local copies, waits for them, and re-layouts: 19.8 us -> 6.64 us
  other arithmetic: 12.3 us -> 1.33 us
  starting transfers between devices: 0.2 us -> 9.83 us
    all_gather x1 -> x0, waiting for transfers between devices: 187 us -> none  [on_device(): piece = lax.all_gather(pre_latent, ('ctx', 'tp'), axis=0, tiled=True)]
    unnamed x9 -> x0, waiting for transfers between devices: 180 us -> none
    dot_general x27 -> x0, matrix products: 86.1 us -> none  [the longest x4 31.5 us: on_device(): jnp.dot(head_out.reshape(rows, heads * VALUE_DIM), out_weight, preferred_...]
    pallas_call x0 -> x3, Pallas kernels: none -> 45.4 us  [the longest x1 22.6 us: prefill(): pl.pallas_call(prefill_kernel, out_shape=jax.ShapeDtypeStruct((TOKENS, HE...]
    all_to_all x0 -> x1, blocking collectives: none -> 32 us  [on_device(): lax.all_to_all(jnp.broadcast_to(pre_latent[None], (64, 16, WIDTH)), BOTH,...]
    unnamed x61 -> x8, local copies, waits for them, and re-layouts: 13.7 us -> 0.02 us
    reduce_sum x5 -> x0, other arithmetic: 10.3 us -> none  [the longest x1 8.24 us: on_device(): totals = jnp.sum(weights, axis=1)]
    ppermute x0 -> x9, starting transfers between devices: none -> 9.83 us  [the longest x7 7.45 us: on_device(): got = lax.ppermute(chip[place], BOTH, to_group(place // 2, place % 2))]
  transfers between devices with their start and end apart: 5 -> 9, of which waited for: 4 -> 2; matrix products, arithmetic and copies ran while one was open for 17% -> 1% of each run, Pallas kernels for 0% -> 27%
where the time goes in v1:
time: 100 us; the launch traced here: 99.1 us
  Pallas kernels  45.4 us (45%)
  blocking collectives  32 us (32%)
  starting transfers between devices  9.83 us (10%)
  local copies, waits for them, and re-layouts  6.64 us (7%)
  waiting for transfers between devices  3.08 us (3%)
  other arithmetic  1.33 us (1%)
    all_to_all x1, blocking collectives, on_device(): lax.all_to_all(jnp.broadcast_to(pre_latent[None], (64, 16, WIDTH)), BOTH,...  32 us
    pallas_call x1, Pallas kernels, prefill(): pl.pallas_call(prefill_kernel, out_shape=jax.ShapeDtypeStruct((TOKENS, HE...  22.6 us
    pallas_call x1, Pallas kernels, decode(): pl.pallas_call(decode_kernel, out_shape=jax.ShapeDtypeStruct((2, 8, SHARE...  18.5 us
    ppermute x7, starting transfers between devices, on_device(): got = lax.ppermute(chip[place], BOTH, to_group(place // 2, place % 2))  7.45 us
    pallas_call x1, Pallas kernels, absorb(): pl.pallas_call(absorb_kernel, out_shape=(jax.ShapeDtypeStruct((HEADS, TOK...  4.39 us
    ppermute x1, waiting for transfers between devices, on_device(): arrived = lax.ppermute(shares[1], BOTH, other_core())  2.46 us
    ppermute x1, starting transfers between devices, on_device(): second = lax.ppermute(first, BOTH, other_core())  2.28 us
  transfers between devices with their start and end apart: 9, of which 2 were waited for; matrix products, arithmetic and copies ran while one was open for 1% of the time, Pallas kernels for 27%

profile of v1, /device:TPU:1, one launch (start us, length us, event | category | flops | bytes accessed | tf_op | source)
XLA Modules:
  0.0 99.1 jit_solution(14574199253006335263)
XLA Ops:
  0.6 0.8 broadcast_in_dim.14
  1.5 32.0 %all_to_all.5 = bf16[64,16,576]{2,1,0:T(8,128)(2,1)S(1)} all-to-all(bf16[64,16,576]{2,1,0:T(8,128)(2,1)S(1)} %broadcast_in_dim.14), channel_id=1, replica_groups={{0,2,4,6,8,10,12,14,16,18,20,22,24,26,28,30,32,34,36,38,40,42,44,46,48,..., dimensions={0} | all-to-all | bytes 2359296 | tf_op jit(solution)/shard_map/all_to_all | solution.py:277
  33.5 0.0 copy-start
  33.5 0.0 copy-start.2
  33.5 0.0 copy-start.3
  33.5 1.5 %copy.17 = bf16[1024,576]{0,1:T(8,128)(2,1)} copy(bf16[1024,576]{1,0:T(8,128)(2,1)S(1)} %bitcast.38) | data formatting | bytes 2359296 | tf_op jit(solution)/shard_map/reshape | solution.py:283
  35.0 2.3 %collective-permute-start = (bf16[1024,576]{0,1:T(8,128)(2,1)}, bf16[1024,576]{0,1:T(8,128)(2,1)S(1)}, u32[]{:S(2)}, u32[]{:S(2)}) collective-permute-start(bf16[1024,576]{0,1:T(8,128)(2,1)} %copy.17), channel_id=1, source_target_pairs={{0,1},{1,0},{4,5},{5,4},{8,9},{9,8},{12,13},{13,12},{2,3},{3,2},{6... | collective-permute-start | bytes 3538952 | tf_op jit(solution)/shard_map/ppermute | solution.py:284
  37.3 4.4 %absorb.1 = (bf16[8,256,576]{2,1,0:T(8,128)(2,1)}, bf16[8,128,576]{2,1,0:T(8,128)(2,1)}) custom-call(bf16[256,1536]{1,0:T(8,128)(2,1)} %pre_ref.1, bf16[128,1536]{1,0:T(8,128)(2,1)} %bitcast.41, bf16[512,1024]{1,0:T(8,128)(2,1)} %key_ref.1), custom_call_target="tpu_custom_call" | custom-call | flops 402653184 | bytes 6000000 | tf_op jit(solution)/shard_map/absorb/pallas_call | solution.py:85
  41.7 0.0 copy-done
  41.7 0.7 pad_add_fusion.info
  42.3 0.0 copy-done.2
  42.3 0.2 select_reduce_fusion
  42.6 0.0 copy-done.3
  42.6 0.1 clamp_convert_fusion
  42.7 0.0 collective-permute-done
  42.7 1.5 %copy.18.second = bf16[1024,576]{1,0:T(8,128)(2,1)} copy(bf16[1024,576]{0,1:T(8,128)(2,1)S(1)} %collective-permute-done) | data formatting | bytes 2359296 | tf_op jit(solution)/shard_map/ppermute | solution.py:284
  44.2 0.6 tile.4
  44.8 18.5 %decode.1 = bf16[2,8,448,128]{3,2,1,0:T(8,128)(2,1)} custom-call(s32[4]{0:T(128)} %pad_add_fusion.info, bf16[4,256,576]{2,1,0:T(8,128)(2,1)} %bitcast.44, bf16[1024,576]{1,0:T(8,128)(2,1)} %bitcast.39, bf16[1024,576]{1,0:T(8,128)(2,1)} %copy.18.second, bf16[128,576]{1,0:T(8,128)(2,1)} %bitcast.45, bf16[128,32]{1,0:T(8,128)(2,1)} %bitcast.43, ...), custom_call_target="tpu_custom_call" | custom-call | flops 6727663616 | bytes 22000000 | tf_op jit(solution)/shard_map/decode/pallas_call | solution.py:230
  63.3 0.0 copy-start.1
  63.3 1.4 %slice_bitcast_fusion = bf16[8,448,128]{2,1,0:T(8,128)(2,1)S(1)} fusion(bf16[2,8,448,128]{3,2,1,0:T(8,128)(2,1)} %decode.1), kind=kLoop, calls=%fused_computation.2 | loop fusion | bytes 1835008 | tf_op jit(solution)/shard_map/squeeze | solution.py:296
  64.6 0.1 collective-permute-start.1
  64.7 2.5 %collective-permute-done.1 = bf16[8,448,128]{2,1,0:T(8,128)(2,1)S(1)} collective-permute-done((bf16[8,448,128]{2,1,0:T(8,128)(2,1)S(1)}, bf16[8,448,128]{2,1,0:T(8,128)(2,1)S(1)}, u32[]{:S(2)}, u32[]{:S(2)}) %collective-permute-start.1) | collective-permute-done | bytes 917536 | tf_op jit(solution)/shard_map/ppermute | solution.py:296
  67.2 0.0 copy-done.1
  67.2 0.2 fusion
  67.4 0.1 slice_bitcast_fusion.8
  67.5 0.1 collective-permute-start.2
  67.6 1.0 %collective-permute-start.8 = (bf16[448,128]{1,0:T(8,128)(2,1)S(1)}, bf16[448,128]{1,0:T(8,128)(2,1)S(1)}, u32[]{:S(2)}, u32[]{:S(2)}) collective-permute-start(bf16[448,128]{1,0:T(8,128)(2,1)S(1)} %get-tuple-element.9), channel_id=1, source_target_pairs={{0,14},{1,15},{4,2},{5,3},{8,6},{9,7},{12,10},{13,11},{2,12},{3,13... | collective-permute-start | bytes 344072 | tf_op jit(solution)/shard_map/ppermute | solution.py:300
  68.6 1.2 %collective-permute-start.7 = (bf16[448,128]{1,0:T(8,128)(2,1)S(1)}, bf16[448,128]{1,0:T(8,128)(2,1)S(1)}, u32[]{:S(2)}, u32[]{:S(2)}) collective-permute-start(bf16[448,128]{1,0:T(8,128)(2,1)S(1)} %get-tuple-element.10), channel_id=1, source_target_pairs={{0,12},{1,13},{4,0},{5,1},{8,4},{9,5},{12,8},{13,9},{2,14},{3,15},... | collective-permute-start | bytes 344072 | tf_op jit(solution)/shard_map/ppermute | solution.py:300
  69.8 2.0 %collective-permute-start.6 = (bf16[448,128]{1,0:T(8,128)(2,1)S(1)}, bf16[448,128]{1,0:T(8,128)(2,1)S(1)}, u32[]{:S(2)}, u32[]{:S(2)}) collective-permute-start(bf16[448,128]{1,0:T(8,128)(2,1)S(1)} %get-tuple-element.11), channel_id=1, source_target_pairs={{0,10},{1,11},{4,14},{5,15},{8,2},{9,3},{12,6},{13,7},{2,8},{3,9},... | collective-permute-start | bytes 344072 | tf_op jit(solution)/shard_map/ppermute | solution.py:300
  71.8 1.0 collective-permute-start.5
  72.8 0.0 collective-permute-done.2
  72.8 1.3 %collective-permute-start.4 = (bf16[448,128]{1,0:T(8,128)(2,1)S(1)}, bf16[448,128]{1,0:T(8,128)(2,1)S(1)}, u32[]{:S(2)}, u32[]{:S(2)}) collective-permute-start(bf16[448,128]{1,0:T(8,128)(2,1)S(1)} %get-tuple-element.13), channel_id=1, source_target_pairs={{0,6},{1,7},{4,10},{5,11},{8,14},{9,15},{12,2},{13,3},{2,4},{3,5},... | collective-permute-start | bytes 344072 | tf_op jit(solution)/shard_map/ppermute | solution.py:300
  74.1 0.6 collective-permute-done.8
  74.7 0.9 collective-permute-start.3
  75.6 22.6 %prefill.1 = bf16[256,1024]{1,0:T(8,128)(2,1)} custom-call(s32[4]{0:T(128)} %pad_add_fusion.info, bf16[8,256,576]{2,1,0:T(8,128)(2,1)} %get-tuple-element.4.queries, bf16[1024,576]{1,0:T(8,128)(2,1)} %bitcast.40, bf16[1024,576]{1,0:T(8,128)(2,1)} %copy.18.second, bf16[512,1024]{1,0:T(8,128)(2,1)} %value_ref.3), custom_call_target="tpu_custom_call" | custom-call | flops 9126805504 | bytes 6000000 | tf_op jit(solution)/shard_map/prefill/pallas_call | solution.py:168
  98.2 0.0 collective-permute-done.7
  98.2 0.0 collective-permute-done.6
  98.2 0.0 collective-permute-done.5
  98.2 0.0 collective-permute-done.4
  98.2 0.0 collective-permute-done.3
  98.2 0.1 fusion.8
  98.3 0.8 copy.20
Async XLA Ops:
  33.5 8.2 %copy-start = (bf16[64,16,576]{2,1,0:T(8,128)(2,1)}, bf16[64,16,576]{2,1,0:T(8,128)(2,1)S(1)}, u32[]{:S(2)}) copy-start(bf16[64,16,576]{2,1,0:T(8,128)(2,1)S(1)} %all_to_all.5) | copy-start | bytes 3538948
  33.5 8.8 %copy-start.2 = (s32[32,32]{1,0:T(8,128)S(1)}, s32[32,32]{1,0:T(8,128)}, u32[]{:S(2)}) copy-start(s32[32,32]{1,0:T(8,128)} %param.16) | copy-start | bytes 12292
  33.5 9.1 %copy-start.3 = (s32[32]{0:T(128)S(1)}, s32[32]{0:T(128)}, u32[]{:S(2)}) copy-start(s32[32]{0:T(128)} %param.15) | copy-start | bytes 388
  35.0 7.7 %collective-permute-start = (bf16[1024,576]{0,1:T(8,128)(2,1)}, bf16[1024,576]{0,1:T(8,128)(2,1)S(1)}, u32[]{:S(2)}, u32[]{:S(2)}) collective-permute-start(bf16[1024,576]{0,1:T(8,128)(2,1)} %copy.17), channel_id=1, source_target_pairs={{0,1},{1,0},{4,5},{5,4},{8,9},{9,8},{12,13},{13,12},{2,3},{3,2},{6... | collective-permute-start | bytes 3538952 | tf_op jit(solution)/shard_map/ppermute | solution.py:284
  63.3 3.9 %copy-start.1 = (bf16[2,8,448,128]{3,2,1,0:T(8,128)(2,1)S(1)}, bf16[2,8,448,128]{3,2,1,0:T(8,128)(2,1)}, u32[]{:S(2)}) copy-start(bf16[2,8,448,128]{3,2,1,0:T(8,128)(2,1)} %decode.1) | copy-start | bytes 5505028
  64.6 2.6 %collective-permute-start.1 = (bf16[8,448,128]{2,1,0:T(8,128)(2,1)S(1)}, bf16[8,448,128]{2,1,0:T(8,128)(2,1)S(1)}, u32[]{:S(2)}, u32[]{:S(2)}) collective-permute-start(bf16[8,448,128]{2,1,0:T(8,128)(2,1)S(1)} %slice_bitcast_fusion), channel_id=1, source_target_pairs={{0,1},{1,0},{4,5},{5,4},{8,9},{9,8},{12,13},{13,12},{2,3},{3,2},{6... | collective-permute-start | bytes 2752520 | tf_op jit(solution)/shard_map/ppermute | solution.py:296
  67.5 5.3 %collective-permute-start.2 = (bf16[448,128]{1,0:T(8,128)(2,1)S(1)}, bf16[448,128]{1,0:T(8,128)(2,1)S(1)}, u32[]{:S(2)}, u32[]{:S(2)}) collective-permute-start(bf16[448,128]{1,0:T(8,128)(2,1)S(1)} %get-tuple-element.8), channel_id=1, source_target_pairs={{0,2},{1,3},{4,6},{5,7},{8,10},{9,11},{12,14},{13,15},{2,0},{3,1},... | collective-permute-start | bytes 344072 | tf_op jit(solution)/shard_map/ppermute | solution.py:300
  67.6 7.1 %collective-permute-start.8 = (bf16[448,128]{1,0:T(8,128)(2,1)S(1)}, bf16[448,128]{1,0:T(8,128)(2,1)S(1)}, u32[]{:S(2)}, u32[]{:S(2)}) collective-permute-start(bf16[448,128]{1,0:T(8,128)(2,1)S(1)} %get-tuple-element.9), channel_id=1, source_target_pairs={{0,14},{1,15},{4,2},{5,3},{8,6},{9,7},{12,10},{13,11},{2,12},{3,13... | collective-permute-start | bytes 344072 | tf_op jit(solution)/shard_map/ppermute | solution.py:300
  68.6 29.5 %collective-permute-start.7 = (bf16[448,128]{1,0:T(8,128)(2,1)S(1)}, bf16[448,128]{1,0:T(8,128)(2,1)S(1)}, u32[]{:S(2)}, u32[]{:S(2)}) collective-permute-start(bf16[448,128]{1,0:T(8,128)(2,1)S(1)} %get-tuple-element.10), channel_id=1, source_target_pairs={{0,12},{1,13},{4,0},{5,1},{8,4},{9,5},{12,8},{13,9},{2,14},{3,15},... | collective-permute-start | bytes 344072 | tf_op jit(solution)/shard_map/ppermute | solution.py:300
  69.8 28.3 %collective-permute-start.6 = (bf16[448,128]{1,0:T(8,128)(2,1)S(1)}, bf16[448,128]{1,0:T(8,128)(2,1)S(1)}, u32[]{:S(2)}, u32[]{:S(2)}) collective-permute-start(bf16[448,128]{1,0:T(8,128)(2,1)S(1)} %get-tuple-element.11), channel_id=1, source_target_pairs={{0,10},{1,11},{4,14},{5,15},{8,2},{9,3},{12,6},{13,7},{2,8},{3,9},... | collective-permute-start | bytes 344072 | tf_op jit(solution)/shard_map/ppermute | solution.py:300
  71.8 26.3 %collective-permute-start.5 = (bf16[448,128]{1,0:T(8,128)(2,1)S(1)}, bf16[448,128]{1,0:T(8,128)(2,1)S(1)}, u32[]{:S(2)}, u32[]{:S(2)}) collective-permute-start(bf16[448,128]{1,0:T(8,128)(2,1)S(1)} %get-tuple-element.12), channel_id=1, source_target_pairs={{0,8},{1,9},{4,12},{5,13},{8,0},{9,1},{12,4},{13,5},{2,10},{3,11},... | collective-permute-start | bytes 344072 | tf_op jit(solution)/shard_map/ppermute | solution.py:300
  72.8 25.4 %collective-permute-start.4 = (bf16[448,128]{1,0:T(8,128)(2,1)S(1)}, bf16[448,128]{1,0:T(8,128)(2,1)S(1)}, u32[]{:S(2)}, u32[]{:S(2)}) collective-permute-start(bf16[448,128]{1,0:T(8,128)(2,1)S(1)} %get-tuple-element.13), channel_id=1, source_target_pairs={{0,6},{1,7},{4,10},{5,11},{8,14},{9,15},{12,2},{13,3},{2,4},{3,5},... | collective-permute-start | bytes 344072 | tf_op jit(solution)/shard_map/ppermute | solution.py:300
  74.7 23.5 %collective-permute-start.3 = (bf16[448,128]{1,0:T(8,128)(2,1)S(1)}, bf16[448,128]{1,0:T(8,128)(2,1)S(1)}, u32[]{:S(2)}, u32[]{:S(2)}) collective-permute-start(bf16[448,128]{1,0:T(8,128)(2,1)S(1)} %get-tuple-element.14), channel_id=1, source_target_pairs={{0,4},{1,5},{4,8},{5,9},{8,12},{9,13},{12,0},{13,1},{2,6},{3,7},{6... | collective-permute-start | bytes 344072 | tf_op jit(solution)/shard_map/ppermute | solution.py:300

commit v2 on v1

v2 whole, which is shorter than its diff:
```python
import functools
import itertools
import math

import jax
import jax.numpy as jnp
from jax import lax
from jax.experimental import pallas as pl
from jax.experimental.pallas import tpu as pltpu
from jax.sharding import PartitionSpec as P

LATENT = 512
ROPE = 64
NOPE = 128
VALUE_DIM = 128
PAGE = 64
STEPS = 4
WIDTH = LATENT + 2 * ROPE
PIECE = 72
BLOCK = 256
HEAD = NOPE + ROPE
HEADS = 8
TOKENS = 256
ROWS = 32
QUERIES = STEPS * ROWS
POOL = 2048
KEYS = POOL + QUERIES
MODEL = 7168
SHARE = 448
BOTH = ("ctx", "tp")

hidden = -1e30
to_exp2 = math.log2(math.e) / math.sqrt(HEAD)
vmem = pl.BlockSpec(memory_space=pltpu.VMEM)
smem = pl.BlockSpec(memory_space=pltpu.SMEM)
anywhere = pl.BlockSpec(memory_space=pl.ANY)
params = pltpu.CompilerParams(vmem_limit_bytes=56 * 1024 * 1024)


def flat(x, y, z, core):
    return (x * 2 + y // 2) * 16 + z * 4 + (y % 2) * 2 + core


def chips():
    return itertools.product(range(4), range(4), range(4), range(2))


def chip_groups():
    return [
        [flat(x, yh * 2 + yl, z, core) for z, yl in itertools.product(range(4), range(2))]
        for x, yh, core in itertools.product(range(4), range(2), range(2))
    ]


def other_core():
    return [(flat(x, y, z, c), flat(x, y, z, 1 - c)) for x, y, z, c in chips()]


def same_core_groups():
    return [
        [
            flat(x, yh * 2 + yl, z, core)
            for x, yh, z, yl in itertools.product(range(4), range(2), range(4), range(2))
        ]
        for core in range(2)
    ]


def dot(a, b):
    return jnp.dot(a, b, preferred_element_type=jnp.float32)


def dot_t(a, b):
    return lax.dot_general(a, b, (((1,), (1,)), ((), ())), preferred_element_type=jnp.float32)


def pack_kernel(latent_ref, out_ref):
    latent = latent_ref[...].astype(jnp.float32)
    rope = latent[:, LATENT:]
    parts = [latent[:, at : at + 128] for at in range(0, LATENT, 128)]
    parts.append(jnp.concatenate([rope[:8], rope[8:]], axis=1))
    piece = jnp.concatenate(parts, axis=0).astype(jnp.bfloat16)
    for place in range(64):
        out_ref[place] = piece


def pack(latent):
    return pl.pallas_call(
        pack_kernel,
        out_shape=jax.ShapeDtypeStruct((64, PIECE, 128), jnp.bfloat16),
        in_specs=[vmem],
        out_specs=vmem,
        name="pack",
    )(latent)


def unpack(own, other, keys):
    for block in range(POOL // BLOCK):
        for half, source in enumerate((own, other)):
            rows = slice(block * BLOCK + half * 128, block * BLOCK + half * 128 + 128)
            pieces = slice(block * 8, block * 8 + 8)
            for tile in range(4):
                keys[rows, tile * 128 : (tile + 1) * 128] = source[
                    pieces, tile * 16 : (tile + 1) * 16, :
                ].reshape(128, 128)
            rope = source[pieces, 64:72, :].astype(jnp.float32)
            left = lax.broadcasted_iota(jnp.int32, rope.shape, 2) < ROPE
            both = jnp.concatenate([jnp.where(left, rope, 0.0), jnp.where(left, 0.0, rope)], axis=1)
            keys[rows, LATENT:] = both.reshape(128, 128).astype(jnp.bfloat16)


def token_of_key(shape, dim, core):
    row = lax.broadcasted_iota(jnp.int32, shape, dim)
    owner = jnp.where((row // 128) % 2 == 0, core, 1 - core)
    return ((row % 128) // 16) * 32 + owner * 16 + row % 16


def absorb_kernel(
    info, pre_ref, step_ref, key_ref, latent_ref, length_ref, table_ref,
    pre_out, step_out, new_out, bias,
):
    core = info[1]
    for source, out in ((pre_ref, pre_out), (step_ref, step_out)):
        for pair in range(HEADS // 2):
            both = source[:, pair * 2 * HEAD : (pair + 1) * 2 * HEAD]
            for part in range(2):
                head = pair * 2 + part
                query = both[:, part * HEAD : (part + 1) * HEAD]
                key_map = key_ref[:, head * NOPE : (head + 1) * NOPE]
                out[head, :, :LATENT] = dot_t(query[:, :NOPE], key_map).astype(jnp.bfloat16)
                rope = query[:, NOPE:]
                out[head, :, LATENT:] = jnp.concatenate([rope, rope], axis=1)
    new_out[:, : LATENT + ROPE] = latent_ref[...]
    new_out[:, LATENT + ROPE :] = jnp.zeros((QUERIES, ROPE), jnp.bfloat16)
    table = table_ref[...]
    pages = table.shape[1]
    page = lax.broadcasted_iota(jnp.int32, table.shape, 1)
    slot = jnp.zeros(table.shape, jnp.int32)
    for place in range(pages):
        slot = slot + jnp.where(table[:, place : place + 1] == page, place, 0)
    limit = jnp.clip(length_ref[...] - slot * PAGE, 0, PAGE).astype(jnp.float32)
    shape = (pages, POOL)
    key = lax.broadcasted_iota(jnp.int32, shape, 1)
    of = (key // BLOCK) * (BLOCK // PAGE) + (key % 128) // (PAGE // 2)
    owner = (lax.broadcasted_iota(jnp.int32, shape, 0) == of).astype(jnp.bfloat16)
    spread = dot(limit.astype(jnp.bfloat16), owner)
    token = (token_of_key((ROWS, POOL), 1, core) % PAGE).astype(jnp.float32)
    rows = jnp.where(token < spread, 0.0, hidden)
    for step in range(STEPS):
        bias[step * ROWS : (step + 1) * ROWS, :POOL] = rows
    mine = lax.broadcasted_iota(jnp.int32, (QUERIES, QUERIES), 0)
    theirs = lax.broadcasted_iota(jnp.int32, (QUERIES, QUERIES), 1)
    seen = (mine % ROWS == theirs % ROWS) & (theirs // ROWS <= mine // ROWS)
    bias[:, POOL:] = jnp.where(seen, 0.0, hidden)


def absorb(info, pre_queries, step_queries, absorb_keys, step_latent, lengths, table):
    return pl.pallas_call(
        absorb_kernel,
        out_shape=(
            jax.ShapeDtypeStruct((HEADS, TOKENS, WIDTH), jnp.bfloat16),
            jax.ShapeDtypeStruct((HEADS, QUERIES, WIDTH), jnp.bfloat16),
            jax.ShapeDtypeStruct((QUERIES, WIDTH), jnp.bfloat16),
            jax.ShapeDtypeStruct((QUERIES, KEYS), jnp.float32),
        ),
        in_specs=[smem] + [vmem] * 6,
        out_specs=(vmem,) * 4,
        compiler_params=params,
        cost_estimate=pl.CostEstimate(
            flops=2 * 3072 * 128 * 512, bytes_accessed=12_000_000, transcendentals=0
        ),
        name="absorb",
    )(info, pre_queries, step_queries, absorb_keys, step_latent, lengths, table)


def softmax_rows(scores, bias, weights, start, count):
    bias_start = start % bias.shape[0]
    shifted = scores[start : start + count, :] + bias[bias_start : bias_start + count, :]
    largest = jnp.max(shifted, axis=1, keepdims=True)
    expo = jnp.exp2(shifted * to_exp2 - largest * to_exp2)
    weights[start : start + count, :] = expo.astype(jnp.bfloat16)
    return 1.0 / jnp.sum(expo, axis=1, keepdims=True)


def attend(queries, keys, bias, scores, weights, emit, block=16):
    count, rows = queries.shape[0], queries.shape[1]
    parts = [(at, min(BLOCK, keys.shape[0] - at)) for at in range(0, keys.shape[0], BLOCK)]

    def score(i, out, at, size):
        out[:, at : at + size] = dot_t(queries[i], keys[at : at + size, :])

    def item(i, now, later, weight, more):
        inverse = []
        turns = rows // block
        for turn in range(turns):
            if more:
                for at, size in parts[turn * len(parts) // turns : (turn + 1) * len(parts) // turns]:
                    score(i + 1, later, at, size)
            inverse.append(softmax_rows(now, bias, weight, turn * block, block))
        inverse = jnp.concatenate(inverse, axis=0)
        mixed = [
            (dot(weight[...], keys[:, at : at + 256]) * inverse).astype(jnp.bfloat16)
            for at in range(0, LATENT, 256)
        ]
        emit(i, jnp.concatenate(mixed, axis=1))

    for at, size in parts:
        score(0, scores[0], at, size)

    def two(turn, carry):
        item(2 * turn, scores[0], scores[1], weights[0], True)
        item(2 * turn + 1, scores[1], scores[0], weights[1], True)
        return carry

    lax.fori_loop(0, count // 2 - 1, two, 0)
    item(count - 2, scores[0], scores[1], weights[0], True)
    item(count - 1, scores[1], scores[0], weights[1], False)


def prefill_kernel(info, queries, own, other, value_ref, out_ref, keys, bias, s0, s1, w0, w1):
    ctx, core = info[0], info[1]
    unpack(own, other, keys)
    key = lax.broadcasted_iota(jnp.int32, (TOKENS, POOL), 1)
    token = (key // BLOCK) * BLOCK + token_of_key((TOKENS, POOL), 1, core)
    query = ctx * TOKENS + lax.broadcasted_iota(jnp.int32, (TOKENS, POOL), 0)
    bias[...] = jnp.where(token <= query, 0.0, hidden)

    def emit(i, mixed):
        columns = pl.ds(pl.multiple_of(i * VALUE_DIM, VALUE_DIM), VALUE_DIM)
        out_ref[:, columns] = dot(mixed, value_ref[:, columns]).astype(jnp.bfloat16)

    attend(queries, keys, bias, (s0, s1), (w0, w1), emit)


def prefill(info, queries, own, other, absorb_values):
    return pl.pallas_call(
        prefill_kernel,
        out_shape=jax.ShapeDtypeStruct((TOKENS, HEADS * VALUE_DIM), jnp.bfloat16),
        in_specs=[smem] + [vmem] * 4,
        out_specs=vmem,
        scratch_shapes=[
            pltpu.VMEM((POOL, WIDTH), jnp.bfloat16),
            pltpu.VMEM((TOKENS, POOL), jnp.float32),
            pltpu.VMEM((TOKENS, POOL), jnp.float32),
            pltpu.VMEM((TOKENS, POOL), jnp.float32),
            pltpu.VMEM((TOKENS, POOL), jnp.bfloat16),
            pltpu.VMEM((TOKENS, POOL), jnp.bfloat16),
        ],
        compiler_params=params,
        cost_estimate=pl.CostEstimate(
            flops=2 * 2048 * 2048 * 1280, bytes_accessed=10_000_000, transcendentals=2048 * 2048
        ),
        name="prefill",
    )(info, queries, own, other, absorb_values)


def decode_kernel(
    info, queries, own, other, newest, bias, value_ref, weight_hbm,
    keep_ref, send_ref, keys, s0, s1, w0, w1, heads_out, weight, sem,
):
    core = info[1]
    load = pltpu.make_async_copy(weight_hbm, weight, sem)
    load.start()
    unpack(own, other, keys)
    keys[POOL:, :] = newest[...]

    def emit(i, mixed):
        for part in range(2):
            columns = pl.ds(pl.multiple_of((i * 2 + part) * VALUE_DIM, VALUE_DIM), VALUE_DIM)
            rows = mixed[part * QUERIES : (part + 1) * QUERIES]
            heads_out[:, columns] = dot(rows, value_ref[:, columns]).astype(jnp.bfloat16)

    attend(queries, keys, bias, (s0, s1), (w0, w1), emit)
    load.wait()

    def project(place, carry):
        columns = pl.ds(pl.multiple_of(place * 2 * SHARE, 2 * SHARE), 2 * SHARE)
        turned = dot(heads_out[...], weight[:, columns]).T
        first, second = turned[:SHARE], turned[SHARE:]
        keep_ref[place] = jnp.where(core == 0, first, second).astype(jnp.bfloat16)
        send_ref[place] = jnp.where(core == 0, second, first).astype(jnp.bfloat16)
        return carry

    lax.fori_loop(0, MODEL // (2 * SHARE), project, 0)


def decode(info, queries, own, other, newest, bias, absorb_values, out_weight):
    share = jax.ShapeDtypeStruct((8, SHARE, QUERIES), jnp.bfloat16)
    return pl.pallas_call(
        decode_kernel,
        out_shape=(share, share),
        in_specs=[smem] + [vmem] * 6 + [anywhere],
        out_specs=(vmem, vmem),
        scratch_shapes=[
            pltpu.VMEM((KEYS, WIDTH), jnp.bfloat16),
            pltpu.VMEM((2 * QUERIES, KEYS), jnp.float32),
            pltpu.VMEM((2 * QUERIES, KEYS), jnp.float32),
            pltpu.VMEM((2 * QUERIES, KEYS), jnp.bfloat16),
            pltpu.VMEM((2 * QUERIES, KEYS), jnp.bfloat16),
            pltpu.VMEM((QUERIES, HEADS * VALUE_DIM), jnp.bfloat16),
            pltpu.VMEM((HEADS * VALUE_DIM, MODEL), jnp.bfloat16),
            pltpu.SemaphoreType.DMA(()),
        ],
        compiler_params=params,
        cost_estimate=pl.CostEstimate(
            flops=2 * 1024 * 2176 * 1280 + 2 * 128 * 1024 * 7168,
            bytes_accessed=22_000_000,
            transcendentals=1024 * 2176,
        ),
        name="decode",
    )(info, queries, own, other, newest, bias, absorb_values, out_weight)


def gather_sum_kernel(parts, out_ref):
    total = parts[0].astype(jnp.float32)
    for place in range(1, parts.shape[0]):
        total = total + parts[place].astype(jnp.float32)
    out_ref[...] = total.T.astype(jnp.bfloat16)


def gather_sum(parts):
    return pl.pallas_call(
        gather_sum_kernel,
        out_shape=jax.ShapeDtypeStruct((QUERIES, SHARE), jnp.bfloat16),
        in_specs=[vmem],
        out_specs=vmem,
        name="gather_sum",
    )(parts)


def on_device(
    pre_queries,
    pre_latent,
    absorb_keys,
    absorb_values,
    step_queries,
    step_latent,
    context_lengths,
    page_table,
    out_weight,
):
    tp = lax.axis_index("tp")
    info = jnp.stack([lax.axis_index("ctx"), tp % 2]).astype(jnp.int32)
    own = lax.all_to_all(pack(pre_latent), BOTH, 0, 0, axis_index_groups=same_core_groups())
    ready = absorb(
        info,
        pre_queries,
        step_queries.reshape(QUERIES, HEADS * HEAD),
        absorb_keys,
        step_latent.reshape(QUERIES, LATENT + ROPE),
        context_lengths.reshape(ROWS, 1),
        page_table,
    )
    own, *ready = lax.optimization_barrier((own, *ready))
    pre_joined, step_joined, newest, bias = ready
    other = lax.ppermute(own, BOTH, other_core())
    keep, send = decode(
        info,
        step_joined.reshape(HEADS // 2, 2 * QUERIES, WIDTH),
        own,
        other,
        newest,
        bias,
        absorb_values,
        out_weight,
    )
    arrived = lax.ppermute(send, BOTH, other_core())
    chip = (keep.astype(jnp.float32) + arrived.astype(jnp.float32)).astype(jnp.bfloat16)
    chip, own, other = lax.optimization_barrier((chip, own, other))
    parts = lax.all_to_all(chip, BOTH, 0, 0, axis_index_groups=chip_groups())
    prefill_heads = prefill(info, pre_joined, own, other, absorb_values)
    decode_out = gather_sum(parts).reshape(STEPS, ROWS, SHARE)
    return (prefill_heads, decode_out)


def solution(mesh):
    return jax.shard_map(
        on_device,
        mesh=mesh,
        in_specs=(
            P("ctx", "tp"),
            P(("ctx", "tp"), None),
            P(None, "tp"),
            P(None, "tp"),
            P(None, "ctx", "tp"),
            P(None, "ctx", None),
            P("ctx"),
            P("ctx", None),
            P("tp", None),
        ),
        out_specs=(P("ctx", "tp"), P(None, "ctx", "tp")),
        check_vma=False,
    )
```

time: 100 us -> 87.2 us (0.87)
  blocking collectives: 32 us -> 0 us
  waiting for transfers between devices: 3.08 us -> 17.6 us
  starting transfers between devices: 9.83 us -> 18.4 us
  local copies, waits for them, and re-layouts: 6.64 us -> 2.66 us
  other arithmetic: 1.33 us -> 3 us
    all_to_all x1 -> x0, blocking collectives: 32 us -> none  [on_device(): lax.all_to_all(jnp.broadcast_to(pre_latent[None], (64, 16, WIDTH)), BOTH,...]
    all_to_all x0 -> x2, starting transfers between devices: none -> 15.7 us  [the longest x1 12 us: on_device(): lax.all_to_all(pack(pre_latent), BOTH, 0, 0, axis_index_groups=same_core_...]
    all_to_all x0 -> x2, waiting for transfers between devices: none -> 12.8 us  [the longest x1 12.8 us: on_device(): lax.all_to_all(pack(pre_latent), BOTH, 0, 0, axis_index_groups=same_core_...]
    ppermute x9 -> x2, starting transfers between devices: 9.83 us -> 2.69 us  [the longest x1 2.24 us: on_device(): other = lax.ppermute(own, BOTH, other_core())]
    pallas_call x1, Pallas kernels: 22.6 us -> 19.6 us  [prefill(): pl.pallas_call(prefill_kernel, out_shape=jax.ShapeDtypeStruct((TOKENS, HE...]
    convert_element_type x2 -> x1, other arithmetic: 0.32 us -> 2.36 us  [on_device(): (keep.astype(jnp.float32) + arrived.astype(jnp.float32)).astype(jnp.bfloa...]
    unnamed x8, local copies, waits for them, and re-layouts: 0.02 us -> 1.97 us
    ppermute x9 -> x2, waiting for transfers between devices: 3.08 us -> 4.79 us  [the longest x1 2.47 us: on_device(): other = lax.ppermute(own, BOTH, other_core())]
  transfers between devices with their start and end apart: 9 -> 4, of which waited for: 2 -> 3; matrix products, arithmetic and copies ran while one was open for 1% -> 2% of each run, Pallas kernels for 27% -> 28%
where the time goes in v2:
time: 87.2 us; the launch traced here: 86.8 us
  Pallas kernels  44.5 us (51%)
  starting transfers between devices  18.4 us (21%)
  waiting for transfers between devices  17.6 us (20%)
  other arithmetic  3 us (3%)
  local copies, waits for them, and re-layouts  2.66 us (3%)
    pallas_call x1, Pallas kernels, prefill(): pl.pallas_call(prefill_kernel, out_shape=jax.ShapeDtypeStruct((TOKENS, HE...  19.6 us
    pallas_call x1, Pallas kernels, decode(): pl.pallas_call(decode_kernel, out_shape=(share, share), in_specs=[smem] +...  16.2 us
    all_to_all x1, waiting for transfers between devices, on_device(): lax.all_to_all(pack(pre_latent), BOTH, 0, 0, axis_index_groups=same_core_...  12.8 us
    all_to_all x1, starting transfers between devices, on_device(): lax.all_to_all(pack(pre_latent), BOTH, 0, 0, axis_index_groups=same_core_...  12 us
    pallas_call x1, Pallas kernels, absorb(): pl.pallas_call(absorb_kernel, out_shape=(jax.ShapeDtypeStruct((HEADS, TOK...  4.78 us
    all_to_all x1, starting transfers between devices, on_device(): parts = lax.all_to_all(chip, BOTH, 0, 0, axis_index_groups=chip_groups())  3.73 us
    ppermute x1, waiting for transfers between devices, on_device(): other = lax.ppermute(own, BOTH, other_core())  2.47 us
    convert_element_type x1, other arithmetic, on_device(): (keep.astype(jnp.float32) + arrived.astype(jnp.float32)).astype(jnp.bfloa...  2.36 us
  transfers between devices with their start and end apart: 4, of which 3 were waited for; matrix products, arithmetic and copies ran while one was open for 2% of the time, Pallas kernels for 28%

profile of v2, /device:TPU:1, one launch (start us, length us, event | category | flops | bytes accessed | tf_op | source)
XLA Modules:
  0.0 86.8 jit_solution(13655425054168321241)
XLA Ops:
  0.6 0.0 copy-start.2
  0.6 1.9 %pack.1 = bf16[64,72,128]{2,1,0:T(8,128)(2,1)} custom-call(bf16[16,576]{1,0:T(8,128)(2,1)} %latent_ref.1), custom_call_target="tpu_custom_call" | custom-call | tf_op jit(solution)/shard_map/pack/pallas_call | solution.py:88
  2.5 12.0 %all-to-all-start = ((bf16[64,72,128]{2,1,0:T(8,128)(2,1)}), bf16[64,72,128]{2,1,0:T(8,128)(2,1)S(1)}, u32[]{:S(2)}, u32[]{:S(2)}) async-start(bf16[64,72,128]{2,1,0:T(8,128)(2,1)} %pack.1), calls=%async_computation | async-start | bytes 2359296 | tf_op jit(solution)/shard_map/all_to_all | solution.py:344
  14.5 0.0 copy-done.2
  14.5 0.7 copy.11.length_ref
  15.2 0.6 pad_add_fusion.info
  15.9 4.8 %absorb.1 = (bf16[8,256,640]{2,1,0:T(8,128)(2,1)}, bf16[8,128,640]{2,1,0:T(8,128)(2,1)}, bf16[128,640]{1,0:T(8,128)(2,1)}, f32[128,2176]{1,0:T(8,128)}) custom-call(s32[2]{0:T(128)} %pad_add_fusion.info, bf16[256,1536]{1,0:T(8,128)(2,1)} %pre_ref.1, bf16[128,1536]{1,0:T(8,128)(2,1)} %bitcast.7, bf16[512,1024]{1,0:T(8,128)(2,1)} %key_ref.1, ...), custom_call_target="tpu_custom_call" | custom-call | flops 402653184 | bytes 12000000 | tf_op jit(solution)/shard_map/absorb/pallas_call | solution.py:158
  20.6 12.8 %all-to-all-done.own = bf16[64,72,128]{2,1,0:T(8,128)(2,1)S(1)} async-done(((bf16[64,72,128]{2,1,0:T(8,128)(2,1)}), bf16[64,72,128]{2,1,0:T(8,128)(2,1)S(1)}, u32[]{:S(2)}, u32[]{:S(2)}) %all-to-all-start) | async-done | bytes 1179680 | tf_op jit(solution)/shard_map/all_to_all | solution.py:344
  33.4 0.0 copy-start.1
  33.4 2.2 %collective-permute-start = (bf16[64,72,128]{2,1,0:T(8,128)(2,1)S(1)}, bf16[64,72,128]{2,1,0:T(8,128)(2,1)S(1)}, u32[]{:S(2)}, u32[]{:S(2)}) collective-permute-start(bf16[64,72,128]{2,1,0:T(8,128)(2,1)S(1)} %all-to-all-done.own), channel_id=1, source_target_pairs={{0,1},{1,0},{4,5},{5,4},{8,9},{9,8},{12,13},{13,12},{2,3},{3,2},{6... | collective-permute-start | bytes 3538952 | tf_op jit(solution)/shard_map/ppermute | solution.py:356
  35.7 2.5 %collective-permute-done.other = bf16[64,72,128]{2,1,0:T(8,128)(2,1)S(1)} collective-permute-done((bf16[64,72,128]{2,1,0:T(8,128)(2,1)S(1)}, bf16[64,72,128]{2,1,0:T(8,128)(2,1)S(1)}, u32[]{:S(2)}, u32[]{:S(2)}) %collective-permute-start) | collective-permute-done | bytes 1179680 | tf_op jit(solution)/shard_map/ppermute | solution.py:356
  38.1 0.0 copy-start.3
  38.1 0.0 copy-done.1
  38.1 1.0 %copy-done.3 = bf16[64,72,128]{2,1,0:T(8,128)(2,1)} copy-done((bf16[64,72,128]{2,1,0:T(8,128)(2,1)}, bf16[64,72,128]{2,1,0:T(8,128)(2,1)S(1)}, u32[]{:S(2)}) %copy-start.3) | copy-done | bytes 1179672
  39.2 16.2 %decode.1 = (bf16[8,448,128]{2,1,0:T(8,128)(2,1)}, bf16[8,448,128]{2,1,0:T(8,128)(2,1)}) custom-call(s32[2]{0:T(128)} %pad_add_fusion.info, bf16[4,256,640]{2,1,0:T(8,128)(2,1)} %bitcast.11, bf16[64,72,128]{2,1,0:T(8,128)(2,1)} %copy-done.1, bf16[64,72,128]{2,1,0:T(8,128)(2,1)} %copy-done.3, bf16[128,640]{1,0:T(8,128)(2,1)} %get-tuple-element.23.newest, ...), custom_call_target="tpu_custom_call" | custom-call | flops 7583301632 | bytes 22000000 | tf_op jit(solution)/shard_map/decode/pallas_call | solution.py:289
  55.4 0.5 collective-permute-start.1
  55.8 2.3 %collective-permute-done.1 = bf16[8,448,128]{2,1,0:T(8,128)(2,1)S(1)} collective-permute-done((bf16[8,448,128]{2,1,0:T(8,128)(2,1)}, bf16[8,448,128]{2,1,0:T(8,128)(2,1)S(1)}, u32[]{:S(2)}, u32[]{:S(2)}) %collective-permute-start.1) | collective-permute-done | bytes 917536 | tf_op jit(solution)/shard_map/ppermute | solution.py:367
  58.2 2.4 %add_convert_fusion = bf16[8,448,128]{2,1,0:T(8,128)(2,1)} fusion(bf16[8,448,128]{2,1,0:T(8,128)(2,1)S(1)} %collective-permute-done.1, bf16[8,448,128]{2,1,0:T(8,128)(2,1)} %get-tuple-element.25), kind=kLoop, calls=%fused_computation | loop fusion | flops 1835008 | bytes 2752512 | tf_op jit(solution)/shard_map/convert_element_type | solution.py:368
  60.5 3.7 %all-to-all-start.1 = ((bf16[8,448,128]{2,1,0:T(8,128)(2,1)}), bf16[8,448,128]{2,1,0:T(8,128)(2,1)S(1)}, u32[]{:S(2)}, u32[]{:S(2)}) async-start(bf16[8,448,128]{2,1,0:T(8,128)(2,1)} %add_convert_fusion), calls=%async_computation.1 | async-start | bytes 1835008 | tf_op jit(solution)/shard_map/all_to_all | solution.py:370
  64.3 19.6 %prefill.1 = bf16[256,1024]{1,0:T(8,128)(2,1)} custom-call(s32[2]{0:T(128)} %pad_add_fusion.info, bf16[8,256,640]{2,1,0:T(8,128)(2,1)} %get-tuple-element.20.queries, bf16[64,72,128]{2,1,0:T(8,128)(2,1)} %copy-done.1, bf16[64,72,128]{2,1,0:T(8,128)(2,1)} %copy-done.3, bf16[512,1024]{1,0:T(8,128)(2,1)} %value_ref.3), custom_call_target="tpu_custom_call" | custom-call | flops 10737418240 | bytes 10000000 | tf_op jit(solution)/shard_map/prefill/pallas_call | solution.py:236
  83.9 0.0 all-to-all-done.1.parts
  83.9 0.0 copy-start
  83.9 0.9 %copy-done = bf16[8,448,128]{2,1,0:T(8,128)(2,1)} copy-done((bf16[8,448,128]{2,1,0:T(8,128)(2,1)}, bf16[8,448,128]{2,1,0:T(8,128)(2,1)S(1)}, u32[]{:S(2)}) %copy-start) | copy-done | bytes 917528
  84.8 2.0 %gather_sum.1 = bf16[128,448]{1,0:T(8,128)(2,1)} custom-call(bf16[8,448,128]{2,1,0:T(8,128)(2,1)} %copy-done), custom_call_target="tpu_custom_call" | custom-call | tf_op jit(solution)/shard_map/gather_sum/pallas_call | solution.py:322
Async XLA Ops:
  0.6 13.9 %copy-start.2 = (s32[32]{0:T(128)S(1)}, s32[32]{0:T(128)}, u32[]{:S(2)}) copy-start(s32[32]{0:T(128)} %param.15) | copy-start | bytes 388
  2.5 30.9 %all-to-all-start = ((bf16[64,72,128]{2,1,0:T(8,128)(2,1)}), bf16[64,72,128]{2,1,0:T(8,128)(2,1)S(1)}, u32[]{:S(2)}, u32[]{:S(2)}) async-start(bf16[64,72,128]{2,1,0:T(8,128)(2,1)} %pack.1), calls=%async_computation | async-start | bytes 2359296 | tf_op jit(solution)/shard_map/all_to_all | solution.py:344
  33.4 4.7 %copy-start.1 = (bf16[64,72,128]{2,1,0:T(8,128)(2,1)}, bf16[64,72,128]{2,1,0:T(8,128)(2,1)S(1)}, u32[]{:S(2)}) copy-start(bf16[64,72,128]{2,1,0:T(8,128)(2,1)S(1)} %all-to-all-done.own) | copy-start | bytes 3538948
  33.4 4.7 %collective-permute-start = (bf16[64,72,128]{2,1,0:T(8,128)(2,1)S(1)}, bf16[64,72,128]{2,1,0:T(8,128)(2,1)S(1)}, u32[]{:S(2)}, u32[]{:S(2)}) collective-permute-start(bf16[64,72,128]{2,1,0:T(8,128)(2,1)S(1)} %all-to-all-done.own), channel_id=1, source_target_pairs={{0,1},{1,0},{4,5},{5,4},{8,9},{9,8},{12,13},{13,12},{2,3},{3,2},{6... | collective-permute-start | bytes 3538952 | tf_op jit(solution)/shard_map/ppermute | solution.py:356
  38.1 1.0 %copy-start.3 = (bf16[64,72,128]{2,1,0:T(8,128)(2,1)}, bf16[64,72,128]{2,1,0:T(8,128)(2,1)S(1)}, u32[]{:S(2)}) copy-start(bf16[64,72,128]{2,1,0:T(8,128)(2,1)S(1)} %collective-permute-done.other) | copy-start | bytes 3538948
  55.4 2.8 %collective-permute-start.1 = (bf16[8,448,128]{2,1,0:T(8,128)(2,1)}, bf16[8,448,128]{2,1,0:T(8,128)(2,1)S(1)}, u32[]{:S(2)}, u32[]{:S(2)}) collective-permute-start(bf16[8,448,128]{2,1,0:T(8,128)(2,1)} %get-tuple-element.26), channel_id=1, source_target_pairs={{0,1},{1,0},{4,5},{5,4},{8,9},{9,8},{12,13},{13,12},{2,3},{3,2},{6... | collective-permute-start | bytes 2752520 | tf_op jit(solution)/shard_map/ppermute | solution.py:367
  60.5 23.3 %all-to-all-start.1 = ((bf16[8,448,128]{2,1,0:T(8,128)(2,1)}), bf16[8,448,128]{2,1,0:T(8,128)(2,1)S(1)}, u32[]{:S(2)}, u32[]{:S(2)}) async-start(bf16[8,448,128]{2,1,0:T(8,128)(2,1)} %add_convert_fusion), calls=%async_computation.1 | async-start | bytes 1835008 | tf_op jit(solution)/shard_map/all_to_all | solution.py:370
  83.9 0.9 %copy-start = (bf16[8,448,128]{2,1,0:T(8,128)(2,1)}, bf16[8,448,128]{2,1,0:T(8,128)(2,1)S(1)}, u32[]{:S(2)}) copy-start(bf16[8,448,128]{2,1,0:T(8,128)(2,1)S(1)} %all-to-all-done.1.parts) | copy-start | bytes 2752516

commit v3 on v2

v3 whole, which is shorter than its diff:
```python
import functools
import itertools
import math

import jax
import jax.numpy as jnp
from jax import lax
from jax.experimental import pallas as pl
from jax.experimental.pallas import tpu as pltpu
from jax.sharding import PartitionSpec as P

LATENT = 512
ROPE = 64
NOPE = 128
VALUE_DIM = 128
PAGE = 64
STEPS = 4
WIDTH = LATENT + 2 * ROPE
DIRECT = NOPE + 2 * ROPE
PIECE = 72
BLOCK = 256
HEAD = NOPE + ROPE
HEADS = 8
TOKENS = 256
ROWS = 32
QUERIES = STEPS * ROWS
POOL = 2048
KEYS = POOL + QUERIES
MODEL = 7168
SHARE = 448
BOTH = ("ctx", "tp")
NEWEST = HEADS * QUERIES
BIAS = NEWEST + QUERIES

hidden = -1e30
CUT = 1024
SOFT = 16
DECODE_CUT = 256
ATTEND_MIB = 52
to_exp2 = math.log2(math.e) / math.sqrt(HEAD)
vmem = pl.BlockSpec(memory_space=pltpu.VMEM)
smem = pl.BlockSpec(memory_space=pltpu.SMEM)
hbm = pl.BlockSpec(memory_space=pltpu.HBM)


def params(mib):
    return pltpu.CompilerParams(vmem_limit_bytes=mib * 1024 * 1024)


def flat(x, y, z, core):
    return (x * 2 + y // 2) * 16 + z * 4 + (y % 2) * 2 + core


def chips():
    return itertools.product(range(4), range(4), range(4), range(2))


def chip_groups():
    return [
        [flat(x, yh * 2 + yl, z, core) for z, yl in itertools.product(range(4), range(2))]
        for x, yh, core in itertools.product(range(4), range(2), range(2))
    ]


def other_core():
    return [(flat(x, y, z, c), flat(x, y, z, 1 - c)) for x, y, z, c in chips()]


def same_core_groups():
    return [
        [
            flat(x, yh * 2 + yl, z, core)
            for x, yh, z, yl in itertools.product(range(4), range(2), range(4), range(2))
        ]
        for core in range(2)
    ]


def dot(a, b):
    return jnp.dot(a, b, preferred_element_type=jnp.float32)


def dot_t(a, b):
    return lax.dot_general(a, b, (((1,), (1,)), ((), ())), preferred_element_type=jnp.float32)


def pack_kernel(latent_ref, out_ref):
    latent = latent_ref[...].astype(jnp.float32)
    rope = latent[:, LATENT:]
    parts = [latent[:, at : at + 128] for at in range(0, LATENT, 128)]
    parts.append(jnp.concatenate([rope[:8], rope[8:]], axis=1))
    piece = jnp.concatenate(parts, axis=0).astype(jnp.bfloat16)
    for place in range(64):
        out_ref[place] = piece


def pack(latent):
    return pl.pallas_call(
        pack_kernel,
        out_shape=jax.ShapeDtypeStruct((64, PIECE, 128), jnp.bfloat16),
        in_specs=[vmem],
        out_specs=vmem,
        name="pack",
    )(latent)


def unpack(own, other, latent, ropes):
    for block in range(POOL // BLOCK):
        for half, source in enumerate((own, other)):
            rows = slice(block * BLOCK + half * 128, block * BLOCK + half * 128 + 128)
            pieces = slice(block * 8, block * 8 + 8)
            for tile in range(4):
                latent[rows, tile * 128 : (tile + 1) * 128] = source[
                    pieces, tile * 16 : (tile + 1) * 16, :
                ].reshape(128, 128)
            rope = source[pieces, 64:72, :].astype(jnp.float32)
            left = lax.broadcasted_iota(jnp.int32, rope.shape, 2) < ROPE
            both = jnp.concatenate([jnp.where(left, rope, 0.0), jnp.where(left, 0.0, rope)], axis=1)
            both = both.reshape(128, 128).astype(jnp.bfloat16)
            for ref in ropes:
                ref[rows, ref.shape[1] - 2 * ROPE :] = both


def token_of_key(shape, dim, core):
    row = lax.broadcasted_iota(jnp.int32, shape, dim)
    owner = jnp.where((row // 128) % 2 == 0, core, 1 - core)
    return ((row % 128) // 16) * 32 + owner * 16 + row % 16


def absorb_kernel(info, query_ref, key_ref, latent_ref, length_ref, table_ref, out):
    core = info[1]
    for pair in range(HEADS // 2):
        both = query_ref[:, pair * 2 * HEAD : (pair + 1) * 2 * HEAD]
        for part in range(2):
            head = pair * 2 + part
            query = both[:, part * HEAD : (part + 1) * HEAD]
            key_map = key_ref[:, head * NOPE : (head + 1) * NOPE]
            rows = slice(head * QUERIES, (head + 1) * QUERIES)
            out[rows, :LATENT] = dot_t(query[:, :NOPE], key_map).astype(jnp.bfloat16)
            rope = query[:, NOPE:]
            out[rows, LATENT:] = jnp.concatenate([rope, rope], axis=1)
    rows = slice(NEWEST, NEWEST + QUERIES)
    out[rows, : LATENT + ROPE] = latent_ref[...]
    out[rows, LATENT + ROPE :] = jnp.zeros((QUERIES, ROPE), jnp.bfloat16)
    table = table_ref[...]
    pages = table.shape[1]
    page = lax.broadcasted_iota(jnp.int32, table.shape, 1)
    slot = jnp.zeros(table.shape, jnp.int32)
    for place in range(pages):
        slot = slot + jnp.where(table[:, place : place + 1] == page, place, 0)
    limit = jnp.clip(length_ref[...] - slot * PAGE, 0, PAGE).astype(jnp.float32)
    shape = (pages, POOL)
    key = lax.broadcasted_iota(jnp.int32, shape, 1)
    of = (key // BLOCK) * (BLOCK // PAGE) + (key % 128) // (PAGE // 2)
    owner = (lax.broadcasted_iota(jnp.int32, shape, 0) == of).astype(jnp.bfloat16)
    spread = dot(limit.astype(jnp.bfloat16), owner)
    token = (token_of_key((ROWS, POOL), 1, core) % PAGE).astype(jnp.float32)
    pool = jnp.where(token < spread, 0.0, hidden)
    mine = lax.broadcasted_iota(jnp.int32, (QUERIES, QUERIES), 0)
    theirs = lax.broadcasted_iota(jnp.int32, (QUERIES, QUERIES), 1)
    seen = (mine % ROWS == theirs % ROWS) & (theirs // ROWS <= mine // ROWS)
    bias = jnp.concatenate([pool] * STEPS, axis=0)
    bias = jnp.concatenate([bias, jnp.where(seen, 0.0, hidden)], axis=1).astype(jnp.bfloat16)
    for at in range(0, KEYS, WIDTH):
        part = bias[:, at : at + WIDTH]
        row = BIAS + at // WIDTH * QUERIES
        out[row : row + QUERIES, : part.shape[1]] = part


def absorb(info, queries, absorb_keys, step_latent, lengths, table):
    return pl.pallas_call(
        absorb_kernel,
        out_shape=jax.ShapeDtypeStruct((BIAS + 4 * QUERIES, WIDTH), jnp.bfloat16),
        in_specs=[smem] + [vmem] * 5,
        out_specs=vmem,
        compiler_params=params(56),
        cost_estimate=pl.CostEstimate(
            flops=2 * 1024 * 128 * 512, bytes_accessed=5_000_000, transcendentals=0
        ),
        name="absorb",
    )(info, queries, absorb_keys, step_latent, lengths, table)


def softmax_rows(scores, bias, weights, start, count):
    bias_start = start % bias.shape[0]
    shifted = scores[start : start + count, :] + bias[bias_start : bias_start + count, :]
    largest = jnp.max(shifted, axis=1, keepdims=True)
    expo = jnp.exp2(shifted * to_exp2 - largest * to_exp2)
    weights[start : start + count, :] = expo.astype(jnp.bfloat16)
    return 1.0 / jnp.sum(expo, axis=1, keepdims=True)


def prefill_kernel(
    info, own, other, query_ref, key_map, value_map, out_ref, queries, latent, bias, *held
):
    ctx, core = info[0], info[1]
    keys, values, scores, weights = held[:2], held[2:6], held[6:8], held[8:]
    unpack(own, other, latent, keys)
    for pair in range(HEADS // 2):
        both = query_ref[:, pair * 2 * HEAD : (pair + 1) * 2 * HEAD]
        for part in range(2):
            query = both[:, part * HEAD : (part + 1) * HEAD]
            rope = query[:, NOPE:]
            queries[pair * 2 + part] = jnp.concatenate([query[:, :NOPE], rope, rope], axis=1)
    key = lax.broadcasted_iota(jnp.int32, (TOKENS, POOL), 1)
    token = (key // BLOCK) * BLOCK + token_of_key((TOKENS, POOL), 1, core)
    query = ctx * TOKENS + lax.broadcasted_iota(jnp.int32, (TOKENS, POOL), 0)
    bias[...] = jnp.where(token <= query, 0.0, hidden)
    inverse = {}

    def make(head, at):
        columns = slice(head * NOPE, (head + 1) * NOPE)
        maps = jnp.concatenate([key_map[:, columns], value_map[:, columns]], axis=1)
        made = dot(latent[at : at + CUT, :], maps).astype(jnp.bfloat16)
        keys[head % 2][at : at + CUT, :NOPE] = made[:, :NOPE]
        values[head % 4][at : at + CUT, :] = made[:, NOPE:]

    def score(head, at):
        scores[head % 2][:, at : at + CUT] = dot_t(queries[head], keys[head % 2][at : at + CUT, :])

    def soften(head, start):
        part = softmax_rows(scores[head % 2], bias, weights[head % 2], start, SOFT)
        inverse.setdefault(head, []).append(part)

    def mix(head):
        mixed = dot(weights[head % 2][...], values[head % 4][...])
        scaled = mixed * jnp.concatenate(inverse[head], axis=0)
        out_ref[:, head * VALUE_DIM : (head + 1) * VALUE_DIM] = scaled.astype(jnp.bfloat16)

    turns = TOKENS // SOFT
    cuts = POOL // CUT
    for stage in range(HEADS + 3):
        if 0 <= stage - 3 < HEADS:
            mix(stage - 3)
        for turn in range(turns):
            for cut in range(turn * cuts // turns, (turn + 1) * cuts // turns):
                if 0 <= stage - 1 < HEADS:
                    score(stage - 1, cut * CUT)
                if stage < HEADS:
                    make(stage, cut * CUT)
            if 0 <= stage - 2 < HEADS:
                soften(stage - 2, turn * SOFT)


def prefill(info, own, other, queries, absorb_keys, absorb_values):
    return pl.pallas_call(
        prefill_kernel,
        out_shape=jax.ShapeDtypeStruct((TOKENS, HEADS * VALUE_DIM), jnp.bfloat16),
        in_specs=[smem] + [vmem] * 5,
        out_specs=vmem,
        scratch_shapes=[
            pltpu.VMEM((HEADS, TOKENS, DIRECT), jnp.bfloat16),
            pltpu.VMEM((POOL, LATENT), jnp.bfloat16),
            pltpu.VMEM((TOKENS, POOL), jnp.float32),
            *[pltpu.VMEM((POOL, DIRECT), jnp.bfloat16)] * 2,
            *[pltpu.VMEM((POOL, VALUE_DIM), jnp.bfloat16)] * 4,
            *[pltpu.VMEM((TOKENS, POOL), jnp.float32)] * 2,
            *[pltpu.VMEM((TOKENS, POOL), jnp.bfloat16)] * 2,
        ],
        compiler_params=params(ATTEND_MIB),
        cost_estimate=pl.CostEstimate(
            flops=2 * 2048 * 2048 * 1024, bytes_accessed=10_000_000, transcendentals=2048 * 2048
        ),
        name="prefill",
    )(info, own, other, queries, absorb_keys, absorb_values)


def decode_kernel(
    info, own, other, ready, value_ref, weight_hbm,
    keep_ref, send_ref, weight, sem, keys, bias, s0, s1, w0, w1, heads_out,
):
    core = info[1]
    load = pltpu.make_async_copy(weight_hbm, weight, sem)
    load.start()
    unpack(own, other, keys, [keys])
    keys[POOL:, :] = ready[NEWEST:BIAS, :]
    for at in range(0, KEYS, WIDTH):
        row = BIAS + at // WIDTH * QUERIES
        size = min(WIDTH, KEYS - at)
        bias[:, at : at + size] = ready[row : row + QUERIES, :size].astype(jnp.float32)
    scores, weights = (s0, s1), (w0, w1)
    inverse = {}
    items = HEADS // 2
    rows = 2 * QUERIES

    def score(item, at, size):
        queries = ready[item * rows : (item + 1) * rows, :]
        scores[item % 2][:, at : at + size] = dot_t(queries, keys[at : at + size, :])

    def soften(item, start):
        part = softmax_rows(scores[item % 2], bias, weights[item % 2], start, SOFT)
        inverse.setdefault(item, []).append(part)

    def mix(item):
        scale = jnp.concatenate(inverse[item], axis=0)
        mixed = [
            (dot(weights[item % 2][...], keys[:, at : at + 256]) * scale).astype(jnp.bfloat16)
            for at in range(0, LATENT, 256)
        ]
        mixed = jnp.concatenate(mixed, axis=1)
        for part in range(2):
            head = item * 2 + part
            columns = slice(head * VALUE_DIM, (head + 1) * VALUE_DIM)
            heads_out[:, columns] = dot(
                mixed[part * QUERIES : (part + 1) * QUERIES], value_ref[:, columns]
            ).astype(jnp.bfloat16)

    turns = rows // SOFT
    parts = [(at, min(DECODE_CUT, KEYS - at)) for at in range(0, KEYS, DECODE_CUT)]
    for stage in range(items + 2):
        if 0 <= stage - 2 < items:
            mix(stage - 2)
        for turn in range(turns):
            if stage < items:
                for at, size in parts[turn * len(parts) // turns : (turn + 1) * len(parts) // turns]:
                    score(stage, at, size)
            if 0 <= stage - 1 < items:
                soften(stage - 1, turn * SOFT)
    load.wait()

    for place in range(8):
        columns = slice(place * 2 * SHARE, (place + 1) * 2 * SHARE)
        turned = dot(heads_out[...], weight[:, columns]).T
        first, second = turned[:SHARE], turned[SHARE:]
        keep_ref[place] = jnp.where(core == 0, first, second).astype(jnp.bfloat16)
        send_ref[place] = jnp.where(core == 0, second, first).astype(jnp.bfloat16)


def decode(info, own, other, ready, absorb_values, out_weight):
    share = jax.ShapeDtypeStruct((8, SHARE, QUERIES), jnp.bfloat16)
    return pl.pallas_call(
        decode_kernel,
        out_shape=(share, share),
        in_specs=[smem] + [vmem] * 4 + [hbm],
        out_specs=(vmem, vmem),
        scratch_shapes=[
            pltpu.VMEM((HEADS * VALUE_DIM, MODEL), jnp.bfloat16),
            pltpu.SemaphoreType.DMA(()),
            pltpu.VMEM((KEYS, WIDTH), jnp.bfloat16),
            pltpu.VMEM((QUERIES, KEYS), jnp.float32),
            pltpu.VMEM((2 * QUERIES, KEYS), jnp.float32),
            pltpu.VMEM((2 * QUERIES, KEYS), jnp.float32),
            pltpu.VMEM((2 * QUERIES, KEYS), jnp.bfloat16),
            pltpu.VMEM((2 * QUERIES, KEYS), jnp.bfloat16),
            pltpu.VMEM((QUERIES, HEADS * VALUE_DIM), jnp.bfloat16),
        ],
        compiler_params=params(ATTEND_MIB),
        cost_estimate=pl.CostEstimate(
            flops=2 * 1024 * 2176 * 1280 + 2 * 128 * 1024 * 7168,
            bytes_accessed=22_000_000,
            transcendentals=1024 * 2176,
        ),
        name="decode",
    )(info, own, other, ready, absorb_values, out_weight)


def gather_sum_kernel(parts, out_ref):
    total = parts[0].astype(jnp.float32)
    for place in range(1, parts.shape[0]):
        total = total + parts[place].astype(jnp.float32)
    out_ref[...] = total.T.astype(jnp.bfloat16)


def gather_sum(parts):
    return pl.pallas_call(
        gather_sum_kernel,
        out_shape=jax.ShapeDtypeStruct((QUERIES, SHARE), jnp.bfloat16),
        in_specs=[vmem],
        out_specs=vmem,
        name="gather_sum",
    )(parts)


def on_device(
    pre_queries,
    pre_latent,
    absorb_keys,
    absorb_values,
    step_queries,
    step_latent,
    context_lengths,
    page_table,
    out_weight,
):
    tp = lax.axis_index("tp")
    info = jnp.stack([lax.axis_index("ctx"), tp % 2]).astype(jnp.int32)
    own = lax.all_to_all(pack(pre_latent), BOTH, 0, 0, axis_index_groups=same_core_groups())
    ready = absorb(
        info,
        step_queries.reshape(QUERIES, HEADS * HEAD),
        absorb_keys,
        step_latent.reshape(QUERIES, LATENT + ROPE),
        context_lengths.reshape(ROWS, 1),
        page_table,
    )
    own, ready = lax.optimization_barrier((own, ready))
    other = lax.ppermute(own, BOTH, other_core())
    keep, send = decode(info, own, other, ready, absorb_values, out_weight)
    arrived = lax.ppermute(send, BOTH, other_core())
    chip = (keep.astype(jnp.float32) + arrived.astype(jnp.float32)).astype(jnp.bfloat16)
    chip, own, other = lax.optimization_barrier((chip, own, other))
    parts = lax.all_to_all(chip, BOTH, 0, 0, axis_index_groups=chip_groups())
    prefill_heads = prefill(info, own, other, pre_queries, absorb_keys, absorb_values)
    decode_out = gather_sum(parts).reshape(STEPS, ROWS, SHARE)
    return (prefill_heads, decode_out)


def solution(mesh):
    return jax.shard_map(
        on_device,
        mesh=mesh,
        in_specs=(
            P("ctx", "tp"),
            P(("ctx", "tp"), None),
            P(None, "tp"),
            P(None, "tp"),
            P(None, "ctx", "tp"),
            P(None, "ctx", None),
            P("ctx"),
            P("ctx", None),
            P("tp", None),
        ),
        out_specs=(P("ctx", "tp"), P(None, "ctx", "tp")),
        check_vma=False,
    )
```

time: 87.2 us -> 77 us (0.88)
  Pallas kernels: 44.5 us -> 33.8 us
  waiting for transfers between devices: 17.6 us -> 19.3 us
  other arithmetic: 3 us -> 1.71 us
    pallas_call x1, Pallas kernels: 19.6 us -> 13.7 us  [prefill(): pl.pallas_call(prefill_kernel, out_shape=jax.ShapeDtypeStruct((TOKENS, HE...]
    pallas_call x1, Pallas kernels: 16.2 us -> 13 us  [decode(): pl.pallas_call(decode_kernel, out_shape=(share, share), in_specs=[smem] +...]
    all_to_all x1, waiting for transfers between devices: 12.8 us -> 14.4 us  [on_device(): lax.all_to_all(pack(pre_latent), BOTH, 0, 0, axis_index_groups=same_core_...]
    pallas_call x1, Pallas kernels: 4.78 us -> 3.28 us  [absorb(): pl.pallas_call(absorb_kernel, out_shape=jax.ShapeDtypeStruct((BIAS + 4 *...]
    convert_element_type x1, other arithmetic: 2.36 us -> 1.16 us  [on_device(): (keep.astype(jnp.float32) + arrived.astype(jnp.float32)).astype(jnp.bfloa...]
    unnamed x8 -> x14, local copies, waits for them, and re-layouts: 1.97 us -> 1.94 us
  transfers between devices with their start and end apart: 4 -> 4, of which waited for: 3 -> 4; matrix products, arithmetic and copies ran while one was open for 2% -> 2% of each run, Pallas kernels for 28% -> 22%
where the time goes in v3:
time: 77 us; the launch traced here: 76.6 us
  Pallas kernels  33.8 us (44%)
  waiting for transfers between devices  19.3 us (25%)
  starting transfers between devices  18.4 us (24%)
  local copies, waits for them, and re-layouts  2.63 us (3%)
  other arithmetic  1.71 us (2%)
    all_to_all x1, waiting for transfers between devices, on_device(): lax.all_to_all(pack(pre_latent), BOTH, 0, 0, axis_index_groups=same_core_...  14.4 us
    pallas_call x1, Pallas kernels, prefill(): pl.pallas_call(prefill_kernel, out_shape=jax.ShapeDtypeStruct((TOKENS, HE...  13.7 us
    pallas_call x1, Pallas kernels, decode(): pl.pallas_call(decode_kernel, out_shape=(share, share), in_specs=[smem] +...  13 us
    all_to_all x1, starting transfers between devices, on_device(): lax.all_to_all(pack(pre_latent), BOTH, 0, 0, axis_index_groups=same_core_...  12 us
    all_to_all x1, starting transfers between devices, on_device(): parts = lax.all_to_all(chip, BOTH, 0, 0, axis_index_groups=chip_groups())  3.55 us
    pallas_call x1, Pallas kernels, absorb(): pl.pallas_call(absorb_kernel, out_shape=jax.ShapeDtypeStruct((BIAS + 4 *...  3.28 us
    ppermute x1, waiting for transfers between devices, on_device(): other = lax.ppermute(own, BOTH, other_core())  2.47 us
    ppermute x1, starting transfers between devices, on_device(): other = lax.ppermute(own, BOTH, other_core())  2.24 us
  transfers between devices with their start and end apart: 4, of which 4 were waited for; matrix products, arithmetic and copies ran while one was open for 2% of the time, Pallas kernels for 22%

profile of v3, /device:TPU:1, one launch (start us, length us, event | category | flops | bytes accessed | tf_op | source)
XLA Modules:
  0.0 76.6 jit_solution(5308766081593874410)
XLA Ops:
  0.6 0.0 copy-start.5
  0.6 1.9 %pack.1 = bf16[64,72,128]{2,1,0:T(8,128)(2,1)} custom-call(bf16[16,576]{1,0:T(8,128)(2,1)} %latent_ref.1), custom_call_target="tpu_custom_call" | custom-call | tf_op jit(solution)/shard_map/pack/pallas_call | solution.py:98
  2.5 12.0 %all-to-all-start = ((bf16[64,72,128]{2,1,0:T(8,128)(2,1)}), bf16[64,72,128]{2,1,0:T(8,128)(2,1)S(1)}, u32[]{:S(2)}, u32[]{:S(2)}) async-start(bf16[64,72,128]{2,1,0:T(8,128)(2,1)} %pack.1), calls=%async_computation | async-start | bytes 2359296 | tf_op jit(solution)/shard_map/all_to_all | solution.py:387
  14.5 0.0 copy-done.5
  14.5 0.7 copy.11.length_ref
  15.2 0.6 pad_add_fusion.info
  15.8 0.0 copy-start.1
  15.8 3.3 %absorb.1.ready = bf16[1664,640]{1,0:T(8,128)(2,1)} custom-call(s32[2]{0:T(128)} %pad_add_fusion.info, bf16[128,1536]{1,0:T(8,128)(2,1)} %bitcast.6, bf16[512,1024]{1,0:T(8,128)(2,1)} %key_map.1, bf16[128,576]{1,0:T(8,128)(2,1)} %bitcast.7, s32[32,1]{1,0:T(8,128)} %copy.11.length_ref, s32[32,32]{1,0:T(8,128)} %table_ref.1), custom_call_target="tpu_custom_call" | custom-call | flops 134217728 | bytes 5000000 | tf_op jit(solution)/shard_map/absorb/pallas_call | solution.py:171
  19.1 14.4 %all-to-all-done.own = bf16[64,72,128]{2,1,0:T(8,128)(2,1)S(1)} async-done(((bf16[64,72,128]{2,1,0:T(8,128)(2,1)}), bf16[64,72,128]{2,1,0:T(8,128)(2,1)S(1)}, u32[]{:S(2)}, u32[]{:S(2)}) %all-to-all-start) | async-done | bytes 1179680 | tf_op jit(solution)/shard_map/all_to_all | solution.py:387
  33.4 0.0 copy-start.4
  33.4 2.2 %collective-permute-start = (bf16[64,72,128]{2,1,0:T(8,128)(2,1)S(1)}, bf16[64,72,128]{2,1,0:T(8,128)(2,1)S(1)}, u32[]{:S(2)}, u32[]{:S(2)}) collective-permute-start(bf16[64,72,128]{2,1,0:T(8,128)(2,1)S(1)} %all-to-all-done.own), channel_id=1, source_target_pairs={{0,1},{1,0},{4,5},{5,4},{8,9},{9,8},{12,13},{13,12},{2,3},{3,2},{6... | collective-permute-start | bytes 3538952 | tf_op jit(solution)/shard_map/ppermute | solution.py:397
  35.7 2.5 %collective-permute-done.other = bf16[64,72,128]{2,1,0:T(8,128)(2,1)S(1)} collective-permute-done((bf16[64,72,128]{2,1,0:T(8,128)(2,1)S(1)}, bf16[64,72,128]{2,1,0:T(8,128)(2,1)S(1)}, u32[]{:S(2)}, u32[]{:S(2)}) %collective-permute-start) | collective-permute-done | bytes 1179680 | tf_op jit(solution)/shard_map/ppermute | solution.py:397
  38.1 0.0 copy-done.4
  38.1 0.0 copy-start.6
  38.1 1.0 %copy-done.6 = bf16[64,72,128]{2,1,0:T(8,128)(2,1)} copy-done((bf16[64,72,128]{2,1,0:T(8,128)(2,1)}, bf16[64,72,128]{2,1,0:T(8,128)(2,1)S(1)}, u32[]{:S(2)}) %copy-start.6) | copy-done | bytes 1179672
  39.1 0.0 copy-done.1
  39.1 13.0 %decode.1 = (bf16[8,448,128]{2,1,0:T(8,128)(2,1)S(1)}, bf16[8,448,128]{2,1,0:T(8,128)(2,1)S(1)}) custom-call(s32[2]{0:T(128)S(1)} %copy-done.1, bf16[64,72,128]{2,1,0:T(8,128)(2,1)} %copy-done.4, bf16[64,72,128]{2,1,0:T(8,128)(2,1)} %copy-done.6, bf16[1664,640]{1,0:T(8,128)(2,1)} %absorb.1.ready, bf16[512,1024]{1,0:T(8,128)(2,1)} %value_map.1, ...), custom_call_target="tpu_custom_call" | custom-call | flops 7583301632 | bytes 22000000 | tf_op jit(solution)/shard_map/decode/pallas_call | solution.py:331
  52.1 0.6 collective-permute-start.1
  52.8 2.1 %collective-permute-done.1 = bf16[8,448,128]{2,1,0:T(8,128)(2,1)S(1)} collective-permute-done((bf16[8,448,128]{2,1,0:T(8,128)(2,1)S(1)}, bf16[8,448,128]{2,1,0:T(8,128)(2,1)S(1)}, u32[]{:S(2)}, u32[]{:S(2)}) %collective-permute-start.1) | collective-permute-done | bytes 917536 | tf_op jit(solution)/shard_map/ppermute | solution.py:399
  54.9 0.0 copy-start
  54.9 0.0 copy-start.2
  54.9 1.2 %add_convert_fusion = bf16[8,448,128]{2,1,0:T(8,128)(2,1)} fusion(bf16[8,448,128]{2,1,0:T(8,128)(2,1)S(1)} %collective-permute-done.1, bf16[8,448,128]{2,1,0:T(8,128)(2,1)S(1)} %get-tuple-element.11), kind=kLoop, calls=%fused_computation | loop fusion | flops 1835008 | bytes 2752512 | tf_op jit(solution)/shard_map/convert_element_type | solution.py:400
  56.0 3.6 %all-to-all-start.1 = ((bf16[8,448,128]{2,1,0:T(8,128)(2,1)}), bf16[8,448,128]{2,1,0:T(8,128)(2,1)S(1)}, u32[]{:S(2)}, u32[]{:S(2)}) async-start(bf16[8,448,128]{2,1,0:T(8,128)(2,1)} %add_convert_fusion), calls=%async_computation.1 | async-start | bytes 1835008 | tf_op jit(solution)/shard_map/all_to_all | solution.py:402
  59.6 0.0 copy-done
  59.6 0.0 copy-done.2
  59.6 13.7 %prefill.1 = bf16[256,1024]{1,0:T(8,128)(2,1)} custom-call(s32[2]{0:T(128)S(1)} %copy-done.1, bf16[64,72,128]{2,1,0:T(8,128)(2,1)} %copy-done.4, bf16[64,72,128]{2,1,0:T(8,128)(2,1)} %copy-done.6, bf16[256,1536]{1,0:T(8,128)(2,1)S(1)} %copy-done.2, bf16[512,1024]{1,0:T(8,128)(2,1)S(1)} %copy-done, bf16[512,1024]{1,0:T(8,128)(2,1)} %value_map.1), custom_call_target="tpu_custom_call" | custom-call | flops 8589934592 | bytes 10000000 | tf_op jit(solution)/shard_map/prefill/pallas_call | solution.py:246
  73.3 0.3 all-to-all-done.1.parts
  73.6 0.0 copy-start.3
  73.6 0.9 %copy-done.3 = bf16[8,448,128]{2,1,0:T(8,128)(2,1)} copy-done((bf16[8,448,128]{2,1,0:T(8,128)(2,1)}, bf16[8,448,128]{2,1,0:T(8,128)(2,1)S(1)}, u32[]{:S(2)}) %copy-start.3) | copy-done | bytes 917528
  74.5 2.0 %gather_sum.1 = bf16[128,448]{1,0:T(8,128)(2,1)} custom-call(bf16[8,448,128]{2,1,0:T(8,128)(2,1)} %copy-done.3), custom_call_target="tpu_custom_call" | custom-call | tf_op jit(solution)/shard_map/gather_sum/pallas_call | solution.py:365
Async XLA Ops:
  0.6 13.9 %copy-start.5 = (s32[32]{0:T(128)S(1)}, s32[32]{0:T(128)}, u32[]{:S(2)}) copy-start(s32[32]{0:T(128)} %param.15) | copy-start | bytes 388
  2.5 30.9 %all-to-all-start = ((bf16[64,72,128]{2,1,0:T(8,128)(2,1)}), bf16[64,72,128]{2,1,0:T(8,128)(2,1)S(1)}, u32[]{:S(2)}, u32[]{:S(2)}) async-start(bf16[64,72,128]{2,1,0:T(8,128)(2,1)} %pack.1), calls=%async_computation | async-start | bytes 2359296 | tf_op jit(solution)/shard_map/all_to_all | solution.py:387
  15.8 23.4 %copy-start.1 = (s32[2]{0:T(128)S(1)}, s32[2]{0:T(128)}, u32[]{:S(2)}) copy-start(s32[2]{0:T(128)} %pad_add_fusion.info) | copy-start | bytes 28
  33.4 4.7 %copy-start.4 = (bf16[64,72,128]{2,1,0:T(8,128)(2,1)}, bf16[64,72,128]{2,1,0:T(8,128)(2,1)S(1)}, u32[]{:S(2)}) copy-start(bf16[64,72,128]{2,1,0:T(8,128)(2,1)S(1)} %all-to-all-done.own) | copy-start | bytes 3538948
  33.4 4.7 %collective-permute-start = (bf16[64,72,128]{2,1,0:T(8,128)(2,1)S(1)}, bf16[64,72,128]{2,1,0:T(8,128)(2,1)S(1)}, u32[]{:S(2)}, u32[]{:S(2)}) collective-permute-start(bf16[64,72,128]{2,1,0:T(8,128)(2,1)S(1)} %all-to-all-done.own), channel_id=1, source_target_pairs={{0,1},{1,0},{4,5},{5,4},{8,9},{9,8},{12,13},{13,12},{2,3},{3,2},{6... | collective-permute-start | bytes 3538952 | tf_op jit(solution)/shard_map/ppermute | solution.py:397
  38.1 1.0 %copy-start.6 = (bf16[64,72,128]{2,1,0:T(8,128)(2,1)}, bf16[64,72,128]{2,1,0:T(8,128)(2,1)S(1)}, u32[]{:S(2)}) copy-start(bf16[64,72,128]{2,1,0:T(8,128)(2,1)S(1)} %collective-permute-done.other) | copy-start | bytes 3538948
  52.1 2.7 %collective-permute-start.1 = (bf16[8,448,128]{2,1,0:T(8,128)(2,1)S(1)}, bf16[8,448,128]{2,1,0:T(8,128)(2,1)S(1)}, u32[]{:S(2)}, u32[]{:S(2)}) collective-permute-start(bf16[8,448,128]{2,1,0:T(8,128)(2,1)S(1)} %get-tuple-element.12), channel_id=1, source_target_pairs={{0,1},{1,0},{4,5},{5,4},{8,9},{9,8},{12,13},{13,12},{2,3},{3,2},{6... | collective-permute-start | bytes 2752520 | tf_op jit(solution)/shard_map/ppermute | solution.py:399
  54.9 4.7 %copy-start = (bf16[512,1024]{1,0:T(8,128)(2,1)S(1)}, bf16[512,1024]{1,0:T(8,128)(2,1)}, u32[]{:S(2)}) copy-start(bf16[512,1024]{1,0:T(8,128)(2,1)} %key_map.1) | copy-start | bytes 3145732
  54.9 4.7 %copy-start.2 = (bf16[256,1536]{1,0:T(8,128)(2,1)S(1)}, bf16[256,1536]{1,0:T(8,128)(2,1)}, u32[]{:S(2)}) copy-start(bf16[256,1536]{1,0:T(8,128)(2,1)} %query_ref.1) | copy-start | bytes 2359300
  56.0 17.6 %all-to-all-start.1 = ((bf16[8,448,128]{2,1,0:T(8,128)(2,1)}), bf16[8,448,128]{2,1,0:T(8,128)(2,1)S(1)}, u32[]{:S(2)}, u32[]{:S(2)}) async-start(bf16[8,448,128]{2,1,0:T(8,128)(2,1)} %add_convert_fusion), calls=%async_computation.1 | async-start | bytes 1835008 | tf_op jit(solution)/shard_map/all_to_all | solution.py:402
  73.6 0.9 %copy-start.3 = (bf16[8,448,128]{2,1,0:T(8,128)(2,1)}, bf16[8,448,128]{2,1,0:T(8,128)(2,1)S(1)}, u32[]{:S(2)}) copy-start(bf16[8,448,128]{2,1,0:T(8,128)(2,1)S(1)} %all-to-all-done.1.parts) | copy-start | bytes 2752516

commit v4 on v3

--- a/solution.py
+++ b/solution.py
@@ -36,7 +36,8 @@
 CUT = 1024
 SOFT = 16
 DECODE_CUT = 256
-ATTEND_MIB = 52
+PREFILL_MIB = 48
+DECODE_MIB = 48
 to_exp2 = math.log2(math.e) / math.sqrt(HEAD)
 vmem = pl.BlockSpec(memory_space=pltpu.VMEM)
 smem = pl.BlockSpec(memory_space=pltpu.SMEM)
@@ -100,6 +101,7 @@
         out_shape=jax.ShapeDtypeStruct((64, PIECE, 128), jnp.bfloat16),
         in_specs=[vmem],
         out_specs=vmem,
+        compiler_params=params(16),
         name="pack",
     )(latent)
 
@@ -127,8 +129,23 @@
     return ((row % 128) // 16) * 32 + owner * 16 + row % 16
 
 
-def absorb_kernel(info, query_ref, key_ref, latent_ref, length_ref, table_ref, out):
+def place_of_head(head):
+    row = 2 * LATENT + head // 4 * TOKENS
+    return slice(row, row + TOKENS), slice(head % 4 * DIRECT, (head % 4 + 1) * DIRECT)
+
+
+def absorb_kernel(
+    info, query_ref, key_ref, latent_ref, length_ref, table_ref, pre_ref, value_ref, out, pre_out
+):
     core = info[1]
+    pre_out[:LATENT, :] = key_ref[...]
+    pre_out[LATENT : 2 * LATENT, :] = value_ref[...]
+    for head in range(HEADS):
+        query = pre_ref[:, head // 2 * 2 * HEAD : (head // 2 + 1) * 2 * HEAD]
+        query = query[:, head % 2 * HEAD : (head % 2 + 1) * HEAD]
+        rope = query[:, NOPE:]
+        rows, columns = place_of_head(head)
+        pre_out[rows, columns] = jnp.concatenate([query[:, :NOPE], rope, rope], axis=1)
     for pair in range(HEADS // 2):
         both = query_ref[:, pair * 2 * HEAD : (pair + 1) * 2 * HEAD]
         for part in range(2):
@@ -167,18 +184,21 @@
         out[row : row + QUERIES, : part.shape[1]] = part
 
 
-def absorb(info, queries, absorb_keys, step_latent, lengths, table):
+def absorb(info, queries, absorb_keys, step_latent, lengths, table, pre_queries, absorb_values):
     return pl.pallas_call(
         absorb_kernel,
-        out_shape=jax.ShapeDtypeStruct((BIAS + 4 * QUERIES, WIDTH), jnp.bfloat16),
-        in_specs=[smem] + [vmem] * 5,
-        out_specs=vmem,
+        out_shape=(
+            jax.ShapeDtypeStruct((BIAS + 4 * QUERIES, WIDTH), jnp.bfloat16),
+            jax.ShapeDtypeStruct((2 * LATENT + 2 * TOKENS, HEADS * NOPE), jnp.bfloat16),
+        ),
+        in_specs=[smem] + [vmem] * 7,
+        out_specs=(vmem, vmem),
         compiler_params=params(56),
         cost_estimate=pl.CostEstimate(
             flops=2 * 1024 * 128 * 512, bytes_accessed=5_000_000, transcendentals=0
         ),
         name="absorb",
-    )(info, queries, absorb_keys, step_latent, lengths, table)
+    )(info, queries, absorb_keys, step_latent, lengths, table, pre_queries, absorb_values)
 
 
 def softmax_rows(scores, bias, weights, start, count):
@@ -190,18 +210,10 @@
     return 1.0 / jnp.sum(expo, axis=1, keepdims=True)
 
 
-def prefill_kernel(
-    info, own, other, query_ref, key_map, value_map, out_ref, queries, latent, bias, *held
-):
+def prefill_kernel(info, own, other, ready, out_ref, latent, bias, *held):
     ctx, core = info[0], info[1]
     keys, values, scores, weights = held[:2], held[2:6], held[6:8], held[8:]
     unpack(own, other, latent, keys)
-    for pair in range(HEADS // 2):
-        both = query_ref[:, pair * 2 * HEAD : (pair + 1) * 2 * HEAD]
-        for part in range(2):
-            query = both[:, part * HEAD : (part + 1) * HEAD]
-            rope = query[:, NOPE:]
-            queries[pair * 2 + part] = jnp.concatenate([query[:, :NOPE], rope, rope], axis=1)
     key = lax.broadcasted_iota(jnp.int32, (TOKENS, POOL), 1)
     token = (key // BLOCK) * BLOCK + token_of_key((TOKENS, POOL), 1, core)
     query = ctx * TOKENS + lax.broadcasted_iota(jnp.int32, (TOKENS, POOL), 0)
@@ -210,13 +222,15 @@
 
     def make(head, at):
         columns = slice(head * NOPE, (head + 1) * NOPE)
-        maps = jnp.concatenate([key_map[:, columns], value_map[:, columns]], axis=1)
+        maps = [ready[:LATENT, columns], ready[LATENT : 2 * LATENT, columns]]
+        maps = jnp.concatenate(maps, axis=1)
         made = dot(latent[at : at + CUT, :], maps).astype(jnp.bfloat16)
         keys[head % 2][at : at + CUT, :NOPE] = made[:, :NOPE]
         values[head % 4][at : at + CUT, :] = made[:, NOPE:]
 
     def score(head, at):
-        scores[head % 2][:, at : at + CUT] = dot_t(queries[head], keys[head % 2][at : at + CUT, :])
+        query = ready[place_of_head(head)]
+        scores[head % 2][:, at : at + CUT] = dot_t(query, keys[head % 2][at : at + CUT, :])
 
     def soften(head, start):
         part = softmax_rows(scores[head % 2], bias, weights[head % 2], start, SOFT)
@@ -242,14 +256,13 @@
                 soften(stage - 2, turn * SOFT)
 
 
-def prefill(info, own, other, queries, absorb_keys, absorb_values):
+def prefill(info, own, other, ready):
     return pl.pallas_call(
         prefill_kernel,
         out_shape=jax.ShapeDtypeStruct((TOKENS, HEADS * VALUE_DIM), jnp.bfloat16),
-        in_specs=[smem] + [vmem] * 5,
+        in_specs=[smem] + [vmem] * 3,
         out_specs=vmem,
         scratch_shapes=[
-            pltpu.VMEM((HEADS, TOKENS, DIRECT), jnp.bfloat16),
             pltpu.VMEM((POOL, LATENT), jnp.bfloat16),
             pltpu.VMEM((TOKENS, POOL), jnp.float32),
             *[pltpu.VMEM((POOL, DIRECT), jnp.bfloat16)] * 2,
@@ -257,12 +270,12 @@
             *[pltpu.VMEM((TOKENS, POOL), jnp.float32)] * 2,
             *[pltpu.VMEM((TOKENS, POOL), jnp.bfloat16)] * 2,
         ],
-        compiler_params=params(ATTEND_MIB),
+        compiler_params=params(PREFILL_MIB),
         cost_estimate=pl.CostEstimate(
             flops=2 * 2048 * 2048 * 1024, bytes_accessed=10_000_000, transcendentals=2048 * 2048
         ),
         name="prefill",
-    )(info, own, other, queries, absorb_keys, absorb_values)
+    )(info, own, other, ready)
 
 
 def decode_kernel(
@@ -344,7 +357,7 @@
             pltpu.VMEM((2 * QUERIES, KEYS), jnp.bfloat16),
             pltpu.VMEM((QUERIES, HEADS * VALUE_DIM), jnp.bfloat16),
         ],
-        compiler_params=params(ATTEND_MIB),
+        compiler_params=params(DECODE_MIB),
         cost_estimate=pl.CostEstimate(
             flops=2 * 1024 * 2176 * 1280 + 2 * 128 * 1024 * 7168,
             bytes_accessed=22_000_000,
@@ -367,6 +380,7 @@
         out_shape=jax.ShapeDtypeStruct((QUERIES, SHARE), jnp.bfloat16),
         in_specs=[vmem],
         out_specs=vmem,
+        compiler_params=params(16),
         name="gather_sum",
     )(parts)
 
@@ -385,22 +399,24 @@
     tp = lax.axis_index("tp")
     info = jnp.stack([lax.axis_index("ctx"), tp % 2]).astype(jnp.int32)
     own = lax.all_to_all(pack(pre_latent), BOTH, 0, 0, axis_index_groups=same_core_groups())
-    ready = absorb(
+    ready, pre_ready = absorb(
         info,
         step_queries.reshape(QUERIES, HEADS * HEAD),
         absorb_keys,
         step_latent.reshape(QUERIES, LATENT + ROPE),
         context_lengths.reshape(ROWS, 1),
         page_table,
+        pre_queries,
+        absorb_values,
     )
-    own, ready = lax.optimization_barrier((own, ready))
+    own, ready, pre_ready = lax.optimization_barrier((own, ready, pre_ready))
     other = lax.ppermute(own, BOTH, other_core())
     keep, send = decode(info, own, other, ready, absorb_values, out_weight)
     arrived = lax.ppermute(send, BOTH, other_core())
     chip = (keep.astype(jnp.float32) + arrived.astype(jnp.float32)).astype(jnp.bfloat16)
     chip, own, other = lax.optimization_barrier((chip, own, other))
     parts = lax.all_to_all(chip, BOTH, 0, 0, axis_index_groups=chip_groups())
-    prefill_heads = prefill(info, own, other, pre_queries, absorb_keys, absorb_values)
+    prefill_heads = prefill(info, own, other, pre_ready)
     decode_out = gather_sum(parts).reshape(STEPS, ROWS, SHARE)
     return (prefill_heads, decode_out)
 

time: 77 us -> 74.6 us (0.969)
  waiting for transfers between devices: 19.3 us -> 17.1 us
  Pallas kernels: 33.8 us -> 31.6 us
  local copies, waits for them, and re-layouts: 2.63 us -> 4.58 us
    unnamed x14, local copies, waits for them, and re-layouts: 1.94 us -> 3.89 us
    all_to_all x1, waiting for transfers between devices: 14.4 us -> 12.5 us  [on_device(): lax.all_to_all(pack(pre_latent), BOTH, 0, 0, axis_index_groups=same_core_...]
    pallas_call x1, Pallas kernels: 3.28 us -> 5.09 us  [absorb(): pl.pallas_call(absorb_kernel, out_shape=(jax.ShapeDtypeStruct((BIAS + 4 *...]
    pallas_call x1, Pallas kernels: 13.7 us -> 12 us  [prefill(): pl.pallas_call(prefill_kernel, out_shape=jax.ShapeDtypeStruct((TOKENS, HE...]
    pallas_call x1, Pallas kernels: 2.02 us -> 0.84 us  [gather_sum(): pl.pallas_call(gather_sum_kernel, out_shape=jax.ShapeDtypeStruct((QUERIES...]
  transfers between devices with their start and end apart: 4 -> 4, of which waited for: 4 -> 3; matrix products, arithmetic and copies ran while one was open for 2% -> 2% of each run, Pallas kernels for 22% -> 23%
where the time goes in v4:
time: 74.6 us; the launch traced here: 74.1 us
  Pallas kernels  31.6 us (42%)
  starting transfers between devices  18.4 us (25%)
  waiting for transfers between devices  17.1 us (23%)
  local copies, waits for them, and re-layouts  4.58 us (6%)
  other arithmetic  1.8 us (2%)
    all_to_all x1, waiting for transfers between devices, on_device(): lax.all_to_all(pack(pre_latent), BOTH, 0, 0, axis_index_groups=same_core_...  12.5 us
    pallas_call x1, Pallas kernels, decode(): pl.pallas_call(decode_kernel, out_shape=(share, share), in_specs=[smem] +...  12.4 us
    pallas_call x1, Pallas kernels, prefill(): pl.pallas_call(prefill_kernel, out_shape=jax.ShapeDtypeStruct((TOKENS, HE...  12 us
    all_to_all x1, starting transfers between devices, on_device(): lax.all_to_all(pack(pre_latent), BOTH, 0, 0, axis_index_groups=same_core_...  12 us
    pallas_call x1, Pallas kernels, absorb(): pl.pallas_call(absorb_kernel, out_shape=(jax.ShapeDtypeStruct((BIAS + 4 *...  5.09 us
    unnamed x14, local copies, waits for them, and re-layouts  3.89 us
    all_to_all x1, starting transfers between devices, on_device(): parts = lax.all_to_all(chip, BOTH, 0, 0, axis_index_groups=chip_groups())  3.55 us
    ppermute x1, waiting for transfers between devices, on_device(): other = lax.ppermute(own, BOTH, other_core())  2.47 us
  transfers between devices with their start and end apart: 4, of which 3 were waited for; matrix products, arithmetic and copies ran while one was open for 2% of the time, Pallas kernels for 23%

profile of v4, /device:TPU:1, one launch (start us, length us, event | category | flops | bytes accessed | tf_op | source)
XLA Modules:
  0.0 74.1 jit_solution(7873585733034638103)
XLA Ops:
  0.6 0.0 copy-start.1
  0.6 0.7 copy-done.1
  1.4 0.0 copy-start.6
  1.4 1.2 %pack.1 = bf16[64,72,128]{2,1,0:T(8,128)(2,1)} custom-call(bf16[16,576]{1,0:T(8,128)(2,1)S(1)} %copy-done.1), custom_call_target="tpu_custom_call" | custom-call | tf_op jit(solution)/shard_map/pack/pallas_call | solution.py:99
  2.6 12.0 %all-to-all-start = ((bf16[64,72,128]{2,1,0:T(8,128)(2,1)}), bf16[64,72,128]{2,1,0:T(8,128)(2,1)S(1)}, u32[]{:S(2)}, u32[]{:S(2)}) async-start(bf16[64,72,128]{2,1,0:T(8,128)(2,1)} %pack.1), calls=%async_computation | async-start | bytes 2359296 | tf_op jit(solution)/shard_map/all_to_all | solution.py:401
  14.5 0.0 copy-start
  14.5 0.0 copy-done.6
  14.6 0.7 copy.11.length_ref
  15.2 0.6 pad_add_fusion.info
  15.9 0.0 copy-start.2
  15.9 5.1 %absorb.1 = (bf16[1664,640]{1,0:T(8,128)(2,1)}, bf16[1536,1024]{1,0:T(8,128)(2,1)}) custom-call(s32[2]{0:T(128)} %pad_add_fusion.info, bf16[128,1536]{1,0:T(8,128)(2,1)} %bitcast.6, bf16[512,1024]{1,0:T(8,128)(2,1)} %key_ref.1, bf16[128,576]{1,0:T(8,128)(2,1)} %bitcast.7, s32[32,1]{1,0:T(8,128)} %copy.11.length_ref, s32[32,32]{1,0:T(8,128)} %table_ref.1, ...), custom_call_target="tpu_custom_call" | custom-call | flops 134217728 | bytes 5000000 | tf_op jit(solution)/shard_map/absorb/pallas_call | solution.py:188
  20.9 12.5 %all-to-all-done.own = bf16[64,72,128]{2,1,0:T(8,128)(2,1)S(1)} async-done(((bf16[64,72,128]{2,1,0:T(8,128)(2,1)}), bf16[64,72,128]{2,1,0:T(8,128)(2,1)S(1)}, u32[]{:S(2)}, u32[]{:S(2)}) %all-to-all-start) | async-done | bytes 1179680 | tf_op jit(solution)/shard_map/all_to_all | solution.py:401
  33.4 2.2 %collective-permute-start = (bf16[64,72,128]{2,1,0:T(8,128)(2,1)S(1)}, bf16[64,72,128]{2,1,0:T(8,128)(2,1)S(1)}, u32[]{:S(2)}, u32[]{:S(2)}) collective-permute-start(bf16[64,72,128]{2,1,0:T(8,128)(2,1)S(1)} %all-to-all-done.own), channel_id=1, source_target_pairs={{0,1},{1,0},{4,5},{5,4},{8,9},{9,8},{12,13},{13,12},{2,3},{3,2},{6... | collective-permute-start | bytes 3538952 | tf_op jit(solution)/shard_map/ppermute | solution.py:413
  35.7 2.5 %collective-permute-done.other = bf16[64,72,128]{2,1,0:T(8,128)(2,1)S(1)} collective-permute-done((bf16[64,72,128]{2,1,0:T(8,128)(2,1)S(1)}, bf16[64,72,128]{2,1,0:T(8,128)(2,1)S(1)}, u32[]{:S(2)}, u32[]{:S(2)}) %collective-permute-start) | collective-permute-done | bytes 1179680 | tf_op jit(solution)/shard_map/ppermute | solution.py:413
  38.2 0.0 copy-done
  38.2 0.0 copy-done.2
  38.2 0.0 copy-start.4
  38.2 12.4 %decode.1 = (bf16[8,448,128]{2,1,0:T(8,128)(2,1)S(1)}, bf16[8,448,128]{2,1,0:T(8,128)(2,1)S(1)}) custom-call(s32[2]{0:T(128)S(1)} %copy-done.2, bf16[64,72,128]{2,1,0:T(8,128)(2,1)S(1)} %all-to-all-done.own, bf16[64,72,128]{2,1,0:T(8,128)(2,1)S(1)} %collective-permute-done.other, bf16[1664,640]{1,0:T(8,128)(2,1)} %get-tuple-element.15.ready, ...), custom_call_target="tpu_custom_call" | custom-call | flops 7583301632 | bytes 22000000 | tf_op jit(solution)/shard_map/decode/pallas_call | solution.py:344
  50.6 0.0 copy-done.4
  50.6 0.6 collective-permute-start.1
  51.2 2.1 %collective-permute-done.1 = bf16[8,448,128]{2,1,0:T(8,128)(2,1)S(1)} collective-permute-done((bf16[8,448,128]{2,1,0:T(8,128)(2,1)S(1)}, bf16[8,448,128]{2,1,0:T(8,128)(2,1)S(1)}, u32[]{:S(2)}, u32[]{:S(2)}) %collective-permute-start.1) | collective-permute-done | bytes 917536 | tf_op jit(solution)/shard_map/ppermute | solution.py:415
  53.3 1.2 %add_convert_fusion = bf16[8,448,128]{2,1,0:T(8,128)(2,1)} fusion(bf16[8,448,128]{2,1,0:T(8,128)(2,1)S(1)} %collective-permute-done.1, bf16[8,448,128]{2,1,0:T(8,128)(2,1)S(1)} %get-tuple-element.16), kind=kLoop, calls=%fused_computation | loop fusion | flops 1835008 | bytes 2752512 | tf_op jit(solution)/shard_map/convert_element_type | solution.py:416
  54.5 3.6 %all-to-all-start.1 = ((bf16[8,448,128]{2,1,0:T(8,128)(2,1)}), bf16[8,448,128]{2,1,0:T(8,128)(2,1)S(1)}, u32[]{:S(2)}, u32[]{:S(2)}) async-start(bf16[8,448,128]{2,1,0:T(8,128)(2,1)} %add_convert_fusion), calls=%async_computation.1 | async-start | bytes 1835008 | tf_op jit(solution)/shard_map/all_to_all | solution.py:418
  58.1 0.0 copy-start.3
  58.1 1.9 %copy-done.3 = bf16[1536,1024]{1,0:T(8,128)(2,1)S(1)} copy-done((bf16[1536,1024]{1,0:T(8,128)(2,1)S(1)}, bf16[1536,1024]{1,0:T(8,128)(2,1)}, u32[]{:S(2)}) %copy-start.3) | copy-done | bytes 3145752
  60.0 0.0 copy-start.5
  60.0 1.3 %copy-done.5 = bf16[64,72,128]{2,1,0:T(8,128)(2,1)S(1)} copy-done((bf16[64,72,128]{2,1,0:T(8,128)(2,1)S(1)}, bf16[64,72,128]{2,1,0:T(8,128)(2,1)}, u32[]{:S(2)}) %copy-start.5) | copy-done | bytes 1179672
  61.3 12.0 %prefill.1 = bf16[256,1024]{1,0:T(8,128)(2,1)} custom-call(s32[2]{0:T(128)S(1)} %copy-done.2, bf16[64,72,128]{2,1,0:T(8,128)(2,1)S(1)} %all-to-all-done.own, bf16[64,72,128]{2,1,0:T(8,128)(2,1)S(1)} %copy-done.5, bf16[1536,1024]{1,0:T(8,128)(2,1)S(1)} %copy-done.3), custom_call_target="tpu_custom_call" | custom-call | flops 8589934592 | bytes 10000000 | tf_op jit(solution)/shard_map/prefill/pallas_call | solution.py:260
  73.3 0.0 all-to-all-done.1.parts
  73.3 0.8 %gather_sum.1 = bf16[128,448]{1,0:T(8,128)(2,1)} custom-call(bf16[8,448,128]{2,1,0:T(8,128)(2,1)S(1)} %all-to-all-done.1.parts), custom_call_target="tpu_custom_call" | custom-call | tf_op jit(solution)/shard_map/gather_sum/pallas_call | solution.py:378
Async XLA Ops:
  0.6 0.7 copy-start.1
  1.4 13.2 %copy-start.6 = (s32[32]{0:T(128)S(1)}, s32[32]{0:T(128)}, u32[]{:S(2)}) copy-start(s32[32]{0:T(128)} %param.15) | copy-start | bytes 388
  2.6 30.9 %all-to-all-start = ((bf16[64,72,128]{2,1,0:T(8,128)(2,1)}), bf16[64,72,128]{2,1,0:T(8,128)(2,1)S(1)}, u32[]{:S(2)}, u32[]{:S(2)}) async-start(bf16[64,72,128]{2,1,0:T(8,128)(2,1)} %pack.1), calls=%async_computation | async-start | bytes 2359296 | tf_op jit(solution)/shard_map/all_to_all | solution.py:401
  14.5 23.6 %copy-start = (bf16[512,1024]{1,0:T(8,128)(2,1)S(1)}, bf16[512,1024]{1,0:T(8,128)(2,1)}, u32[]{:S(2)}) copy-start(bf16[512,1024]{1,0:T(8,128)(2,1)} %value_ref.3) | copy-start | bytes 3145732
  15.9 22.3 %copy-start.2 = (s32[2]{0:T(128)S(1)}, s32[2]{0:T(128)}, u32[]{:S(2)}) copy-start(s32[2]{0:T(128)} %pad_add_fusion.info) | copy-start | bytes 28
  33.4 4.7 %collective-permute-start = (bf16[64,72,128]{2,1,0:T(8,128)(2,1)S(1)}, bf16[64,72,128]{2,1,0:T(8,128)(2,1)S(1)}, u32[]{:S(2)}, u32[]{:S(2)}) collective-permute-start(bf16[64,72,128]{2,1,0:T(8,128)(2,1)S(1)} %all-to-all-done.own), channel_id=1, source_target_pairs={{0,1},{1,0},{4,5},{5,4},{8,9},{9,8},{12,13},{13,12},{2,3},{3,2},{6... | collective-permute-start | bytes 3538952 | tf_op jit(solution)/shard_map/ppermute | solution.py:413
  38.2 12.4 %copy-start.4 = (bf16[64,72,128]{2,1,0:T(8,128)(2,1)}, bf16[64,72,128]{2,1,0:T(8,128)(2,1)S(1)}, u32[]{:S(2)}) copy-start(bf16[64,72,128]{2,1,0:T(8,128)(2,1)S(1)} %collective-permute-done.other) | copy-start | bytes 3538948
  50.6 2.7 %collective-permute-start.1 = (bf16[8,448,128]{2,1,0:T(8,128)(2,1)S(1)}, bf16[8,448,128]{2,1,0:T(8,128)(2,1)S(1)}, u32[]{:S(2)}, u32[]{:S(2)}) collective-permute-start(bf16[8,448,128]{2,1,0:T(8,128)(2,1)S(1)} %get-tuple-element.17), channel_id=1, source_target_pairs={{0,1},{1,0},{4,5},{5,4},{8,9},{9,8},{12,13},{13,12},{2,3},{3,2},{6... | collective-permute-start | bytes 2752520 | tf_op jit(solution)/shard_map/ppermute | solution.py:415
  54.5 18.8 %all-to-all-start.1 = ((bf16[8,448,128]{2,1,0:T(8,128)(2,1)}), bf16[8,448,128]{2,1,0:T(8,128)(2,1)S(1)}, u32[]{:S(2)}, u32[]{:S(2)}) async-start(bf16[8,448,128]{2,1,0:T(8,128)(2,1)} %add_convert_fusion), calls=%async_computation.1 | async-start | bytes 1835008 | tf_op jit(solution)/shard_map/all_to_all | solution.py:418
  58.1 1.9 %copy-start.3 = (bf16[1536,1024]{1,0:T(8,128)(2,1)S(1)}, bf16[1536,1024]{1,0:T(8,128)(2,1)}, u32[]{:S(2)}) copy-start(bf16[1536,1024]{1,0:T(8,128)(2,1)} %get-tuple-element.20.ready) | copy-start | bytes 9437188
  60.0 1.3 %copy-start.5 = (bf16[64,72,128]{2,1,0:T(8,128)(2,1)S(1)}, bf16[64,72,128]{2,1,0:T(8,128)(2,1)}, u32[]{:S(2)}) copy-start(bf16[64,72,128]{2,1,0:T(8,128)(2,1)} %copy-done.4) | copy-start | bytes 3538948

commit v5 on v4

--- a/solution.py
+++ b/solution.py
@@ -18,7 +18,7 @@
 WIDTH = LATENT + 2 * ROPE
 DIRECT = NOPE + 2 * ROPE
 PIECE = 72
-BLOCK = 256
+HALF = 1024
 HEAD = NOPE + ROPE
 HEADS = 8
 TOKENS = 256
@@ -37,7 +37,9 @@
 SOFT = 16
 DECODE_CUT = 256
 PREFILL_MIB = 48
-DECODE_MIB = 48
+DECODE_MIB = 34
+EARLY_MIB = 43
+EARLY = 256
 to_exp2 = math.log2(math.e) / math.sqrt(HEAD)
 vmem = pl.BlockSpec(memory_space=pltpu.VMEM)
 smem = pl.BlockSpec(memory_space=pltpu.SMEM)
@@ -106,27 +108,27 @@
     )(latent)
 
 
-def unpack(own, other, latent, ropes):
-    for block in range(POOL // BLOCK):
-        for half, source in enumerate((own, other)):
-            rows = slice(block * BLOCK + half * 128, block * BLOCK + half * 128 + 128)
-            pieces = slice(block * 8, block * 8 + 8)
-            for tile in range(4):
-                latent[rows, tile * 128 : (tile + 1) * 128] = source[
-                    pieces, tile * 16 : (tile + 1) * 16, :
-                ].reshape(128, 128)
-            rope = source[pieces, 64:72, :].astype(jnp.float32)
-            left = lax.broadcasted_iota(jnp.int32, rope.shape, 2) < ROPE
-            both = jnp.concatenate([jnp.where(left, rope, 0.0), jnp.where(left, 0.0, rope)], axis=1)
-            both = both.reshape(128, 128).astype(jnp.bfloat16)
-            for ref in ropes:
-                ref[rows, ref.shape[1] - 2 * ROPE :] = both
+def unpack(source, latent, ropes, at):
+    for piece in range(0, 64, 8):
+        rows = slice(at + piece * 16, at + piece * 16 + 128)
+        pieces = slice(piece, piece + 8)
+        for tile in range(4):
+            latent[rows, tile * 128 : (tile + 1) * 128] = source[
+                pieces, tile * 16 : (tile + 1) * 16, :
+            ].reshape(128, 128)
+        rope = source[pieces, 64:72, :].astype(jnp.float32)
+        left = lax.broadcasted_iota(jnp.int32, rope.shape, 2) < ROPE
+        both = jnp.concatenate([jnp.where(left, rope, 0.0), jnp.where(left, 0.0, rope)], axis=1)
+        both = both.reshape(128, 128).astype(jnp.bfloat16)
+        for ref in ropes:
+            ref[rows, ref.shape[1] - 2 * ROPE :] = both
 
 
 def token_of_key(shape, dim, core):
-    row = lax.broadcasted_iota(jnp.int32, shape, dim)
-    owner = jnp.where((row // 128) % 2 == 0, core, 1 - core)
-    return ((row % 128) // 16) * 32 + owner * 16 + row % 16
+    key = lax.broadcasted_iota(jnp.int32, shape, dim)
+    row = key % HALF
+    owner = jnp.where(key < HALF, core, 1 - core)
+    return (row // 16) * 32 + owner * 16 + row % 16
 
 
 def place_of_head(head):
@@ -168,7 +170,7 @@
     limit = jnp.clip(length_ref[...] - slot * PAGE, 0, PAGE).astype(jnp.float32)
     shape = (pages, POOL)
     key = lax.broadcasted_iota(jnp.int32, shape, 1)
-    of = (key // BLOCK) * (BLOCK // PAGE) + (key % 128) // (PAGE // 2)
+    of = (key % HALF) // (PAGE // 2)
     owner = (lax.broadcasted_iota(jnp.int32, shape, 0) == of).astype(jnp.bfloat16)
     spread = dot(limit.astype(jnp.bfloat16), owner)
     token = (token_of_key((ROWS, POOL), 1, core) % PAGE).astype(jnp.float32)
@@ -203,19 +205,32 @@
 
 def softmax_rows(scores, bias, weights, start, count):
     bias_start = start % bias.shape[0]
-    shifted = scores[start : start + count, :] + bias[bias_start : bias_start + count, :]
-    largest = jnp.max(shifted, axis=1, keepdims=True)
-    expo = jnp.exp2(shifted * to_exp2 - largest * to_exp2)
-    weights[start : start + count, :] = expo.astype(jnp.bfloat16)
-    return 1.0 / jnp.sum(expo, axis=1, keepdims=True)
+    shifted = []
+    at = 0
+    for part in scores:
+        size = part.shape[1]
+        mask = bias[bias_start : bias_start + count, at : at + size]
+        shifted.append(part[start : start + count, :] + mask)
+        at += size
+    largest = functools.reduce(
+        jnp.maximum, [jnp.max(part, axis=1, keepdims=True) for part in shifted]
+    )
+    total = 0.0
+    at = 0
+    for part in shifted:
+        expo = jnp.exp2(part * to_exp2 - largest * to_exp2)
+        weights[start : start + count, at : at + part.shape[1]] = expo.astype(jnp.bfloat16)
+        total = total + jnp.sum(expo, axis=1, keepdims=True)
+        at += part.shape[1]
+    return 1.0 / total
 
 
 def prefill_kernel(info, own, other, ready, out_ref, latent, bias, *held):
     ctx, core = info[0], info[1]
     keys, values, scores, weights = held[:2], held[2:6], held[6:8], held[8:]
-    unpack(own, other, latent, keys)
-    key = lax.broadcasted_iota(jnp.int32, (TOKENS, POOL), 1)
-    token = (key // BLOCK) * BLOCK + token_of_key((TOKENS, POOL), 1, core)
+    unpack(own, latent, keys, 0)
+    unpack(other, latent, keys, HALF)
+    token = token_of_key((TOKENS, POOL), 1, core)
     query = ctx * TOKENS + lax.broadcasted_iota(jnp.int32, (TOKENS, POOL), 0)
     bias[...] = jnp.where(token <= query, 0.0, hidden)
     inverse = {}
@@ -233,7 +248,7 @@
         scores[head % 2][:, at : at + CUT] = dot_t(query, keys[head % 2][at : at + CUT, :])
 
     def soften(head, start):
-        part = softmax_rows(scores[head % 2], bias, weights[head % 2], start, SOFT)
+        part = softmax_rows([scores[head % 2]], bias, weights[head % 2], start, SOFT)
         inverse.setdefault(head, []).append(part)
 
     def mix(head):
@@ -278,14 +293,54 @@
     )(info, own, other, ready)
 
 
+def early_kernel(own, ready_hbm, weight_hbm, scores, ready, weight, keys, sems):
+    loads = [
+        pltpu.make_async_copy(ready_hbm, ready, sems.at[0]),
+        pltpu.make_async_copy(weight_hbm.at[:EARLY, :], weight, sems.at[1]),
+    ]
+    for load in loads:
+        load.start()
+    unpack(own, keys, [keys], 0)
+    loads[0].wait()
+    rows = 2 * QUERIES
+    for item in range(HEADS // 2):
+        for at in range(0, HALF, DECODE_CUT):
+            queries = ready[item * rows : (item + 1) * rows, :]
+            scores[item, :, at : at + DECODE_CUT] = dot_t(queries, keys[at : at + DECODE_CUT, :])
+    loads[1].wait()
+
+
+def early(own, ready, out_weight):
+    return pl.pallas_call(
+        early_kernel,
+        out_shape=(
+            pltpu.VMEM((HEADS // 2, 2 * QUERIES, HALF), jnp.float32),
+            pltpu.VMEM(ready.shape, ready.dtype),
+            pltpu.VMEM((EARLY, MODEL), jnp.bfloat16),
+        ),
+        in_specs=[vmem, hbm, hbm],
+        out_specs=(vmem,) * 3,
+        scratch_shapes=[
+            pltpu.VMEM((HALF, WIDTH), jnp.bfloat16),
+            pltpu.SemaphoreType.DMA((2,)),
+        ],
+        compiler_params=params(EARLY_MIB),
+        cost_estimate=pl.CostEstimate(
+            flops=2 * 1024 * 1024 * 640, bytes_accessed=12_000_000, transcendentals=0
+        ),
+        name="early",
+    )(own, ready, out_weight)
+
+
 def decode_kernel(
-    info, own, other, ready, value_ref, weight_hbm,
+    info, own, other, early, ready, first_weight, value_ref, weight_hbm,
     keep_ref, send_ref, weight, sem, keys, bias, s0, s1, w0, w1, heads_out,
 ):
     core = info[1]
-    load = pltpu.make_async_copy(weight_hbm, weight, sem)
+    load = pltpu.make_async_copy(weight_hbm.at[EARLY:, :], weight, sem)
     load.start()
-    unpack(own, other, keys, [keys])
+    unpack(own, keys, [], 0)
+    unpack(other, keys, [keys], HALF)
     keys[POOL:, :] = ready[NEWEST:BIAS, :]
     for at in range(0, KEYS, WIDTH):
         row = BIAS + at // WIDTH * QUERIES
@@ -298,10 +353,12 @@
 
     def score(item, at, size):
         queries = ready[item * rows : (item + 1) * rows, :]
-        scores[item % 2][:, at : at + size] = dot_t(queries, keys[at : at + size, :])
+        scores[item % 2][:, at - HALF : at - HALF + size] = dot_t(queries, keys[at : at + size, :])
 
     def soften(item, start):
-        part = softmax_rows(scores[item % 2], bias, weights[item % 2], start, SOFT)
+        part = softmax_rows(
+            [early.at[item], scores[item % 2]], bias, weights[item % 2], start, SOFT
+        )
         inverse.setdefault(item, []).append(part)
 
     def mix(item):
@@ -319,7 +376,7 @@
             ).astype(jnp.bfloat16)
 
     turns = rows // SOFT
-    parts = [(at, min(DECODE_CUT, KEYS - at)) for at in range(0, KEYS, DECODE_CUT)]
+    parts = [(at, min(DECODE_CUT, KEYS - at)) for at in range(HALF, KEYS, DECODE_CUT)]
     for stage in range(items + 2):
         if 0 <= stage - 2 < items:
             mix(stage - 2)
@@ -333,26 +390,27 @@
 
     for place in range(8):
         columns = slice(place * 2 * SHARE, (place + 1) * 2 * SHARE)
-        turned = dot(heads_out[...], weight[:, columns]).T
+        turned = dot(heads_out[:, :EARLY], first_weight[:, columns])
+        turned = (turned + dot(heads_out[:, EARLY:], weight[:, columns])).T
         first, second = turned[:SHARE], turned[SHARE:]
         keep_ref[place] = jnp.where(core == 0, first, second).astype(jnp.bfloat16)
         send_ref[place] = jnp.where(core == 0, second, first).astype(jnp.bfloat16)
 
 
-def decode(info, own, other, ready, absorb_values, out_weight):
+def decode(info, own, other, scores, ready, first_weight, absorb_values, out_weight):
     share = jax.ShapeDtypeStruct((8, SHARE, QUERIES), jnp.bfloat16)
     return pl.pallas_call(
         decode_kernel,
         out_shape=(share, share),
-        in_specs=[smem] + [vmem] * 4 + [hbm],
+        in_specs=[smem] + [vmem] * 6 + [hbm],
         out_specs=(vmem, vmem),
         scratch_shapes=[
-            pltpu.VMEM((HEADS * VALUE_DIM, MODEL), jnp.bfloat16),
+            pltpu.VMEM((HEADS * VALUE_DIM - EARLY, MODEL), jnp.bfloat16),
             pltpu.SemaphoreType.DMA(()),
             pltpu.VMEM((KEYS, WIDTH), jnp.bfloat16),
             pltpu.VMEM((QUERIES, KEYS), jnp.float32),
-            pltpu.VMEM((2 * QUERIES, KEYS), jnp.float32),
-            pltpu.VMEM((2 * QUERIES, KEYS), jnp.float32),
+            pltpu.VMEM((2 * QUERIES, KEYS - HALF), jnp.float32),
+            pltpu.VMEM((2 * QUERIES, KEYS - HALF), jnp.float32),
             pltpu.VMEM((2 * QUERIES, KEYS), jnp.bfloat16),
             pltpu.VMEM((2 * QUERIES, KEYS), jnp.bfloat16),
             pltpu.VMEM((QUERIES, HEADS * VALUE_DIM), jnp.bfloat16),
@@ -364,7 +422,7 @@
             transcendentals=1024 * 2176,
         ),
         name="decode",
-    )(info, own, other, ready, absorb_values, out_weight)
+    )(info, own, other, scores, ready, first_weight, absorb_values, out_weight)
 
 
 def gather_sum_kernel(parts, out_ref):
@@ -411,7 +469,10 @@
     )
     own, ready, pre_ready = lax.optimization_barrier((own, ready, pre_ready))
     other = lax.ppermute(own, BOTH, other_core())
-    keep, send = decode(info, own, other, ready, absorb_values, out_weight)
+    scores, ready, first_weight = early(own, ready, out_weight)
+    keep, send = decode(
+        info, own, other, scores, ready, first_weight, absorb_values, out_weight
+    )
     arrived = lax.ppermute(send, BOTH, other_core())
     chip = (keep.astype(jnp.float32) + arrived.astype(jnp.float32)).astype(jnp.bfloat16)
     chip, own, other = lax.optimization_barrier((chip, own, other))

time: 74.6 us -> 71.7 us (0.961)
  waiting for transfers between devices: 17.1 us -> 14.9 us
  local copies, waits for them, and re-layouts: 4.58 us -> 3.31 us
  Pallas kernels: 31.6 us -> 32.4 us
    pallas_call x0 -> x1, Pallas kernels: none -> 3.45 us  [early(): pl.pallas_call(early_kernel, out_shape=(pltpu.VMEM((HEADS // 2, 2 * QUERI...]
    pallas_call x1, Pallas kernels: 12.4 us -> 9.73 us  [decode(): pl.pallas_call(decode_kernel, out_shape=(share, share), in_specs=[smem] +...]
    ppermute x1, waiting for transfers between devices: 2.47 us -> 0.01 us  [on_device(): other = lax.ppermute(own, BOTH, other_core())]
    unnamed x14 -> x10, local copies, waits for them, and re-layouts: 3.89 us -> 2.61 us
  transfers between devices with their start and end apart: 4 -> 4, of which waited for: 3 -> 3; matrix products, arithmetic and copies ran while one was open for 2% -> 2% of each run, Pallas kernels for 23% -> 29%
where the time goes in v5:
time: 71.7 us; the launch traced here: 71.3 us
  Pallas kernels  32.4 us (45%)
  starting transfers between devices  18.1 us (25%)
  waiting for transfers between devices  14.9 us (21%)
  local copies, waits for them, and re-layouts  3.31 us (5%)
  other arithmetic  1.84 us (3%)
  between operations  0.73 us (1%)
    all_to_all x1, waiting for transfers between devices, on_device(): lax.all_to_all(pack(pre_latent), BOTH, 0, 0, axis_index_groups=same_core_...  12.4 us
    pallas_call x1, Pallas kernels, prefill(): pl.pallas_call(prefill_kernel, out_shape=jax.ShapeDtypeStruct((TOKENS, HE...  12.1 us
    all_to_all x1, starting transfers between devices, on_device(): lax.all_to_all(pack(pre_latent), BOTH, 0, 0, axis_index_groups=same_core_...  12 us
    pallas_call x1, Pallas kernels, decode(): pl.pallas_call(decode_kernel, out_shape=(share, share), in_specs=[smem] +...  9.73 us
    pallas_call x1, Pallas kernels, absorb(): pl.pallas_call(absorb_kernel, out_shape=(jax.ShapeDtypeStruct((BIAS + 4 *...  5.08 us
    all_to_all x1, starting transfers between devices, on_device(): parts = lax.all_to_all(chip, BOTH, 0, 0, axis_index_groups=chip_groups())  3.77 us
    pallas_call x1, Pallas kernels, early(): pl.pallas_call(early_kernel, out_shape=(pltpu.VMEM((HEADS // 2, 2 * QUERI...  3.45 us
    unnamed x10, local copies, waits for them, and re-layouts  2.61 us
  transfers between devices with their start and end apart: 4, of which 3 were waited for; matrix products, arithmetic and copies ran while one was open for 2% of the time, Pallas kernels for 29%

profile of v5, /device:TPU:1, one launch (start us, length us, event | category | flops | bytes accessed | tf_op | source)
XLA Modules:
  0.0 71.3 jit_solution(17167014771424943517)
XLA Ops:
  0.6 0.0 copy-start.1
  0.6 0.7 %copy-done.1 = bf16[16,576]{1,0:T(8,128)(2,1)S(1)} copy-done((bf16[16,576]{1,0:T(8,128)(2,1)S(1)}, bf16[16,576]{1,0:T(8,128)(2,1)}, u32[]{:S(2)}) %copy-start.1) | copy-done | bytes 18456
  1.4 0.0 copy-start.4
  1.4 1.2 %pack.1 = bf16[64,72,128]{2,1,0:T(8,128)(2,1)} custom-call(bf16[16,576]{1,0:T(8,128)(2,1)S(1)} %copy-done.1), custom_call_target="tpu_custom_call" | custom-call | tf_op jit(solution)/shard_map/pack/pallas_call | solution.py:101
  2.6 12.0 %all-to-all-start = ((bf16[64,72,128]{2,1,0:T(8,128)(2,1)}), bf16[64,72,128]{2,1,0:T(8,128)(2,1)S(1)}, u32[]{:S(2)}, u32[]{:S(2)}) async-start(bf16[64,72,128]{2,1,0:T(8,128)(2,1)} %pack.1), calls=%async_computation | async-start | bytes 2359296 | tf_op jit(solution)/shard_map/all_to_all | solution.py:459
  14.5 0.0 copy-done.4
  14.5 0.7 copy.11.length_ref
  15.2 0.7 pad_add_fusion.info
  15.9 5.1 %absorb.1 = (bf16[1664,640]{1,0:T(8,128)(2,1)}, bf16[1536,1024]{1,0:T(8,128)(2,1)}) custom-call(s32[2]{0:T(128)} %pad_add_fusion.info, bf16[128,1536]{1,0:T(8,128)(2,1)} %bitcast.6, bf16[512,1024]{1,0:T(8,128)(2,1)} %key_ref.1, bf16[128,576]{1,0:T(8,128)(2,1)} %bitcast.7, s32[32,1]{1,0:T(8,128)} %copy.11.length_ref, s32[32,32]{1,0:T(8,128)} %table_ref.1, ...), custom_call_target="tpu_custom_call" | custom-call | flops 134217728 | bytes 5000000 | tf_op jit(solution)/shard_map/absorb/pallas_call | solution.py:190
  21.0 12.4 %all-to-all-done.own = bf16[64,72,128]{2,1,0:T(8,128)(2,1)S(1)} async-done(((bf16[64,72,128]{2,1,0:T(8,128)(2,1)}), bf16[64,72,128]{2,1,0:T(8,128)(2,1)S(1)}, u32[]{:S(2)}, u32[]{:S(2)}) %all-to-all-start) | async-done | bytes 1179680 | tf_op jit(solution)/shard_map/all_to_all | solution.py:459
  33.4 0.0 copy-start
  33.4 0.0 copy-start.2
  33.4 2.2 %collective-permute-start = (bf16[64,72,128]{2,1,0:T(8,128)(2,1)S(1)}, bf16[64,72,128]{2,1,0:T(8,128)(2,1)S(1)}, u32[]{:S(2)}, u32[]{:S(2)}) collective-permute-start(bf16[64,72,128]{2,1,0:T(8,128)(2,1)S(1)} %all-to-all-done.own), channel_id=1, source_target_pairs={{0,1},{1,0},{4,5},{5,4},{8,9},{9,8},{12,13},{13,12},{2,3},{3,2},{6... | collective-permute-start | bytes 3538952 | tf_op jit(solution)/shard_map/ppermute | solution.py:471
  35.7 3.4 %early.1 = (f32[4,256,1024]{2,1,0:T(8,128)S(1)}, bf16[1664,640]{1,0:T(8,128)(2,1)S(1)}, bf16[256,7168]{1,0:T(8,128)(2,1)S(1)}) custom-call(bf16[64,72,128]{2,1,0:T(8,128)(2,1)S(1)} %all-to-all-done.own, bf16[1664,640]{1,0:T(8,128)(2,1)} %get-tuple-element.18.ready_hbm, bf16[1024,7168]{1,0:T(8,128)(2,1)} %weight_hbm.3), custom_call_target="tpu_custom_call" | custom-call | flops 1342177280 | bytes 12000000 | tf_op jit(solution)/shard_map/early/pallas_call | solution.py:314
  39.1 0.0 collective-permute-done.other
  39.1 0.0 copy-done
  39.2 0.0 copy-done.2
  39.2 9.7 %decode.1 = (bf16[8,448,128]{2,1,0:T(8,128)(2,1)S(1)}, bf16[8,448,128]{2,1,0:T(8,128)(2,1)S(1)}) custom-call(s32[2]{0:T(128)S(1)} %copy-done.2, bf16[64,72,128]{2,1,0:T(8,128)(2,1)S(1)} %all-to-all-done.own, bf16[64,72,128]{2,1,0:T(8,128)(2,1)S(1)} %collective-permute-done.other, f32[4,256,1024]{2,1,0:T(8,128)S(1)} %get-tuple-element.19.early, ...), custom_call_target="tpu_custom_call" | custom-call | flops 7583301632 | bytes 22000000 | tf_op jit(solution)/shard_map/decode/pallas_call | solution.py:402
  48.9 0.2 collective-permute-start.1
  49.1 2.4 %collective-permute-done.1 = bf16[8,448,128]{2,1,0:T(8,128)(2,1)S(1)} collective-permute-done((bf16[8,448,128]{2,1,0:T(8,128)(2,1)S(1)}, bf16[8,448,128]{2,1,0:T(8,128)(2,1)S(1)}, u32[]{:S(2)}, u32[]{:S(2)}) %collective-permute-start.1) | collective-permute-done | bytes 917536 | tf_op jit(solution)/shard_map/ppermute | solution.py:476
  51.5 1.2 %add_convert_fusion = bf16[8,448,128]{2,1,0:T(8,128)(2,1)} fusion(bf16[8,448,128]{2,1,0:T(8,128)(2,1)S(1)} %collective-permute-done.1, bf16[8,448,128]{2,1,0:T(8,128)(2,1)S(1)} %get-tuple-element.22), kind=kLoop, calls=%fused_computation | loop fusion | flops 1835008 | bytes 2752512 | tf_op jit(solution)/shard_map/convert_element_type | solution.py:477
  52.6 3.8 %all-to-all-start.1 = ((bf16[8,448,128]{2,1,0:T(8,128)(2,1)}), bf16[8,448,128]{2,1,0:T(8,128)(2,1)S(1)}, u32[]{:S(2)}, u32[]{:S(2)}) async-start(bf16[8,448,128]{2,1,0:T(8,128)(2,1)} %add_convert_fusion), calls=%async_computation.1 | async-start | bytes 1835008 | tf_op jit(solution)/shard_map/all_to_all | solution.py:479
  56.4 0.0 copy-start.3
  56.4 1.9 %copy-done.3 = bf16[1536,1024]{1,0:T(8,128)(2,1)S(1)} copy-done((bf16[1536,1024]{1,0:T(8,128)(2,1)S(1)}, bf16[1536,1024]{1,0:T(8,128)(2,1)}, u32[]{:S(2)}) %copy-start.3) | copy-done | bytes 3145752
  58.3 12.1 %prefill.1 = bf16[256,1024]{1,0:T(8,128)(2,1)} custom-call(s32[2]{0:T(128)S(1)} %copy-done.2, bf16[64,72,128]{2,1,0:T(8,128)(2,1)S(1)} %all-to-all-done.own, bf16[64,72,128]{2,1,0:T(8,128)(2,1)S(1)} %collective-permute-done.other, bf16[1536,1024]{1,0:T(8,128)(2,1)S(1)} %copy-done.3), custom_call_target="tpu_custom_call" | custom-call | flops 8589934592 | bytes 10000000 | tf_op jit(solution)/shard_map/prefill/pallas_call | solution.py:275
  70.4 0.1 all-to-all-done.1.parts
  70.5 0.8 %gather_sum.1 = bf16[128,448]{1,0:T(8,128)(2,1)} custom-call(bf16[8,448,128]{2,1,0:T(8,128)(2,1)S(1)} %all-to-all-done.1.parts), custom_call_target="tpu_custom_call" | custom-call | tf_op jit(solution)/shard_map/gather_sum/pallas_call | solution.py:436
Async XLA Ops:
  0.6 0.7 %copy-start.1 = (bf16[16,576]{1,0:T(8,128)(2,1)S(1)}, bf16[16,576]{1,0:T(8,128)(2,1)}, u32[]{:S(2)}) copy-start(bf16[16,576]{1,0:T(8,128)(2,1)} %latent_ref.1) | copy-start | bytes 55300
  1.4 13.2 %copy-start.4 = (s32[32]{0:T(128)S(1)}, s32[32]{0:T(128)}, u32[]{:S(2)}) copy-start(s32[32]{0:T(128)} %param.15) | copy-start | bytes 388
  2.6 30.9 %all-to-all-start = ((bf16[64,72,128]{2,1,0:T(8,128)(2,1)}), bf16[64,72,128]{2,1,0:T(8,128)(2,1)S(1)}, u32[]{:S(2)}, u32[]{:S(2)}) async-start(bf16[64,72,128]{2,1,0:T(8,128)(2,1)} %pack.1), calls=%async_computation | async-start | bytes 2359296 | tf_op jit(solution)/shard_map/all_to_all | solution.py:459
  33.4 5.7 %copy-start = (bf16[512,1024]{1,0:T(8,128)(2,1)S(1)}, bf16[512,1024]{1,0:T(8,128)(2,1)}, u32[]{:S(2)}) copy-start(bf16[512,1024]{1,0:T(8,128)(2,1)} %value_ref.3) | copy-start | bytes 3145732
  33.4 5.7 %copy-start.2 = (s32[2]{0:T(128)S(1)}, s32[2]{0:T(128)}, u32[]{:S(2)}) copy-start(s32[2]{0:T(128)} %pad_add_fusion.info) | copy-start | bytes 28
  33.4 5.7 %collective-permute-start = (bf16[64,72,128]{2,1,0:T(8,128)(2,1)S(1)}, bf16[64,72,128]{2,1,0:T(8,128)(2,1)S(1)}, u32[]{:S(2)}, u32[]{:S(2)}) collective-permute-start(bf16[64,72,128]{2,1,0:T(8,128)(2,1)S(1)} %all-to-all-done.own), channel_id=1, source_target_pairs={{0,1},{1,0},{4,5},{5,4},{8,9},{9,8},{12,13},{13,12},{2,3},{3,2},{6... | collective-permute-start | bytes 3538952 | tf_op jit(solution)/shard_map/ppermute | solution.py:471
  48.9 2.6 %collective-permute-start.1 = (bf16[8,448,128]{2,1,0:T(8,128)(2,1)S(1)}, bf16[8,448,128]{2,1,0:T(8,128)(2,1)S(1)}, u32[]{:S(2)}, u32[]{:S(2)}) collective-permute-start(bf16[8,448,128]{2,1,0:T(8,128)(2,1)S(1)} %get-tuple-element.23), channel_id=1, source_target_pairs={{0,1},{1,0},{4,5},{5,4},{8,9},{9,8},{12,13},{13,12},{2,3},{3,2},{6... | collective-permute-start | bytes 2752520 | tf_op jit(solution)/shard_map/ppermute | solution.py:476
  52.6 17.8 %all-to-all-start.1 = ((bf16[8,448,128]{2,1,0:T(8,128)(2,1)}), bf16[8,448,128]{2,1,0:T(8,128)(2,1)S(1)}, u32[]{:S(2)}, u32[]{:S(2)}) async-start(bf16[8,448,128]{2,1,0:T(8,128)(2,1)} %add_convert_fusion), calls=%async_computation.1 | async-start | bytes 1835008 | tf_op jit(solution)/shard_map/all_to_all | solution.py:479
  56.4 1.9 %copy-start.3 = (bf16[1536,1024]{1,0:T(8,128)(2,1)S(1)}, bf16[1536,1024]{1,0:T(8,128)(2,1)}, u32[]{:S(2)}) copy-start(bf16[1536,1024]{1,0:T(8,128)(2,1)} %get-tuple-element.26.ready) | copy-start | bytes 9437188

commit v6 on v5

--- a/solution.py
+++ b/solution.py
@@ -37,7 +37,8 @@
 SOFT = 16
 DECODE_CUT = 256
 PREFILL_MIB = 48
-DECODE_MIB = 34
+DECODE_MIB = 24
+KEEP_MIB = 24
 EARLY_MIB = 43
 EARLY = 256
 to_exp2 = math.log2(math.e) / math.sqrt(HEAD)
@@ -88,19 +89,23 @@
 
 
 def pack_kernel(latent_ref, out_ref):
+    late = (lax.axis_index("tp") // 2) % 2
     latent = latent_ref[...].astype(jnp.float32)
     rope = latent[:, LATENT:]
     parts = [latent[:, at : at + 128] for at in range(0, LATENT, 128)]
-    parts.append(jnp.concatenate([rope[:8], rope[8:]], axis=1))
-    piece = jnp.concatenate(parts, axis=0).astype(jnp.bfloat16)
-    for place in range(64):
-        out_ref[place] = piece
+    rope = jnp.concatenate([rope[:8], rope[8:]], axis=1)
+    piece = jnp.where(
+        late == 0, jnp.concatenate([*parts, rope], axis=0), jnp.concatenate([rope, *parts], axis=0)
+    )
+    two = jnp.concatenate([piece, piece], axis=0).astype(jnp.bfloat16)
+    for place in range(32):
+        out_ref[place] = two
 
 
 def pack(latent):
     return pl.pallas_call(
         pack_kernel,
-        out_shape=jax.ShapeDtypeStruct((64, PIECE, 128), jnp.bfloat16),
+        out_shape=jax.ShapeDtypeStruct((32, 2 * PIECE, 128), jnp.bfloat16),
         in_specs=[vmem],
         out_specs=vmem,
         compiler_params=params(16),
@@ -109,14 +114,16 @@
 
 
 def unpack(source, latent, ropes, at):
-    for piece in range(0, 64, 8):
-        rows = slice(at + piece * 16, at + piece * 16 + 128)
-        pieces = slice(piece, piece + 8)
+    for pair in range(0, 32, 4):
+        rows = slice(at + pair * 32, at + pair * 32 + 128)
+        pairs = slice(pair, pair + 4)
         for tile in range(4):
-            latent[rows, tile * 128 : (tile + 1) * 128] = source[
-                pieces, tile * 16 : (tile + 1) * 16, :
-            ].reshape(128, 128)
-        rope = source[pieces, 64:72, :].astype(jnp.float32)
+            first = source[pairs, tile * 16 : (tile + 1) * 16, :]
+            second = source[pairs, 80 + tile * 16 : 96 + tile * 16, :]
+            latent[rows, tile * 128 : (tile + 1) * 128] = jnp.stack([first, second], axis=1).reshape(
+                128, 128
+            )
+        rope = source[pairs, 64:80, :].astype(jnp.float32).reshape(8, 8, 128)
         left = lax.broadcasted_iota(jnp.int32, rope.shape, 2) < ROPE
         both = jnp.concatenate([jnp.where(left, rope, 0.0), jnp.where(left, 0.0, rope)], axis=1)
         both = both.reshape(128, 128).astype(jnp.bfloat16)
@@ -295,8 +302,9 @@
 
 def early_kernel(own, ready_hbm, weight_hbm, scores, ready, weight, keys, sems):
     loads = [
-        pltpu.make_async_copy(ready_hbm, ready, sems.at[0]),
-        pltpu.make_async_copy(weight_hbm.at[:EARLY, :], weight, sems.at[1]),
+        pltpu.make_async_copy(ready_hbm.at[:NEWEST, :], ready.at[:NEWEST, :], sems.at[0]),
+        pltpu.make_async_copy(ready_hbm.at[NEWEST:, :], ready.at[NEWEST:, :], sems.at[1]),
+        pltpu.make_async_copy(weight_hbm.at[:EARLY, :], weight, sems.at[2]),
     ]
     for load in loads:
         load.start()
@@ -308,6 +316,7 @@
             queries = ready[item * rows : (item + 1) * rows, :]
             scores[item, :, at : at + DECODE_CUT] = dot_t(queries, keys[at : at + DECODE_CUT, :])
     loads[1].wait()
+    loads[2].wait()
 
 
 def early(own, ready, out_weight):
@@ -322,7 +331,7 @@
         out_specs=(vmem,) * 3,
         scratch_shapes=[
             pltpu.VMEM((HALF, WIDTH), jnp.bfloat16),
-            pltpu.SemaphoreType.DMA((2,)),
+            pltpu.SemaphoreType.DMA((3,)),
         ],
         compiler_params=params(EARLY_MIB),
         cost_estimate=pl.CostEstimate(
@@ -334,11 +343,17 @@
 
 def decode_kernel(
     info, own, other, early, ready, first_weight, value_ref, weight_hbm,
-    keep_ref, send_ref, weight, sem, keys, bias, s0, s1, w0, w1, heads_out,
+    send_ref, heads_out, weight, sems, partial, keys, bias, s0, s1, w0, w1,
 ):
     core = info[1]
-    load = pltpu.make_async_copy(weight_hbm.at[EARLY:, :], weight, sem)
-    load.start()
+    loads = [
+        pltpu.make_async_copy(
+            weight_hbm.at[at : at + size, :], weight.at[at - EARLY : at - EARLY + size, :], sem
+        )
+        for at, size, sem in ((EARLY, 256, sems.at[0]), (EARLY + 256, 512, sems.at[1]))
+    ]
+    for load in loads:
+        load.start()
     unpack(own, keys, [], 0)
     unpack(other, keys, [keys], HALF)
     keys[POOL:, :] = ready[NEWEST:BIAS, :]
@@ -380,40 +395,78 @@
     for stage in range(items + 2):
         if 0 <= stage - 2 < items:
             mix(stage - 2)
+        if stage == items:
+            loads[0].wait()
+            for place in range(8):
+                columns = columns_for(place, 1 - core)
+                partial[place] = dot(heads_out[:, :EARLY], first_weight[:, columns]) + dot(
+                    heads_out[:, EARLY : EARLY + 256], weight[:256, columns]
+                )
         for turn in range(turns):
             if stage < items:
                 for at, size in parts[turn * len(parts) // turns : (turn + 1) * len(parts) // turns]:
                     score(stage, at, size)
             if 0 <= stage - 1 < items:
                 soften(stage - 1, turn * SOFT)
-    load.wait()
-
+    loads[1].wait()
     for place in range(8):
-        columns = slice(place * 2 * SHARE, (place + 1) * 2 * SHARE)
-        turned = dot(heads_out[:, :EARLY], first_weight[:, columns])
-        turned = (turned + dot(heads_out[:, EARLY:], weight[:, columns])).T
-        first, second = turned[:SHARE], turned[SHARE:]
-        keep_ref[place] = jnp.where(core == 0, first, second).astype(jnp.bfloat16)
-        send_ref[place] = jnp.where(core == 0, second, first).astype(jnp.bfloat16)
+        rest = dot(heads_out[:, EARLY + 256 :], weight[256:, columns_for(place, 1 - core)])
+        send_ref[place] = turned(partial[place] + rest, 1 - core)
+
+
+def columns_for(place, core):
+    start = place * 2 * SHARE + core * (SHARE - 64)
+    return pl.ds(pl.multiple_of(start, 128), SHARE + 64)
+
+
+def turned(product, core):
+    columns = product.T
+    return jnp.where(core == 0, columns[:SHARE], columns[64:]).astype(jnp.bfloat16)
+
+
+def keep_kernel(info, heads_out, first_weight, weight, keep_ref):
+    core = info[1]
+    for place in range(8):
+        columns = columns_for(place, core)
+        product = dot(heads_out[:, :EARLY], first_weight[:, columns])
+        product = product + dot(heads_out[:, EARLY:], weight[:, columns])
+        keep_ref[place] = turned(product, core)
+
+
+def own_share(info, heads_out, first_weight, weight):
+    return pl.pallas_call(
+        keep_kernel,
+        out_shape=jax.ShapeDtypeStruct((8, SHARE, QUERIES), jnp.bfloat16),
+        in_specs=[smem] + [vmem] * 3,
+        out_specs=vmem,
+        compiler_params=params(KEEP_MIB),
+        cost_estimate=pl.CostEstimate(
+            flops=2 * 128 * 1024 * 4096, bytes_accessed=8_000_000, transcendentals=0
+        ),
+        name="own_share",
+    )(info, heads_out, first_weight, weight)
 
 
 def decode(info, own, other, scores, ready, first_weight, absorb_values, out_weight):
-    share = jax.ShapeDtypeStruct((8, SHARE, QUERIES), jnp.bfloat16)
+    width = HEADS * VALUE_DIM
     return pl.pallas_call(
         decode_kernel,
-        out_shape=(share, share),
+        out_shape=(
+            jax.ShapeDtypeStruct((8, SHARE, QUERIES), jnp.bfloat16),
+            pltpu.VMEM((QUERIES, width), jnp.bfloat16),
+            pltpu.VMEM((width - EARLY, MODEL), jnp.bfloat16),
+        ),
         in_specs=[smem] + [vmem] * 6 + [hbm],
-        out_specs=(vmem, vmem),
+        out_specs=(vmem,) * 3,
         scratch_shapes=[
-            pltpu.VMEM((HEADS * VALUE_DIM - EARLY, MODEL), jnp.bfloat16),
-            pltpu.SemaphoreType.DMA(()),
+            pltpu.SemaphoreType.DMA((2,)),
+            pltpu.VMEM((8, QUERIES, SHARE + 64), jnp.float32),
             pltpu.VMEM((KEYS, WIDTH), jnp.bfloat16),
             pltpu.VMEM((QUERIES, KEYS), jnp.float32),
             pltpu.VMEM((2 * QUERIES, KEYS - HALF), jnp.float32),
             pltpu.VMEM((2 * QUERIES, KEYS - HALF), jnp.float32),
             pltpu.VMEM((2 * QUERIES, KEYS), jnp.bfloat16),
             pltpu.VMEM((2 * QUERIES, KEYS), jnp.bfloat16),
-            pltpu.VMEM((QUERIES, HEADS * VALUE_DIM), jnp.bfloat16),
         ],
         compiler_params=params(DECODE_MIB),
         cost_estimate=pl.CostEstimate(
@@ -456,7 +509,9 @@
 ):
     tp = lax.axis_index("tp")
     info = jnp.stack([lax.axis_index("ctx"), tp % 2]).astype(jnp.int32)
-    own = lax.all_to_all(pack(pre_latent), BOTH, 0, 0, axis_index_groups=same_core_groups())
+    pieces = pack(pre_latent).reshape(64, PIECE, 128)
+    own = lax.all_to_all(pieces, BOTH, 0, 0, axis_index_groups=same_core_groups())
+    own = own.reshape(32, 2 * PIECE, 128)
     ready, pre_ready = absorb(
         info,
         step_queries.reshape(QUERIES, HEADS * HEAD),
@@ -470,10 +525,11 @@
     own, ready, pre_ready = lax.optimization_barrier((own, ready, pre_ready))
     other = lax.ppermute(own, BOTH, other_core())
     scores, ready, first_weight = early(own, ready, out_weight)
-    keep, send = decode(
+    send, heads_out, weight = decode(
         info, own, other, scores, ready, first_weight, absorb_values, out_weight
     )
     arrived = lax.ppermute(send, BOTH, other_core())
+    keep = own_share(info, heads_out, first_weight, weight)
     chip = (keep.astype(jnp.float32) + arrived.astype(jnp.float32)).astype(jnp.bfloat16)
     chip, own, other = lax.optimization_barrier((chip, own, other))
     parts = lax.all_to_all(chip, BOTH, 0, 0, axis_index_groups=chip_groups())

time: 71.7 us -> 70.9 us (0.989)
  waiting for transfers between devices: 14.9 us -> 13.2 us
  Pallas kernels: 32.4 us -> 33.4 us
    ppermute x1, waiting for transfers between devices: 2.39 us -> 0.45 us  [on_device(): arrived = lax.ppermute(send, BOTH, other_core())]
    pallas_call x2 -> x3, Pallas kernels: 10.9 us -> 12.2 us  [the longest x1 9.05 us: decode(): pl.pallas_call(decode_kernel, out_shape=(jax.ShapeDtypeStruct((8, SHARE,...]
    unnamed x10 -> x14, local copies, waits for them, and re-layouts: 2.61 us -> 2.62 us
  transfers between devices with their start and end apart: 4 -> 4, of which waited for: 3 -> 3; matrix products, arithmetic and copies ran while one was open for 2% -> 2% of each run, Pallas kernels for 29% -> 32%
where the time goes in v6:
time: 70.9 us; the launch traced here: 70.5 us
  Pallas kernels  33.4 us (47%)
  starting transfers between devices  18.1 us (26%)
  waiting for transfers between devices  13.2 us (19%)
  local copies, waits for them, and re-layouts  3.31 us (5%)
  other arithmetic  1.81 us (3%)
  between operations  0.77 us (1%)
    all_to_all x1, waiting for transfers between devices, on_device(): lax.all_to_all(pieces, BOTH, 0, 0, axis_index_groups=same_core_groups())  12.5 us
    pallas_call x1, Pallas kernels, prefill(): pl.pallas_call(prefill_kernel, out_shape=jax.ShapeDtypeStruct((TOKENS, HE...  12.1 us
    all_to_all x1, starting transfers between devices, on_device(): lax.all_to_all(pieces, BOTH, 0, 0, axis_index_groups=same_core_groups())  12 us
    pallas_call x1, Pallas kernels, decode(): pl.pallas_call(decode_kernel, out_shape=(jax.ShapeDtypeStruct((8, SHARE,...  9.05 us
    pallas_call x1, Pallas kernels, absorb(): pl.pallas_call(absorb_kernel, out_shape=(jax.ShapeDtypeStruct((BIAS + 4 *...  5.09 us
    all_to_all x1, starting transfers between devices, on_device(): parts = lax.all_to_all(chip, BOTH, 0, 0, axis_index_groups=chip_groups())  3.55 us
    pallas_call x1, Pallas kernels, early(): pl.pallas_call(early_kernel, out_shape=(pltpu.VMEM((HEADS // 2, 2 * QUERI...  3.17 us
    unnamed x14, local copies, waits for them, and re-layouts  2.62 us
  transfers between devices with their start and end apart: 4, of which 3 were waited for; matrix products, arithmetic and copies ran while one was open for 2% of the time, Pallas kernels for 32%

profile of v6, /device:TPU:1, one launch (start us, length us, event | category | flops | bytes accessed | tf_op | source)
XLA Modules:
  0.0 70.5 jit_solution(18252959513447375202)
XLA Ops:
  0.6 0.0 copy-start.3
  0.6 0.7 %copy-done.3 = bf16[16,576]{1,0:T(8,128)(2,1)S(1)} copy-done((bf16[16,576]{1,0:T(8,128)(2,1)S(1)}, bf16[16,576]{1,0:T(8,128)(2,1)}, u32[]{:S(2)}) %copy-start.3) | copy-done | bytes 18456
  1.4 0.0 copy-start.6
  1.4 1.1 %pack.1 = bf16[32,144,128]{2,1,0:T(8,128)(2,1)} custom-call(bf16[16,576]{1,0:T(8,128)(2,1)S(1)} %copy-done.3), custom_call_target="tpu_custom_call" | custom-call | tf_op jit(solution)/shard_map/pack/pallas_call | solution.py:106
  2.5 12.0 %all-to-all-start = ((bf16[64,72,128]{2,1,0:T(8,128)(2,1)}), bf16[64,72,128]{2,1,0:T(8,128)(2,1)S(1)}, u32[]{:S(2)}, u32[]{:S(2)}) async-start(bf16[64,72,128]{2,1,0:T(8,128)(2,1)} %bitcast.2), calls=%async_computation | async-start | bytes 2359296 | tf_op jit(solution)/shard_map/all_to_all | solution.py:513
  14.5 0.0 copy-done.6
  14.5 0.7 copy.11.length_ref
  15.2 0.6 pad_add_fusion.info
  15.8 5.1 %absorb.1 = (bf16[1664,640]{1,0:T(8,128)(2,1)}, bf16[1536,1024]{1,0:T(8,128)(2,1)}) custom-call(s32[2]{0:T(128)} %pad_add_fusion.info, bf16[128,1536]{1,0:T(8,128)(2,1)} %bitcast.12, bf16[512,1024]{1,0:T(8,128)(2,1)} %key_ref.1, bf16[128,576]{1,0:T(8,128)(2,1)} %bitcast.13, s32[32,1]{1,0:T(8,128)} %copy.11.length_ref, s32[32,32]{1,0:T(8,128)} %table_ref.1, ...), custom_call_target="tpu_custom_call" | custom-call | flops 134217728 | bytes 5000000 | tf_op jit(solution)/shard_map/absorb/pallas_call | solution.py:197
  20.9 12.5 %all-to-all-done = bf16[64,72,128]{2,1,0:T(8,128)(2,1)S(1)} async-done(((bf16[64,72,128]{2,1,0:T(8,128)(2,1)}), bf16[64,72,128]{2,1,0:T(8,128)(2,1)S(1)}, u32[]{:S(2)}, u32[]{:S(2)}) %all-to-all-start) | async-done | bytes 1179680 | tf_op jit(solution)/shard_map/all_to_all | solution.py:513
  33.4 0.0 copy-start
  33.4 0.0 copy-start.4
  33.4 2.2 %collective-permute-start = (bf16[32,144,128]{2,1,0:T(8,128)(2,1)S(1)}, bf16[32,144,128]{2,1,0:T(8,128)(2,1)S(1)}, u32[]{:S(2)}, u32[]{:S(2)}) collective-permute-start(bf16[32,144,128]{2,1,0:T(8,128)(2,1)S(1)} %bitcast.8), channel_id=1, source_target_pairs={{0,1},{1,0},{4,5},{5,4},{8,9},{9,8},{12,13},{13,12},{2,3},{3,2},{6... | collective-permute-start | bytes 3538952 | tf_op jit(solution)/shard_map/ppermute | solution.py:526
  35.6 3.2 %early.1 = (f32[4,256,1024]{2,1,0:T(8,128)S(1)}, bf16[1664,640]{1,0:T(8,128)(2,1)S(1)}, bf16[256,7168]{1,0:T(8,128)(2,1)S(1)}) custom-call(bf16[32,144,128]{2,1,0:T(8,128)(2,1)S(1)} %bitcast.9, bf16[1664,640]{1,0:T(8,128)(2,1)} %get-tuple-element.19.ready_hbm, bf16[1024,7168]{1,0:T(8,128)(2,1)} %weight_hbm.3), custom_call_target="tpu_custom_call" | custom-call | flops 1342177280 | bytes 12000000 | tf_op jit(solution)/shard_map/early/pallas_call | solution.py:323
  38.8 0.0 collective-permute-done.other
  38.8 0.0 copy-start.1
  38.8 0.0 copy-done
  38.8 0.0 copy-done.4
  38.9 9.0 %decode.1 = (bf16[8,448,128]{2,1,0:T(8,128)(2,1)S(1)}, bf16[128,1024]{1,0:T(8,128)(2,1)S(1)}, bf16[768,7168]{1,0:T(8,128)(2,1)S(1)}) custom-call(s32[2]{0:T(128)S(1)} %copy-done.4, bf16[32,144,128]{2,1,0:T(8,128)(2,1)S(1)} %bitcast.10, bf16[32,144,128]{2,1,0:T(8,128)(2,1)S(1)} %collective-permute-done.other, f32[4,256,1024]{2,1,0:T(8,128)S(1)} %get-tuple-element.20.early, ...), custom_call_target="tpu_custom_call" | custom-call | flops 7583301632 | bytes 22000000 | tf_op jit(solution)/shard_map/decode/pallas_call | solution.py:452
  47.9 0.0 copy-done.1
  47.9 0.3 collective-permute-start.1
  48.2 2.0 %own_share.1 = bf16[8,448,128]{2,1,0:T(8,128)(2,1)S(1)} custom-call(s32[2]{0:T(128)S(1)} %copy-done.4, bf16[128,1024]{1,0:T(8,128)(2,1)S(1)} %get-tuple-element.23.heads_out, bf16[256,7168]{1,0:T(8,128)(2,1)S(1)} %get-tuple-element.22.first_weight, bf16[768,7168]{1,0:T(8,128)(2,1)S(1)} %get-tuple-element.24.weight), custom_call_target="tpu_custom_call" | custom-call | flops 1073741824 | bytes 8000000 | tf_op jit(solution)/shard_map/own_share/pallas_call | solution.py:437
  50.2 0.0 copy-start.2
  50.2 0.5 collective-permute-done.1
  50.7 1.2 %add_convert_fusion = bf16[8,448,128]{2,1,0:T(8,128)(2,1)} fusion(bf16[8,448,128]{2,1,0:T(8,128)(2,1)S(1)} %collective-permute-done.1, bf16[8,448,128]{2,1,0:T(8,128)(2,1)S(1)} %own_share.1), kind=kLoop, calls=%fused_computation | loop fusion | flops 1835008 | bytes 2752512 | tf_op jit(solution)/shard_map/convert_element_type | solution.py:533
  51.8 3.6 %all-to-all-start.1 = ((bf16[8,448,128]{2,1,0:T(8,128)(2,1)}), bf16[8,448,128]{2,1,0:T(8,128)(2,1)S(1)}, u32[]{:S(2)}, u32[]{:S(2)}) async-start(bf16[8,448,128]{2,1,0:T(8,128)(2,1)} %add_convert_fusion), calls=%async_computation.1 | async-start | bytes 1835008 | tf_op jit(solution)/shard_map/all_to_all | solution.py:535
  55.4 0.0 copy-done.2
  55.4 0.0 copy-start.5
  55.4 1.9 %copy-done.5 = bf16[1536,1024]{1,0:T(8,128)(2,1)S(1)} copy-done((bf16[1536,1024]{1,0:T(8,128)(2,1)S(1)}, bf16[1536,1024]{1,0:T(8,128)(2,1)}, u32[]{:S(2)}) %copy-start.5) | copy-done | bytes 3145752
  57.3 12.1 %prefill.1 = bf16[256,1024]{1,0:T(8,128)(2,1)} custom-call(s32[2]{0:T(128)S(1)} %copy-done.4, bf16[32,144,128]{2,1,0:T(8,128)(2,1)S(1)} %bitcast.11, bf16[32,144,128]{2,1,0:T(8,128)(2,1)S(1)} %copy-done.2, bf16[1536,1024]{1,0:T(8,128)(2,1)S(1)} %copy-done.5), custom_call_target="tpu_custom_call" | custom-call | flops 8589934592 | bytes 10000000 | tf_op jit(solution)/shard_map/prefill/pallas_call | solution.py:282
  69.4 0.3 all-to-all-done.1.parts
  69.7 0.8 %gather_sum.1 = bf16[128,448]{1,0:T(8,128)(2,1)} custom-call(bf16[8,448,128]{2,1,0:T(8,128)(2,1)S(1)} %all-to-all-done.1.parts), custom_call_target="tpu_custom_call" | custom-call | tf_op jit(solution)/shard_map/gather_sum/pallas_call | solution.py:489
Async XLA Ops:
  0.6 0.7 %copy-start.3 = (bf16[16,576]{1,0:T(8,128)(2,1)S(1)}, bf16[16,576]{1,0:T(8,128)(2,1)}, u32[]{:S(2)}) copy-start(bf16[16,576]{1,0:T(8,128)(2,1)} %latent_ref.1) | copy-start | bytes 55300
  1.4 13.1 %copy-start.6 = (s32[32]{0:T(128)S(1)}, s32[32]{0:T(128)}, u32[]{:S(2)}) copy-start(s32[32]{0:T(128)} %param.15) | copy-start | bytes 388
  2.5 30.9 %all-to-all-start = ((bf16[64,72,128]{2,1,0:T(8,128)(2,1)}), bf16[64,72,128]{2,1,0:T(8,128)(2,1)S(1)}, u32[]{:S(2)}, u32[]{:S(2)}) async-start(bf16[64,72,128]{2,1,0:T(8,128)(2,1)} %bitcast.2), calls=%async_computation | async-start | bytes 2359296 | tf_op jit(solution)/shard_map/all_to_all | solution.py:513
  33.4 5.5 %copy-start = (bf16[512,1024]{1,0:T(8,128)(2,1)S(1)}, bf16[512,1024]{1,0:T(8,128)(2,1)}, u32[]{:S(2)}) copy-start(bf16[512,1024]{1,0:T(8,128)(2,1)} %value_ref.3) | copy-start | bytes 3145732
  33.4 5.5 %copy-start.4 = (s32[2]{0:T(128)S(1)}, s32[2]{0:T(128)}, u32[]{:S(2)}) copy-start(s32[2]{0:T(128)} %pad_add_fusion.info) | copy-start | bytes 28
  33.4 5.4 %collective-permute-start = (bf16[32,144,128]{2,1,0:T(8,128)(2,1)S(1)}, bf16[32,144,128]{2,1,0:T(8,128)(2,1)S(1)}, u32[]{:S(2)}, u32[]{:S(2)}) collective-permute-start(bf16[32,144,128]{2,1,0:T(8,128)(2,1)S(1)} %bitcast.8), channel_id=1, source_target_pairs={{0,1},{1,0},{4,5},{5,4},{8,9},{9,8},{12,13},{13,12},{2,3},{3,2},{6... | collective-permute-start | bytes 3538952 | tf_op jit(solution)/shard_map/ppermute | solution.py:526
  38.8 9.1 %copy-start.1 = (bf16[32,144,128]{2,1,0:T(8,128)(2,1)}, bf16[32,144,128]{2,1,0:T(8,128)(2,1)S(1)}, u32[]{:S(2)}) copy-start(bf16[32,144,128]{2,1,0:T(8,128)(2,1)S(1)} %collective-permute-done.other) | copy-start | bytes 3538948
  47.9 2.7 %collective-permute-start.1 = (bf16[8,448,128]{2,1,0:T(8,128)(2,1)S(1)}, bf16[8,448,128]{2,1,0:T(8,128)(2,1)S(1)}, u32[]{:S(2)}, u32[]{:S(2)}) collective-permute-start(bf16[8,448,128]{2,1,0:T(8,128)(2,1)S(1)} %get-tuple-element.25), channel_id=1, source_target_pairs={{0,1},{1,0},{4,5},{5,4},{8,9},{9,8},{12,13},{13,12},{2,3},{3,2},{6... | collective-permute-start | bytes 2752520 | tf_op jit(solution)/shard_map/ppermute | solution.py:531
  50.2 5.2 %copy-start.2 = (bf16[32,144,128]{2,1,0:T(8,128)(2,1)S(1)}, bf16[32,144,128]{2,1,0:T(8,128)(2,1)}, u32[]{:S(2)}) copy-start(bf16[32,144,128]{2,1,0:T(8,128)(2,1)} %copy-done.1) | copy-start | bytes 3538948
  51.8 17.8 %all-to-all-start.1 = ((bf16[8,448,128]{2,1,0:T(8,128)(2,1)}), bf16[8,448,128]{2,1,0:T(8,128)(2,1)S(1)}, u32[]{:S(2)}, u32[]{:S(2)}) async-start(bf16[8,448,128]{2,1,0:T(8,128)(2,1)} %add_convert_fusion), calls=%async_computation.1 | async-start | bytes 1835008 | tf_op jit(solution)/shard_map/all_to_all | solution.py:535
  55.4 1.9 %copy-start.5 = (bf16[1536,1024]{1,0:T(8,128)(2,1)S(1)}, bf16[1536,1024]{1,0:T(8,128)(2,1)}, u32[]{:S(2)}) copy-start(bf16[1536,1024]{1,0:T(8,128)(2,1)} %get-tuple-element.28.ready) | copy-start | bytes 9437188

commit v7 on v6

--- a/solution.py
+++ b/solution.py
@@ -43,7 +43,6 @@
 EARLY = 256
 to_exp2 = math.log2(math.e) / math.sqrt(HEAD)
 vmem = pl.BlockSpec(memory_space=pltpu.VMEM)
-smem = pl.BlockSpec(memory_space=pltpu.SMEM)
 hbm = pl.BlockSpec(memory_space=pltpu.HBM)
 
 
@@ -78,6 +77,10 @@
         ]
         for core in range(2)
     ]
+
+
+def own_core():
+    return lax.axis_index("tp") % 2
 
 
 def dot(a, b):
@@ -144,9 +147,9 @@
 
 
 def absorb_kernel(
-    info, query_ref, key_ref, latent_ref, length_ref, table_ref, pre_ref, value_ref, out, pre_out
+    query_ref, key_ref, latent_ref, length_ref, table_ref, pre_ref, value_ref, out, pre_out
 ):
-    core = info[1]
+    core = own_core()
     pre_out[:LATENT, :] = key_ref[...]
     pre_out[LATENT : 2 * LATENT, :] = value_ref[...]
     for head in range(HEADS):
@@ -193,21 +196,21 @@
         out[row : row + QUERIES, : part.shape[1]] = part
 
 
-def absorb(info, queries, absorb_keys, step_latent, lengths, table, pre_queries, absorb_values):
+def absorb(queries, absorb_keys, step_latent, lengths, table, pre_queries, absorb_values):
     return pl.pallas_call(
         absorb_kernel,
         out_shape=(
             jax.ShapeDtypeStruct((BIAS + 4 * QUERIES, WIDTH), jnp.bfloat16),
             jax.ShapeDtypeStruct((2 * LATENT + 2 * TOKENS, HEADS * NOPE), jnp.bfloat16),
         ),
-        in_specs=[smem] + [vmem] * 7,
+        in_specs=[vmem] * 7,
         out_specs=(vmem, vmem),
         compiler_params=params(56),
         cost_estimate=pl.CostEstimate(
             flops=2 * 1024 * 128 * 512, bytes_accessed=5_000_000, transcendentals=0
         ),
         name="absorb",
-    )(info, queries, absorb_keys, step_latent, lengths, table, pre_queries, absorb_values)
+    )(queries, absorb_keys, step_latent, lengths, table, pre_queries, absorb_values)
 
 
 def softmax_rows(scores, bias, weights, start, count):
@@ -232,8 +235,8 @@
     return 1.0 / total
 
 
-def prefill_kernel(info, own, other, ready, out_ref, latent, bias, *held):
-    ctx, core = info[0], info[1]
+def prefill_kernel(own, other, ready, out_ref, latent, bias, *held):
+    ctx, core = lax.axis_index("ctx"), own_core()
     keys, values, scores, weights = held[:2], held[2:6], held[6:8], held[8:]
     unpack(own, latent, keys, 0)
     unpack(other, latent, keys, HALF)
@@ -278,11 +281,11 @@
                 soften(stage - 2, turn * SOFT)
 
 
-def prefill(info, own, other, ready):
+def prefill(own, other, ready):
     return pl.pallas_call(
         prefill_kernel,
         out_shape=jax.ShapeDtypeStruct((TOKENS, HEADS * VALUE_DIM), jnp.bfloat16),
-        in_specs=[smem] + [vmem] * 3,
+        in_specs=[vmem] * 3,
         out_specs=vmem,
         scratch_shapes=[
             pltpu.VMEM((POOL, LATENT), jnp.bfloat16),
@@ -297,7 +300,7 @@
             flops=2 * 2048 * 2048 * 1024, bytes_accessed=10_000_000, transcendentals=2048 * 2048
         ),
         name="prefill",
-    )(info, own, other, ready)
+    )(own, other, ready)
 
 
 def early_kernel(own, ready_hbm, weight_hbm, scores, ready, weight, keys, sems):
@@ -342,10 +345,10 @@
 
 
 def decode_kernel(
-    info, own, other, early, ready, first_weight, value_ref, weight_hbm,
+    own, other, early, ready, first_weight, value_ref, weight_hbm,
     send_ref, heads_out, weight, sems, partial, keys, bias, s0, s1, w0, w1,
 ):
-    core = info[1]
+    core = own_core()
     loads = [
         pltpu.make_async_copy(
             weight_hbm.at[at : at + size, :], weight.at[at - EARLY : at - EARLY + size, :], sem
@@ -424,8 +427,8 @@
     return jnp.where(core == 0, columns[:SHARE], columns[64:]).astype(jnp.bfloat16)
 
 
-def keep_kernel(info, heads_out, first_weight, weight, keep_ref):
-    core = info[1]
+def keep_kernel(heads_out, first_weight, weight, keep_ref):
+    core = own_core()
     for place in range(8):
         columns = columns_for(place, core)
         product = dot(heads_out[:, :EARLY], first_weight[:, columns])
@@ -433,21 +436,21 @@
         keep_ref[place] = turned(product, core)
 
 
-def own_share(info, heads_out, first_weight, weight):
+def own_share(heads_out, first_weight, weight):
     return pl.pallas_call(
         keep_kernel,
         out_shape=jax.ShapeDtypeStruct((8, SHARE, QUERIES), jnp.bfloat16),
-        in_specs=[smem] + [vmem] * 3,
+        in_specs=[vmem] * 3,
         out_specs=vmem,
         compiler_params=params(KEEP_MIB),
         cost_estimate=pl.CostEstimate(
             flops=2 * 128 * 1024 * 4096, bytes_accessed=8_000_000, transcendentals=0
         ),
         name="own_share",
-    )(info, heads_out, first_weight, weight)
-
-
-def decode(info, own, other, scores, ready, first_weight, absorb_values, out_weight):
+    )(heads_out, first_weight, weight)
+
+
+def decode(own, other, scores, ready, first_weight, absorb_values, out_weight):
     width = HEADS * VALUE_DIM
     return pl.pallas_call(
         decode_kernel,
@@ -456,7 +459,7 @@
             pltpu.VMEM((QUERIES, width), jnp.bfloat16),
             pltpu.VMEM((width - EARLY, MODEL), jnp.bfloat16),
         ),
-        in_specs=[smem] + [vmem] * 6 + [hbm],
+        in_specs=[vmem] * 6 + [hbm],
         out_specs=(vmem,) * 3,
         scratch_shapes=[
             pltpu.SemaphoreType.DMA((2,)),
@@ -475,7 +478,7 @@
             transcendentals=1024 * 2176,
         ),
         name="decode",
-    )(info, own, other, scores, ready, first_weight, absorb_values, out_weight)
+    )(own, other, scores, ready, first_weight, absorb_values, out_weight)
 
 
 def gather_sum_kernel(parts, out_ref):
@@ -507,13 +510,10 @@
     page_table,
     out_weight,
 ):
-    tp = lax.axis_index("tp")
-    info = jnp.stack([lax.axis_index("ctx"), tp % 2]).astype(jnp.int32)
     pieces = pack(pre_latent).reshape(64, PIECE, 128)
     own = lax.all_to_all(pieces, BOTH, 0, 0, axis_index_groups=same_core_groups())
     own = own.reshape(32, 2 * PIECE, 128)
     ready, pre_ready = absorb(
-        info,
         step_queries.reshape(QUERIES, HEADS * HEAD),
         absorb_keys,
         step_latent.reshape(QUERIES, LATENT + ROPE),
@@ -526,14 +526,14 @@
     other = lax.ppermute(own, BOTH, other_core())
     scores, ready, first_weight = early(own, ready, out_weight)
     send, heads_out, weight = decode(
-        info, own, other, scores, ready, first_weight, absorb_values, out_weight
+        own, other, scores, ready, first_weight, absorb_values, out_weight
     )
     arrived = lax.ppermute(send, BOTH, other_core())
-    keep = own_share(info, heads_out, first_weight, weight)
+    keep = own_share(heads_out, first_weight, weight)
     chip = (keep.astype(jnp.float32) + arrived.astype(jnp.float32)).astype(jnp.bfloat16)
     chip, own, other = lax.optimization_barrier((chip, own, other))
     parts = lax.all_to_all(chip, BOTH, 0, 0, axis_index_groups=chip_groups())
-    prefill_heads = prefill(info, own, other, pre_ready)
+    prefill_heads = prefill(own, other, pre_ready)
     decode_out = gather_sum(parts).reshape(STEPS, ROWS, SHARE)
     return (prefill_heads, decode_out)
 

time: 70.9 us -> 70.3 us (level)
  waiting for transfers between devices: 13.2 us -> 15 us
  Pallas kernels: 33.4 us -> 31.6 us
    unnamed x14 -> x12, local copies, waits for them, and re-layouts: 2.62 us -> 2.62 us
  transfers between devices with their start and end apart: 4 -> 4, of which waited for: 3 -> 3; matrix products, arithmetic and copies ran while one was open for 2% -> 1% of each run, Pallas kernels for 32% -> 30%
where the time goes in v7:
time: 70.3 us; the launch traced here: 69.9 us
  Pallas kernels  31.6 us (45%)
  starting transfers between devices  18.1 us (26%)
  waiting for transfers between devices  15 us (21%)
  local copies, waits for them, and re-layouts  3.31 us (5%)
  other arithmetic  1.17 us (2%)
  between operations  0.75 us (1%)
    all_to_all x1, waiting for transfers between devices, on_device(): lax.all_to_all(pieces, BOTH, 0, 0, axis_index_groups=same_core_groups())  13.1 us
    all_to_all x1, starting transfers between devices, on_device(): lax.all_to_all(pieces, BOTH, 0, 0, axis_index_groups=same_core_groups())  12 us
    pallas_call x1, Pallas kernels, prefill(): pl.pallas_call(prefill_kernel, out_shape=jax.ShapeDtypeStruct((TOKENS, HE...  11.5 us
    pallas_call x1, Pallas kernels, decode(): pl.pallas_call(decode_kernel, out_shape=(jax.ShapeDtypeStruct((8, SHARE,...  8.48 us
    pallas_call x1, Pallas kernels, absorb(): pl.pallas_call(absorb_kernel, out_shape=(jax.ShapeDtypeStruct((BIAS + 4 *...  5.07 us
    all_to_all x1, starting transfers between devices, on_device(): parts = lax.all_to_all(chip, BOTH, 0, 0, axis_index_groups=chip_groups())  3.55 us
    pallas_call x1, Pallas kernels, early(): pl.pallas_call(early_kernel, out_shape=(pltpu.VMEM((HEADS // 2, 2 * QUERI...  3.17 us
    unnamed x12, local copies, waits for them, and re-layouts  2.62 us
  transfers between devices with their start and end apart: 4, of which 3 were waited for; matrix products, arithmetic and copies ran while one was open for 1% of the time, Pallas kernels for 30%

profile of v7, /device:TPU:1, one launch (start us, length us, event | category | flops | bytes accessed | tf_op | source)
XLA Modules:
  0.0 69.9 jit_solution(15348442866980126288)
XLA Ops:
  0.6 0.0 copy-start.3
  0.6 0.7 %copy-done.3 = bf16[16,576]{1,0:T(8,128)(2,1)S(1)} copy-done((bf16[16,576]{1,0:T(8,128)(2,1)S(1)}, bf16[16,576]{1,0:T(8,128)(2,1)}, u32[]{:S(2)}) %copy-start.3) | copy-done | bytes 18456
  1.4 0.0 copy-start.5
  1.4 1.1 %pack.1 = bf16[32,144,128]{2,1,0:T(8,128)(2,1)} custom-call(bf16[16,576]{1,0:T(8,128)(2,1)S(1)} %copy-done.3), custom_call_target="tpu_custom_call" | custom-call | tf_op jit(solution)/shard_map/pack/pallas_call | solution.py:109
  2.5 12.0 %all-to-all-start = ((bf16[64,72,128]{2,1,0:T(8,128)(2,1)}), bf16[64,72,128]{2,1,0:T(8,128)(2,1)S(1)}, u32[]{:S(2)}, u32[]{:S(2)}) async-start(bf16[64,72,128]{2,1,0:T(8,128)(2,1)} %bitcast), calls=%async_computation | async-start | bytes 2359296 | tf_op jit(solution)/shard_map/all_to_all | solution.py:514
  14.5 0.0 copy-done.5
  14.5 0.7 copy.11.length_ref
  15.2 5.1 %absorb.1 = (bf16[1664,640]{1,0:T(8,128)(2,1)}, bf16[1536,1024]{1,0:T(8,128)(2,1)}) custom-call(bf16[128,1536]{1,0:T(8,128)(2,1)} %bitcast.10, bf16[512,1024]{1,0:T(8,128)(2,1)} %key_ref.1, bf16[128,576]{1,0:T(8,128)(2,1)} %bitcast.11, s32[32,1]{1,0:T(8,128)} %copy.11.length_ref, s32[32,32]{1,0:T(8,128)} %table_ref.1, bf16[256,1536]{1,0:T(8,128)(2,1)} %pre_ref.1, ...), custom_call_target="tpu_custom_call" | custom-call | flops 134217728 | bytes 5000000 | tf_op jit(solution)/shard_map/absorb/pallas_call | solution.py:200
  20.2 13.1 %all-to-all-done = bf16[64,72,128]{2,1,0:T(8,128)(2,1)S(1)} async-done(((bf16[64,72,128]{2,1,0:T(8,128)(2,1)}), bf16[64,72,128]{2,1,0:T(8,128)(2,1)S(1)}, u32[]{:S(2)}, u32[]{:S(2)}) %all-to-all-start) | async-done | bytes 1179680 | tf_op jit(solution)/shard_map/all_to_all | solution.py:514
  33.4 0.0 copy-start
  33.4 2.2 %collective-permute-start = (bf16[32,144,128]{2,1,0:T(8,128)(2,1)S(1)}, bf16[32,144,128]{2,1,0:T(8,128)(2,1)S(1)}, u32[]{:S(2)}, u32[]{:S(2)}) collective-permute-start(bf16[32,144,128]{2,1,0:T(8,128)(2,1)S(1)} %bitcast.6), channel_id=1, source_target_pairs={{0,1},{1,0},{4,5},{5,4},{8,9},{9,8},{12,13},{13,12},{2,3},{3,2},{6... | collective-permute-start | bytes 3538952 | tf_op jit(solution)/shard_map/ppermute | solution.py:526
  35.6 3.2 %early.1 = (f32[4,256,1024]{2,1,0:T(8,128)S(1)}, bf16[1664,640]{1,0:T(8,128)(2,1)S(1)}, bf16[256,7168]{1,0:T(8,128)(2,1)S(1)}) custom-call(bf16[32,144,128]{2,1,0:T(8,128)(2,1)S(1)} %bitcast.7, bf16[1664,640]{1,0:T(8,128)(2,1)} %get-tuple-element.19.ready_hbm, bf16[1024,7168]{1,0:T(8,128)(2,1)} %weight_hbm.3), custom_call_target="tpu_custom_call" | custom-call | flops 1342177280 | bytes 12000000 | tf_op jit(solution)/shard_map/early/pallas_call | solution.py:326
  38.8 0.0 collective-permute-done.other
  38.8 0.0 copy-start.1
  38.8 0.0 copy-done
  38.8 8.5 %decode.1 = (bf16[8,448,128]{2,1,0:T(8,128)(2,1)S(1)}, bf16[128,1024]{1,0:T(8,128)(2,1)S(1)}, bf16[768,7168]{1,0:T(8,128)(2,1)S(1)}) custom-call(bf16[32,144,128]{2,1,0:T(8,128)(2,1)S(1)} %bitcast.8, bf16[32,144,128]{2,1,0:T(8,128)(2,1)S(1)} %collective-permute-done.other, f32[4,256,1024]{2,1,0:T(8,128)S(1)} %get-tuple-element.20.early, ...), custom_call_target="tpu_custom_call" | custom-call | flops 7583301632 | bytes 22000000 | tf_op jit(solution)/shard_map/decode/pallas_call | solution.py:455
  47.3 0.0 copy-done.1
  47.3 0.3 collective-permute-start.1
  47.7 1.4 %own_share.1 = bf16[8,448,128]{2,1,0:T(8,128)(2,1)S(1)} custom-call(bf16[128,1024]{1,0:T(8,128)(2,1)S(1)} %get-tuple-element.23.heads_out, bf16[256,7168]{1,0:T(8,128)(2,1)S(1)} %get-tuple-element.22.first_weight, bf16[768,7168]{1,0:T(8,128)(2,1)S(1)} %get-tuple-element.24.weight), custom_call_target="tpu_custom_call" | custom-call | flops 1073741824 | bytes 8000000 | tf_op jit(solution)/shard_map/own_share/pallas_call | solution.py:440
  49.1 0.0 copy-start.2
  49.1 1.0 %collective-permute-done.1 = bf16[8,448,128]{2,1,0:T(8,128)(2,1)S(1)} collective-permute-done((bf16[8,448,128]{2,1,0:T(8,128)(2,1)S(1)}, bf16[8,448,128]{2,1,0:T(8,128)(2,1)S(1)}, u32[]{:S(2)}, u32[]{:S(2)}) %collective-permute-start.1) | collective-permute-done | bytes 917536 | tf_op jit(solution)/shard_map/ppermute | solution.py:531
  50.1 1.2 %add_convert_fusion = bf16[8,448,128]{2,1,0:T(8,128)(2,1)} fusion(bf16[8,448,128]{2,1,0:T(8,128)(2,1)S(1)} %collective-permute-done.1, bf16[8,448,128]{2,1,0:T(8,128)(2,1)S(1)} %own_share.1), kind=kLoop, calls=%fused_computation | loop fusion | flops 1835008 | bytes 2752512 | tf_op jit(solution)/shard_map/convert_element_type | solution.py:533
  51.2 3.6 %all-to-all-start.1 = ((bf16[8,448,128]{2,1,0:T(8,128)(2,1)}), bf16[8,448,128]{2,1,0:T(8,128)(2,1)S(1)}, u32[]{:S(2)}, u32[]{:S(2)}) async-start(bf16[8,448,128]{2,1,0:T(8,128)(2,1)} %add_convert_fusion), calls=%async_computation.1 | async-start | bytes 1835008 | tf_op jit(solution)/shard_map/all_to_all | solution.py:535
  54.8 0.0 copy-done.2
  54.8 0.0 copy-start.4
  54.8 1.9 %copy-done.4 = bf16[1536,1024]{1,0:T(8,128)(2,1)S(1)} copy-done((bf16[1536,1024]{1,0:T(8,128)(2,1)S(1)}, bf16[1536,1024]{1,0:T(8,128)(2,1)}, u32[]{:S(2)}) %copy-start.4) | copy-done | bytes 3145752
  56.7 11.5 %prefill.1 = bf16[256,1024]{1,0:T(8,128)(2,1)} custom-call(bf16[32,144,128]{2,1,0:T(8,128)(2,1)S(1)} %bitcast.9, bf16[32,144,128]{2,1,0:T(8,128)(2,1)S(1)} %copy-done.2, bf16[1536,1024]{1,0:T(8,128)(2,1)S(1)} %copy-done.4), custom_call_target="tpu_custom_call" | custom-call | flops 8589934592 | bytes 10000000 | tf_op jit(solution)/shard_map/prefill/pallas_call | solution.py:285
  68.2 0.9 %all-to-all-done.1.parts = bf16[8,448,128]{2,1,0:T(8,128)(2,1)S(1)} async-done(((bf16[8,448,128]{2,1,0:T(8,128)(2,1)}), bf16[8,448,128]{2,1,0:T(8,128)(2,1)S(1)}, u32[]{:S(2)}, u32[]{:S(2)}) %all-to-all-start.1) | async-done | bytes 917536 | tf_op jit(solution)/shard_map/all_to_all | solution.py:535
  69.1 0.8 %gather_sum.1 = bf16[128,448]{1,0:T(8,128)(2,1)} custom-call(bf16[8,448,128]{2,1,0:T(8,128)(2,1)S(1)} %all-to-all-done.1.parts), custom_call_target="tpu_custom_call" | custom-call | tf_op jit(solution)/shard_map/gather_sum/pallas_call | solution.py:492
Async XLA Ops:
  0.6 0.7 %copy-start.3 = (bf16[16,576]{1,0:T(8,128)(2,1)S(1)}, bf16[16,576]{1,0:T(8,128)(2,1)}, u32[]{:S(2)}) copy-start(bf16[16,576]{1,0:T(8,128)(2,1)} %latent_ref.1) | copy-start | bytes 55300
  1.4 13.1 %copy-start.5 = (s32[32]{0:T(128)S(1)}, s32[32]{0:T(128)}, u32[]{:S(2)}) copy-start(s32[32]{0:T(128)} %param.15) | copy-start | bytes 388
  2.5 30.9 %all-to-all-start = ((bf16[64,72,128]{2,1,0:T(8,128)(2,1)}), bf16[64,72,128]{2,1,0:T(8,128)(2,1)S(1)}, u32[]{:S(2)}, u32[]{:S(2)}) async-start(bf16[64,72,128]{2,1,0:T(8,128)(2,1)} %bitcast), calls=%async_computation | async-start | bytes 2359296 | tf_op jit(solution)/shard_map/all_to_all | solution.py:514
  33.4 5.5 %copy-start = (bf16[512,1024]{1,0:T(8,128)(2,1)S(1)}, bf16[512,1024]{1,0:T(8,128)(2,1)}, u32[]{:S(2)}) copy-start(bf16[512,1024]{1,0:T(8,128)(2,1)} %value_ref.3) | copy-start | bytes 3145732
  33.4 5.4 %collective-permute-start = (bf16[32,144,128]{2,1,0:T(8,128)(2,1)S(1)}, bf16[32,144,128]{2,1,0:T(8,128)(2,1)S(1)}, u32[]{:S(2)}, u32[]{:S(2)}) collective-permute-start(bf16[32,144,128]{2,1,0:T(8,128)(2,1)S(1)} %bitcast.6), channel_id=1, source_target_pairs={{0,1},{1,0},{4,5},{5,4},{8,9},{9,8},{12,13},{13,12},{2,3},{3,2},{6... | collective-permute-start | bytes 3538952 | tf_op jit(solution)/shard_map/ppermute | solution.py:526
  38.8 8.5 %copy-start.1 = (bf16[32,144,128]{2,1,0:T(8,128)(2,1)}, bf16[32,144,128]{2,1,0:T(8,128)(2,1)S(1)}, u32[]{:S(2)}) copy-start(bf16[32,144,128]{2,1,0:T(8,128)(2,1)S(1)} %collective-permute-done.other) | copy-start | bytes 3538948
  47.3 2.7 %collective-permute-start.1 = (bf16[8,448,128]{2,1,0:T(8,128)(2,1)S(1)}, bf16[8,448,128]{2,1,0:T(8,128)(2,1)S(1)}, u32[]{:S(2)}, u32[]{:S(2)}) collective-permute-start(bf16[8,448,128]{2,1,0:T(8,128)(2,1)S(1)} %get-tuple-element.25), channel_id=1, source_target_pairs={{0,1},{1,0},{4,5},{5,4},{8,9},{9,8},{12,13},{13,12},{2,3},{3,2},{6... | collective-permute-start | bytes 2752520 | tf_op jit(solution)/shard_map/ppermute | solution.py:531
  49.1 5.7 %copy-start.2 = (bf16[32,144,128]{2,1,0:T(8,128)(2,1)S(1)}, bf16[32,144,128]{2,1,0:T(8,128)(2,1)}, u32[]{:S(2)}) copy-start(bf16[32,144,128]{2,1,0:T(8,128)(2,1)} %copy-done.1) | copy-start | bytes 3538948
  51.2 17.8 %all-to-all-start.1 = ((bf16[8,448,128]{2,1,0:T(8,128)(2,1)}), bf16[8,448,128]{2,1,0:T(8,128)(2,1)S(1)}, u32[]{:S(2)}, u32[]{:S(2)}) async-start(bf16[8,448,128]{2,1,0:T(8,128)(2,1)} %add_convert_fusion), calls=%async_computation.1 | async-start | bytes 1835008 | tf_op jit(solution)/shard_map/all_to_all | solution.py:535
  54.8 1.9 %copy-start.4 = (bf16[1536,1024]{1,0:T(8,128)(2,1)S(1)}, bf16[1536,1024]{1,0:T(8,128)(2,1)}, u32[]{:S(2)}) copy-start(bf16[1536,1024]{1,0:T(8,128)(2,1)} %get-tuple-element.28.ready) | copy-start | bytes 9437188

commit v8 on v7

--- a/solution.py
+++ b/solution.py
@@ -481,6 +481,23 @@
     )(own, other, scores, ready, first_weight, absorb_values, out_weight)
 
 
+def add_kernel(a_ref, b_ref, out_ref):
+    for place in range(8):
+        both = a_ref[place].astype(jnp.float32) + b_ref[place].astype(jnp.float32)
+        out_ref[place] = both.astype(jnp.bfloat16)
+
+
+def add_shares(a, b):
+    return pl.pallas_call(
+        add_kernel,
+        out_shape=jax.ShapeDtypeStruct(a.shape, a.dtype),
+        in_specs=[vmem] * 2,
+        out_specs=vmem,
+        compiler_params=params(16),
+        name="add_shares",
+    )(a, b)
+
+
 def gather_sum_kernel(parts, out_ref):
     total = parts[0].astype(jnp.float32)
     for place in range(1, parts.shape[0]):
@@ -530,7 +547,7 @@
     )
     arrived = lax.ppermute(send, BOTH, other_core())
     keep = own_share(heads_out, first_weight, weight)
-    chip = (keep.astype(jnp.float32) + arrived.astype(jnp.float32)).astype(jnp.bfloat16)
+    chip = add_shares(keep, arrived)
     chip, own, other = lax.optimization_barrier((chip, own, other))
     parts = lax.all_to_all(chip, BOTH, 0, 0, axis_index_groups=chip_groups())
     prefill_heads = prefill(own, other, pre_ready)

time: 70.3 us -> 70.3 us (level)
  Pallas kernels: 31.6 us -> 32.8 us
  other arithmetic: 1.17 us -> 0 us
    convert_element_type x1 -> x0, other arithmetic: 1.17 us -> none  [on_device(): (keep.astype(jnp.float32) + arrived.astype(jnp.float32)).astype(jnp.bfloa...]
    pallas_call x0 -> x1, Pallas kernels: none -> 1.14 us  [add_shares(): pl.pallas_call(add_kernel, out_shape=jax.ShapeDtypeStruct(a.shape, a.dtyp...]
where the time goes in v8:
time: 70.3 us; the launch traced here: 69.9 us
  Pallas kernels  32.8 us (47%)
  starting transfers between devices  18.1 us (26%)
  waiting for transfers between devices  15 us (21%)
  local copies, waits for them, and re-layouts  3.31 us (5%)
  between operations  0.75 us (1%)
    all_to_all x1, waiting for transfers between devices, on_device(): lax.all_to_all(pieces, BOTH, 0, 0, axis_index_groups=same_core_groups())  13.1 us
    all_to_all x1, starting transfers between devices, on_device(): lax.all_to_all(pieces, BOTH, 0, 0, axis_index_groups=same_core_groups())  12 us
    pallas_call x1, Pallas kernels, prefill(): pl.pallas_call(prefill_kernel, out_shape=jax.ShapeDtypeStruct((TOKENS, HE...  11.5 us
    pallas_call x1, Pallas kernels, decode(): pl.pallas_call(decode_kernel, out_shape=(jax.ShapeDtypeStruct((8, SHARE,...  8.48 us
    pallas_call x1, Pallas kernels, absorb(): pl.pallas_call(absorb_kernel, out_shape=(jax.ShapeDtypeStruct((BIAS + 4 *...  5.07 us
    all_to_all x1, starting transfers between devices, on_device(): parts = lax.all_to_all(chip, BOTH, 0, 0, axis_index_groups=chip_groups())  3.55 us
    pallas_call x1, Pallas kernels, early(): pl.pallas_call(early_kernel, out_shape=(pltpu.VMEM((HEADS // 2, 2 * QUERI...  3.17 us
    unnamed x12, local copies, waits for them, and re-layouts  2.62 us
  transfers between devices with their start and end apart: 4, of which 3 were waited for; matrix products, arithmetic and copies ran while one was open for 1% of the time, Pallas kernels for 30%

profile of v8, /device:TPU:1, one launch (start us, length us, event | category | flops | bytes accessed | tf_op | source)
XLA Modules:
  0.0 69.9 jit_solution(16882231446700584136)
XLA Ops:
  0.6 0.0 copy-start.3
  0.6 0.7 %copy-done.3 = bf16[16,576]{1,0:T(8,128)(2,1)S(1)} copy-done((bf16[16,576]{1,0:T(8,128)(2,1)S(1)}, bf16[16,576]{1,0:T(8,128)(2,1)}, u32[]{:S(2)}) %copy-start.3) | copy-done | bytes 18456
  1.4 0.0 copy-start.5
  1.4 1.1 %pack.1 = bf16[32,144,128]{2,1,0:T(8,128)(2,1)} custom-call(bf16[16,576]{1,0:T(8,128)(2,1)S(1)} %copy-done.3), custom_call_target="tpu_custom_call" | custom-call | tf_op jit(solution)/shard_map/pack/pallas_call | solution.py:109
  2.5 12.0 %all-to-all-start = ((bf16[64,72,128]{2,1,0:T(8,128)(2,1)}), bf16[64,72,128]{2,1,0:T(8,128)(2,1)S(1)}, u32[]{:S(2)}, u32[]{:S(2)}) async-start(bf16[64,72,128]{2,1,0:T(8,128)(2,1)} %bitcast), calls=%async_computation | async-start | bytes 2359296 | tf_op jit(solution)/shard_map/all_to_all | solution.py:531
  14.5 0.0 copy-done.5
  14.5 0.7 copy.11.length_ref
  15.2 5.1 %absorb.1 = (bf16[1664,640]{1,0:T(8,128)(2,1)}, bf16[1536,1024]{1,0:T(8,128)(2,1)}) custom-call(bf16[128,1536]{1,0:T(8,128)(2,1)} %bitcast.10, bf16[512,1024]{1,0:T(8,128)(2,1)} %key_ref.1, bf16[128,576]{1,0:T(8,128)(2,1)} %bitcast.11, s32[32,1]{1,0:T(8,128)} %copy.11.length_ref, s32[32,32]{1,0:T(8,128)} %table_ref.1, bf16[256,1536]{1,0:T(8,128)(2,1)} %pre_ref.1, ...), custom_call_target="tpu_custom_call" | custom-call | flops 134217728 | bytes 5000000 | tf_op jit(solution)/shard_map/absorb/pallas_call | solution.py:200
  20.2 13.1 %all-to-all-done = bf16[64,72,128]{2,1,0:T(8,128)(2,1)S(1)} async-done(((bf16[64,72,128]{2,1,0:T(8,128)(2,1)}), bf16[64,72,128]{2,1,0:T(8,128)(2,1)S(1)}, u32[]{:S(2)}, u32[]{:S(2)}) %all-to-all-start) | async-done | bytes 1179680 | tf_op jit(solution)/shard_map/all_to_all | solution.py:531
  33.4 0.0 copy-start
  33.4 2.2 %collective-permute-start = (bf16[32,144,128]{2,1,0:T(8,128)(2,1)S(1)}, bf16[32,144,128]{2,1,0:T(8,128)(2,1)S(1)}, u32[]{:S(2)}, u32[]{:S(2)}) collective-permute-start(bf16[32,144,128]{2,1,0:T(8,128)(2,1)S(1)} %bitcast.6), channel_id=1, source_target_pairs={{0,1},{1,0},{4,5},{5,4},{8,9},{9,8},{12,13},{13,12},{2,3},{3,2},{6... | collective-permute-start | bytes 3538952 | tf_op jit(solution)/shard_map/ppermute | solution.py:543
  35.6 3.2 %early.1 = (f32[4,256,1024]{2,1,0:T(8,128)S(1)}, bf16[1664,640]{1,0:T(8,128)(2,1)S(1)}, bf16[256,7168]{1,0:T(8,128)(2,1)S(1)}) custom-call(bf16[32,144,128]{2,1,0:T(8,128)(2,1)S(1)} %bitcast.7, bf16[1664,640]{1,0:T(8,128)(2,1)} %get-tuple-element.19.ready_hbm, bf16[1024,7168]{1,0:T(8,128)(2,1)} %weight_hbm.3), custom_call_target="tpu_custom_call" | custom-call | flops 1342177280 | bytes 12000000 | tf_op jit(solution)/shard_map/early/pallas_call | solution.py:326
  38.8 0.0 collective-permute-done.other
  38.8 0.0 copy-start.1
  38.8 0.0 copy-done
  38.8 8.5 %decode.1 = (bf16[8,448,128]{2,1,0:T(8,128)(2,1)S(1)}, bf16[128,1024]{1,0:T(8,128)(2,1)S(1)}, bf16[768,7168]{1,0:T(8,128)(2,1)S(1)}) custom-call(bf16[32,144,128]{2,1,0:T(8,128)(2,1)S(1)} %bitcast.8, bf16[32,144,128]{2,1,0:T(8,128)(2,1)S(1)} %collective-permute-done.other, f32[4,256,1024]{2,1,0:T(8,128)S(1)} %get-tuple-element.20.early, ...), custom_call_target="tpu_custom_call" | custom-call | flops 7583301632 | bytes 22000000 | tf_op jit(solution)/shard_map/decode/pallas_call | solution.py:455
  47.3 0.0 copy-done.1
  47.3 0.3 collective-permute-start.1
  47.7 1.4 %own_share.1.a_ref = bf16[8,448,128]{2,1,0:T(8,128)(2,1)S(1)} custom-call(bf16[128,1024]{1,0:T(8,128)(2,1)S(1)} %get-tuple-element.23.heads_out, bf16[256,7168]{1,0:T(8,128)(2,1)S(1)} %get-tuple-element.22.first_weight, bf16[768,7168]{1,0:T(8,128)(2,1)S(1)} %get-tuple-element.24.weight), custom_call_target="tpu_custom_call" | custom-call | flops 1073741824 | bytes 8000000 | tf_op jit(solution)/shard_map/own_share/pallas_call | solution.py:440
  49.1 0.0 copy-start.2
  49.1 1.0 %collective-permute-done.1.b_ref = bf16[8,448,128]{2,1,0:T(8,128)(2,1)S(1)} collective-permute-done((bf16[8,448,128]{2,1,0:T(8,128)(2,1)S(1)}, bf16[8,448,128]{2,1,0:T(8,128)(2,1)S(1)}, u32[]{:S(2)}, u32[]{:S(2)}) %collective-permute-start.1) | collective-permute-done | bytes 917536 | tf_op jit(solution)/shard_map/ppermute | solution.py:548
  50.1 1.1 %add_shares.1 = bf16[8,448,128]{2,1,0:T(8,128)(2,1)} custom-call(bf16[8,448,128]{2,1,0:T(8,128)(2,1)S(1)} %own_share.1.a_ref, bf16[8,448,128]{2,1,0:T(8,128)(2,1)S(1)} %collective-permute-done.1.b_ref), custom_call_target="tpu_custom_call" | custom-call | tf_op jit(solution)/shard_map/add_shares/pallas_call | solution.py:491
  51.2 3.6 %all-to-all-start.1 = ((bf16[8,448,128]{2,1,0:T(8,128)(2,1)}), bf16[8,448,128]{2,1,0:T(8,128)(2,1)S(1)}, u32[]{:S(2)}, u32[]{:S(2)}) async-start(bf16[8,448,128]{2,1,0:T(8,128)(2,1)} %add_shares.1), calls=%async_computation.1 | async-start | bytes 1835008 | tf_op jit(solution)/shard_map/all_to_all | solution.py:552
  54.8 0.0 copy-done.2
  54.8 0.0 copy-start.4
  54.8 1.9 %copy-done.4 = bf16[1536,1024]{1,0:T(8,128)(2,1)S(1)} copy-done((bf16[1536,1024]{1,0:T(8,128)(2,1)S(1)}, bf16[1536,1024]{1,0:T(8,128)(2,1)}, u32[]{:S(2)}) %copy-start.4) | copy-done | bytes 3145752
  56.7 11.5 %prefill.1 = bf16[256,1024]{1,0:T(8,128)(2,1)} custom-call(bf16[32,144,128]{2,1,0:T(8,128)(2,1)S(1)} %bitcast.9, bf16[32,144,128]{2,1,0:T(8,128)(2,1)S(1)} %copy-done.2, bf16[1536,1024]{1,0:T(8,128)(2,1)S(1)} %copy-done.4), custom_call_target="tpu_custom_call" | custom-call | flops 8589934592 | bytes 10000000 | tf_op jit(solution)/shard_map/prefill/pallas_call | solution.py:285
  68.2 0.8 %all-to-all-done.1.parts = bf16[8,448,128]{2,1,0:T(8,128)(2,1)S(1)} async-done(((bf16[8,448,128]{2,1,0:T(8,128)(2,1)}), bf16[8,448,128]{2,1,0:T(8,128)(2,1)S(1)}, u32[]{:S(2)}, u32[]{:S(2)}) %all-to-all-start.1) | async-done | bytes 917536 | tf_op jit(solution)/shard_map/all_to_all | solution.py:552
  69.1 0.8 %gather_sum.1 = bf16[128,448]{1,0:T(8,128)(2,1)} custom-call(bf16[8,448,128]{2,1,0:T(8,128)(2,1)S(1)} %all-to-all-done.1.parts), custom_call_target="tpu_custom_call" | custom-call | tf_op jit(solution)/shard_map/gather_sum/pallas_call | solution.py:509
Async XLA Ops:
  0.6 0.7 %copy-start.3 = (bf16[16,576]{1,0:T(8,128)(2,1)S(1)}, bf16[16,576]{1,0:T(8,128)(2,1)}, u32[]{:S(2)}) copy-start(bf16[16,576]{1,0:T(8,128)(2,1)} %latent_ref.1) | copy-start | bytes 55300
  1.4 13.1 %copy-start.5 = (s32[32]{0:T(128)S(1)}, s32[32]{0:T(128)}, u32[]{:S(2)}) copy-start(s32[32]{0:T(128)} %param.15) | copy-start | bytes 388
  2.5 30.9 %all-to-all-start = ((bf16[64,72,128]{2,1,0:T(8,128)(2,1)}), bf16[64,72,128]{2,1,0:T(8,128)(2,1)S(1)}, u32[]{:S(2)}, u32[]{:S(2)}) async-start(bf16[64,72,128]{2,1,0:T(8,128)(2,1)} %bitcast), calls=%async_computation | async-start | bytes 2359296 | tf_op jit(solution)/shard_map/all_to_all | solution.py:531
  33.4 5.5 %copy-start = (bf16[512,1024]{1,0:T(8,128)(2,1)S(1)}, bf16[512,1024]{1,0:T(8,128)(2,1)}, u32[]{:S(2)}) copy-start(bf16[512,1024]{1,0:T(8,128)(2,1)} %value_ref.3) | copy-start | bytes 3145732
  33.4 5.4 %collective-permute-start = (bf16[32,144,128]{2,1,0:T(8,128)(2,1)S(1)}, bf16[32,144,128]{2,1,0:T(8,128)(2,1)S(1)}, u32[]{:S(2)}, u32[]{:S(2)}) collective-permute-start(bf16[32,144,128]{2,1,0:T(8,128)(2,1)S(1)} %bitcast.6), channel_id=1, source_target_pairs={{0,1},{1,0},{4,5},{5,4},{8,9},{9,8},{12,13},{13,12},{2,3},{3,2},{6... | collective-permute-start | bytes 3538952 | tf_op jit(solution)/shard_map/ppermute | solution.py:543
  38.8 8.5 %copy-start.1 = (bf16[32,144,128]{2,1,0:T(8,128)(2,1)}, bf16[32,144,128]{2,1,0:T(8,128)(2,1)S(1)}, u32[]{:S(2)}) copy-start(bf16[32,144,128]{2,1,0:T(8,128)(2,1)S(1)} %collective-permute-done.other) | copy-start | bytes 3538948
  47.3 2.7 %collective-permute-start.1 = (bf16[8,448,128]{2,1,0:T(8,128)(2,1)S(1)}, bf16[8,448,128]{2,1,0:T(8,128)(2,1)S(1)}, u32[]{:S(2)}, u32[]{:S(2)}) collective-permute-start(bf16[8,448,128]{2,1,0:T(8,128)(2,1)S(1)} %get-tuple-element.25), channel_id=1, source_target_pairs={{0,1},{1,0},{4,5},{5,4},{8,9},{9,8},{12,13},{13,12},{2,3},{3,2},{6... | collective-permute-start | bytes 2752520 | tf_op jit(solution)/shard_map/ppermute | solution.py:548
  49.1 5.7 %copy-start.2 = (bf16[32,144,128]{2,1,0:T(8,128)(2,1)S(1)}, bf16[32,144,128]{2,1,0:T(8,128)(2,1)}, u32[]{:S(2)}) copy-start(bf16[32,144,128]{2,1,0:T(8,128)(2,1)} %copy-done.1) | copy-start | bytes 3538948
  51.2 17.8 %all-to-all-start.1 = ((bf16[8,448,128]{2,1,0:T(8,128)(2,1)}), bf16[8,448,128]{2,1,0:T(8,128)(2,1)S(1)}, u32[]{:S(2)}, u32[]{:S(2)}) async-start(bf16[8,448,128]{2,1,0:T(8,128)(2,1)} %add_shares.1), calls=%async_computation.1 | async-start | bytes 1835008 | tf_op jit(solution)/shard_map/all_to_all | solution.py:552
  54.8 1.9 %copy-start.4 = (bf16[1536,1024]{1,0:T(8,128)(2,1)S(1)}, bf16[1536,1024]{1,0:T(8,128)(2,1)}, u32[]{:S(2)}) copy-start(bf16[1536,1024]{1,0:T(8,128)(2,1)} %get-tuple-element.28.ready) | copy-start | bytes 9437188
